TPU v7x, 768 devices: a whole 4x8x12 slice. The times are simulated.
768 devices in a mesh: row: 24 (over z, x_hi), col: 32 (over y, x_lo, core).
Axes of the slice: x: 4 (x_hi: 2, x_lo: 2; x = x_hi * 2 + x_lo), y: 8, z: 12, core: 2. Of those that a mesh axis runs over, the one named last changes fastest.
Arguments:
- a_vals: bfloat16 [24, 32, 32, 256, 256], P('row', 'col'), may hold values from -1 to 1
- a_place: int32 [24, 32, 2, 32], P('row', 'col'), may hold values from 0 to 31, as said below
- a_count: int32 [24, 32], P('row', 'col'), may hold values from 8 to 32, as said below
- p_cols: int32 [768, 2], replicated, may hold values from 0 to 7, all different within a row
- r_cols: int32 [768, 2], replicated, may hold values from 0 to 7, all different within a row
- null_layout: int32 [64], replicated, may hold values from 0 to 63, each once
- mass: float32 [768, 256], P(('row', 'col')), may hold values from 1 to 2
- p_now: bfloat16 [768, 256, 128], P(('row', 'col')), may hold values from -4 to 4
- res_p: bfloat16 [768, 256, 128], P(('row', 'col')), may hold values from -60 to 60
- rt_now: bfloat16 [768, 256, 128], P(('row', 'col')), may hold values from -4 to 4
- res_r: bfloat16 [768, 256, 128], P(('row', 'col')), may hold values from -60 to 60
Outputs:
- p_next: bfloat16 [768, 256, 128], P(('row', 'col'))
- res_p_next: bfloat16 [768, 256, 128], P(('row', 'col'))
- rt_next: bfloat16 [768, 256, 128], P(('row', 'col'))
- res_r_next: bfloat16 [768, 256, 128], P(('row', 'col'))
Inputs may be any that keep to these rules, and one draw needn't show every extreme that they name: Slots 0 to a_count[r, c] - 1 of device block (r, c) are live; some device block has exactly 32. `a_place`: entry 0 is below 32, entry 1 below 24; the slots of one device block hold distinct positions.
All inputs are finite; a program needn't handle non-finite values.
Results may differ from a plain program's by a relative error of at most 0.015.
Values may be sent and summed in bfloat16 or wider, within the bound.
No kernel may reach another device: no remote copies, remote signals or barrier semaphores. Data moves between devices by JAX's collectives and lax.ppermute only.
A program may use at most 64 MiB of HBM per device.

v0:
```python
import jax
import jax.numpy as jnp
from jax import lax
from jax.sharding import PartitionSpec as P

NS = 4


EXACT_DOTS = lax.Precision.HIGHEST
EPSILON = 1e-06


def projector(null_layout, block_width):
    group_count = block_width // null_layout.shape[0]
    component = jnp.tile(null_layout % NS, group_count)
    same_group = (component[:, None] == component[None, :]).astype(jnp.float32)
    return same_group * (NS / block_width)


def pick_blocks(tile_set, source, target, live_slot, block_count):
    matched = ((source[:, :, None] == target[:, None, :]) & live_slot[:, None, None]).astype(
        jnp.bfloat16
    )
    split_tiles = tile_set.reshape(tile_set.shape[0], tile_set.shape[1], block_count, -1)
    picked = jnp.einsum("ats,axty->axsy", matched, split_tiles, preferred_element_type=jnp.float32)
    return picked.reshape(tile_set.shape).astype(jnp.bfloat16)


def shards(
    a_vals, a_place, a_count, p_cols, r_cols, null_layout, mass, p_now, res_p, rt_now, res_r
):
    col_count = lax.axis_size("col")
    row_id = lax.axis_index("row")
    col_id = lax.axis_index("col")
    tile_vals = a_vals[0, 0]
    local_row = a_place[0, 0, 0]
    local_col = a_place[0, 0, 1]
    slot_count = tile_vals.shape[0]
    block_count = p_cols.shape[1]
    block_width = res_p.shape[2]
    live_slot = jnp.arange(slot_count, dtype=jnp.int32) < a_count[0, 0]
    tile_row = row_id * col_count + local_row
    tile_col = local_col * col_count + col_id
    prolong_rows = lax.all_gather(res_p, "row", axis=0, tiled=True)
    prolong_pick = pick_blocks(
        prolong_rows[local_col], p_cols[tile_col], p_cols[tile_row], live_slot, block_count
    )
    restrict_rows = lax.all_gather(res_r, "col", axis=0, tiled=True)
    restrict_pick = pick_blocks(
        restrict_rows[local_row], r_cols[tile_row], r_cols[tile_col], live_slot, block_count
    )
    prolong_prod = jnp.einsum(
        "axy,ayz->axz", tile_vals, prolong_pick, preferred_element_type=jnp.float32
    )
    restrict_prod = jnp.einsum(
        "axy,axz->ayz", tile_vals, restrict_pick, preferred_element_type=jnp.float32
    )
    selector = (
        local_row[None, :] == jnp.arange(1 * lax.axis_size("col"), dtype=jnp.int32)[:, None]
    ).astype(jnp.float32)
    prolong_sum = lax.psum_scatter(
        jnp.einsum("la,axz->lxz", selector, prolong_prod, precision=EXACT_DOTS).astype(
            jnp.bfloat16
        ),
        "col",
        scatter_dimension=0,
        tiled=True,
    ).astype(jnp.float32)[0]
    selector = (
        local_col[None, :] == jnp.arange(1 * lax.axis_size("row"), dtype=jnp.int32)[:, None]
    ).astype(jnp.float32)
    restrict_sum = lax.psum_scatter(
        jnp.einsum("la,ayz->lyz", selector, restrict_prod, precision=EXACT_DOTS).astype(
            jnp.bfloat16
        ),
        "row",
        scatter_dimension=0,
        tiled=True,
    ).astype(jnp.float32)[0]
    projector_m = projector(null_layout, block_width)
    mass_rows = mass[0][:, None]
    resid_p = res_p[0].astype(jnp.float32)
    resid_r = res_r[0].astype(jnp.float32)
    prolong_full = prolong_sum + mass_rows * resid_p
    restrict_full = restrict_sum + mass_rows * resid_r
    update_p = prolong_full - jnp.dot(prolong_full, projector_m, precision=EXACT_DOTS)
    update_r = restrict_full - jnp.dot(restrict_full, projector_m, precision=EXACT_DOTS)
    across_p = jnp.sum(update_p * resid_p)
    square_p = jnp.sum(update_p * update_p)
    across_r = jnp.sum(update_r * resid_r)
    square_r = jnp.sum(update_r * update_r)
    across_p, square_p = lax.psum((across_p, square_p), ("row", "col"))
    across_r, square_r = lax.psum((across_r, square_r), ("row", "col"))
    alpha_p = across_p / (square_p + EPSILON)
    alpha_r = across_r / (square_r + EPSILON)
    p_next = (p_now[0].astype(jnp.float32) + alpha_p * resid_p).astype(jnp.bfloat16)
    res_p_next = (resid_p - alpha_p * update_p).astype(jnp.bfloat16)
    rt_next = (rt_now[0].astype(jnp.float32) + alpha_r * resid_r).astype(jnp.bfloat16)
    res_r_next = (resid_r - alpha_r * update_r).astype(jnp.bfloat16)
    return (p_next[None], res_p_next[None], rt_next[None], res_r_next[None])


def solution(mesh):
    in_specs = (
        P("row", "col", None, None, None),
        P("row", "col", None, None),
        P("row", "col"),
        P(),
        P(),
        P(),
        P(("row", "col"), None),
        P(("row", "col"), None, None),
        P(("row", "col"), None, None),
        P(("row", "col"), None, None),
        P(("row", "col"), None, None),
    )
    out_specs = (
        P(("row", "col"), None, None),
        P(("row", "col"), None, None),
        P(("row", "col"), None, None),
        P(("row", "col"), None, None),
    )
    return jax.shard_map(shards, mesh=mesh, in_specs=in_specs, out_specs=out_specs, check_vma=False)
```

profile of v0, /device:TPU:1, one launch (start us, length us, event | category | flops | bytes accessed | tf_op | source)
XLA Modules:
  0.0 835.3 jit_solution(8184819556021336905)
XLA Ops:
  7.2 0.0 all-gather.3.cloned.1.call-start
  7.2 0.7 all-gather.3.cloned.1.call-update
  7.9 0.0 all-gather.5.cloned.1.call-start
  7.9 0.7 all-gather.5.cloned.1.call-update
  8.6 0.0 reduce-scatter.3.cloned.1.call-start
  8.7 0.9 copy.45
  9.6 0.8 fusion.71
  10.4 0.6 gather_fusion.1
  10.9 0.6 gather_fusion.2
  12.2 0.8 slice_bitcast_fusion
  12.9 121.7 %all-gather.3.cloned.1.call-done = bf16[24,256,128]{2,1,0:T(8,128)(2,1)} async-done(((bf16[1,256,128]{2,1,0:T(8,128)(2,1)}), bf16[24,256,128]{2,1,0:T(8,128)(2,1)}) %all-gather.3.cloned.1.call-update) | async-done | bytes 1572880 | tf_op jit(solution)/shard_map/all_gather | solution.py:44
  134.6 2.4 gather_fusion
  137.0 2.9 copy.44
  139.9 4.0 fusion.4
  143.9 0.0 copy-start
  143.9 0.4 copy.48
  144.3 1.7 copy-done
  146.1 3.4 fusion.6
  149.5 5.5 copy.49
  155.0 4.4 convolution_convert_fusion.2
  159.5 2.2 copy.50
  161.6 0.0 copy-start.6
  161.6 0.0 reduce-scatter.3.cloned.1.call-update
  161.7 0.2 reduce-scatter.5.cloned.1.call-start
  161.9 0.4 copy-done.6
  162.3 0.2 copy.52
  162.5 0.6 gather_fusion.4
  163.1 0.6 gather_fusion.5
  163.7 46.1 %all-gather.5.cloned.1.call-done = bf16[32,256,128]{2,1,0:T(8,128)(2,1)} async-done(((bf16[1,256,128]{2,1,0:T(8,128)(2,1)}), bf16[32,256,128]{2,1,0:T(8,128)(2,1)}) %all-gather.5.cloned.1.call-update) | async-done | bytes 2097168 | tf_op jit(solution)/shard_map/all_gather | solution.py:48
  209.8 2.5 gather_fusion.3
  212.3 2.9 copy.51
  215.3 4.0 fusion.5
  219.3 0.0 copy-start.1
  219.3 0.4 copy.55
  219.7 1.7 copy-done.1
  221.5 2.7 fusion.9
  224.1 5.5 copy.56
  229.6 4.1 fusion.63
  233.7 0.0 copy-start.8
  233.7 0.0 copy-start.3
  233.8 0.0 copy-start.7
  233.8 0.0 copy-start.2
  233.8 0.0 copy-start.4
  233.8 1.5 copy.65
  235.3 0.0 copy-start.5
  235.3 0.0 reduce-scatter.5.cloned.1.call-update
  235.3 0.0 copy-done.8
  235.4 0.1 eq.80
  235.4 98.8 %reduce-scatter.3.cloned.1.call-done = bf16[1,256,128]{2,1,0:T(8,128)(2,1)} async-done(((bf16[32,256,128]{2,1,0:T(8,128)(2,1)}), bf16[1,256,128]{2,1,0:T(8,128)(2,1)}) %reduce-scatter.3.cloned.1.call-update) | async-done | bytes 65552 | tf_op jit(solution)/shard_map/reduce_scatter | solution.py:61
  334.2 0.0 copy-done.3
  334.2 0.0 copy-done.7
  334.2 1.9 multiply_reduce_fusion.1
  336.1 371.4 %reduce-scatter.5.cloned.1.call-done = bf16[1,256,128]{2,1,0:T(8,128)(2,1)} async-done(((bf16[24,256,128]{2,1,0:T(8,128)(2,1)}), bf16[1,256,128]{2,1,0:T(8,128)(2,1)}) %reduce-scatter.5.cloned.1.call-update) | async-done | bytes 65552 | tf_op jit(solution)/shard_map/reduce_scatter | solution.py:72
  707.5 0.0 copy-done.2
  707.5 1.9 multiply_reduce_fusion
  709.4 114.1 %all-reduce = (f32[]{:T(128)}, f32[]{:T(128)}, f32[]{:T(128)}, f32[]{:T(128)}) all-reduce(f32[]{:T(128)} %get-tuple-element.7, f32[]{:T(128)} %get-tuple-element.6, f32[]{:T(128)} %get-tuple-element.5, f32[]{:T(128)} %get-tuple-element.4), channel_id=1, replica_groups=mesh['row'=24,'col'=32] {'row','col'}, use_global_device_ids=true, to_apply=%region_2.3 | all-reduce | flops 4 | bytes 32 | tf_op jit(solution)/shard_map/psum | solution.py:92
  824.8 0.7 fusion.38
  825.5 0.0 copy-done.4
  825.5 0.7 fusion.31
  827.4 0.7 fusion.39
  828.1 0.0 copy-done.5
  828.1 0.7 fusion.25
  (6 shorter events, 0.0 us)
Async XLA Ops:
  7.2 127.4 %all-gather.3.cloned.1.call-start = ((), (), s32[]{:S(2)}) async-start(), calls=%async_computation.2 | async-start | bytes 1638400 | tf_op jit(solution)/shard_map/all_gather | solution.py:44
  7.9 201.9 %all-gather.5.cloned.1.call-start = ((), (), s32[]{:S(2)}) async-start(), calls=%async_computation.4 | async-start | bytes 2162688 | tf_op jit(solution)/shard_map/all_gather | solution.py:48
  8.6 325.6 %reduce-scatter.3.cloned.1.call-start = ((), (), s32[]{:S(2)}) async-start(), calls=%async_computation.3 | async-start | bytes 2162688 | tf_op jit(solution)/shard_map/reduce_scatter | solution.py:61
  143.9 2.2 copy-start
  161.6 0.7 copy-start.6
  161.7 545.9 %reduce-scatter.5.cloned.1.call-start = ((), (), s32[]{:S(2)}) async-start(), calls=%async_computation.5 | async-start | bytes 1638400 | tf_op jit(solution)/shard_map/reduce_scatter | solution.py:72
  219.3 2.2 copy-start.1
  233.7 1.6 copy-start.8
  233.7 100.5 %copy-start.3 = (bf16[1,256,128]{2,1,0:T(8,128)(2,1)S(1)}, bf16[1,256,128]{2,1,0:T(8,128)(2,1)}, u32[]{:S(2)}) copy-start(bf16[1,256,128]{2,1,0:T(8,128)(2,1)} %param.19) | copy-start | bytes 196612
  233.8 100.5 %copy-start.7 = (f32[1,256]{1,0:T(1,128)S(1)}, f32[1,256]{1,0:T(1,128)}, u32[]{:S(2)}) copy-start(f32[1,256]{1,0:T(1,128)} %param.17) | copy-start | bytes 3076
  233.8 473.8 %copy-start.2 = (bf16[1,256,128]{2,1,0:T(8,128)(2,1)S(1)}, bf16[1,256,128]{2,1,0:T(8,128)(2,1)}, u32[]{:S(2)}) copy-start(bf16[1,256,128]{2,1,0:T(8,128)(2,1)} %param.21) | copy-start | bytes 196612
  233.8 591.7 %copy-start.4 = (bf16[1,256,128]{2,1,0:T(8,128)(2,1)S(1)}, bf16[1,256,128]{2,1,0:T(8,128)(2,1)}, u32[]{:S(2)}) copy-start(bf16[1,256,128]{2,1,0:T(8,128)(2,1)} %param.20) | copy-start | bytes 196612
  235.3 592.8 %copy-start.5 = (bf16[1,256,128]{2,1,0:T(8,128)(2,1)S(1)}, bf16[1,256,128]{2,1,0:T(8,128)(2,1)}, u32[]{:S(2)}) copy-start(bf16[1,256,128]{2,1,0:T(8,128)(2,1)} %param.18) | copy-start | bytes 196612
Sparse Core Ops, SparseCore 0:
  11.6 122.9 all-gather.2
  137.0 72.7 all-gather.4
  212.9 121.2 reduce-scatter.2
  339.8 367.6 reduce-scatter.4
where the time goes:
time: 836 us; the launch traced here: 835 us
  waiting for transfers between devices  639 us (76%)
  blocking collectives  114 us (14%)
  local copies, waits for them, and re-layouts  34.5 us (4%)
  matrix products  26.4 us (3%)
  between operations  17.2 us (2%)
    reduce_scatter x1, waiting for transfers between devices, shards(): lax.psum_scatter(jnp.einsum('la,ayz->lyz', selector, restrict_prod, preci...  371 us
    all_gather x1, waiting for transfers between devices, shards(): prolong_rows = lax.all_gather(res_p, 'row', axis=0, tiled=True)  122 us
    psum x1, blocking collectives, shards(): across_p, square_p = lax.psum((across_p, square_p), ('row', 'col'))  114 us
    reduce_scatter x1, waiting for transfers between devices, shards(): lax.psum_scatter(jnp.einsum('la,axz->lxz', selector, prolong_prod, precis...  98.8 us
    all_gather x1, waiting for transfers between devices, shards(): restrict_rows = lax.all_gather(res_r, 'col', axis=0, tiled=True)  46.1 us
  transfers between devices with their start and end apart: 4, of which 4 were waited for; matrix products, arithmetic and copies ran while one was open for 7% of the time, Pallas kernels for 0%

commit v1 on v0

v1 whole, which is shorter than its diff:
```python
import functools

import jax
import jax.numpy as jnp
from jax import lax
from jax.experimental import pallas as pl
from jax.experimental.pallas import tpu as pltpu
from jax.sharding import Mesh
from jax.sharding import PartitionSpec as P

NS = 4
EPSILON = 1e-06
EXACT = lax.Precision.HIGHEST

SIZES = (12, 2, 8, 2, 2)
AXES = ("z", "xh", "y", "xl", "core")
N_Z, N_XH, N_Y, N_XL, N_CORE = SIZES
N_ROW, N_COL = N_Z * N_XH, N_Y * N_XL * N_CORE
HALF_COL = N_COL // 2
SWAP = ((0, 1), (1, 0))

VMEM = pl.BlockSpec(memory_space=pltpu.VMEM)
SMEM = pl.BlockSpec(memory_space=pltpu.SMEM)
PARAMS = pltpu.CompilerParams(vmem_limit_bytes=48 * 1024 * 1024)


def pick_columns(tile, straight, crossed):
    block = tile.shape[1] // 2
    lane = lax.broadcasted_iota(jnp.int32, tile.shape, 1)
    left = lane < block
    wide = tile.astype(jnp.float32)
    turned = pltpu.roll(wide, block, 1)
    as_is = jnp.where(left, straight[0], straight[1]) != 0
    other = jnp.where(left, crossed[0], crossed[1]) != 0
    picked = jnp.where(as_is, wide, jnp.where(other, turned, 0.0))
    return picked.astype(jnp.bfloat16)


def matches(cols_ref, source, target):
    s0, s1 = cols_ref[2 * source], cols_ref[2 * source + 1]
    t0, t1 = cols_ref[2 * target], cols_ref[2 * target + 1]
    flag = lambda same: same.astype(jnp.int32)
    return (flag(s0 == t0), flag(s1 == t1)), (flag(s1 == t0), flag(s0 == t1))


def clear(acc_ref):
    def body(i, carry):
        acc_ref[i] = jnp.zeros(acc_ref.shape[1:], acc_ref.dtype)
        return carry

    lax.fori_loop(0, acc_ref.shape[0], body, 0)


def prolong_kernel(where_ref, place_ref, cols_ref, a_ref, tiles_ref, mine_ref, theirs_ref, acc_ref):
    count, xh, core = where_ref[0], where_ref[1], where_ref[2]
    row_id, col_id = where_ref[3], where_ref[4]
    slots = a_ref.shape[0]
    clear(acc_ref)

    def body(a, carry):
        local_row, local_col = place_ref[a], place_ref[slots + a]
        straight, crossed = matches(
            cols_ref, local_col * N_COL + col_id, row_id * N_COL + local_row
        )

        @pl.when(straight[0] + straight[1] + crossed[0] + crossed[1] > 0)
        def _():
            tile = tiles_ref[local_col // 2, jnp.where(local_col % 2 == xh, 0, 1)]
            picked = pick_columns(tile, straight, crossed)
            acc_ref[local_row] += jnp.dot(a_ref[a], picked, preferred_element_type=jnp.float32)

        return carry

    lax.fori_loop(0, count, body, 0)

    def store(q, carry):
        mine_ref[q] = acc_ref[2 * q + core].astype(jnp.bfloat16)
        theirs_ref[q] = acc_ref[2 * q + 1 - core].astype(jnp.bfloat16)
        return carry

    lax.fori_loop(0, HALF_COL, store, 0)


def restrict_kernel(
    where_ref, place_ref, cols_ref, a_ref, own_ref, other_ref, mine_ref, theirs_ref, acc_ref
):
    count, xh, core = where_ref[0], where_ref[1], where_ref[2]
    row_id, col_id, xl = where_ref[3], where_ref[4], where_ref[5]
    slots = a_ref.shape[0]
    clear(acc_ref)

    def body(a, carry):
        local_row, local_col = place_ref[a], place_ref[slots + a]
        straight, crossed = matches(
            cols_ref, row_id * N_COL + local_row, local_col * N_COL + col_id
        )

        @pl.when(straight[0] + straight[1] + crossed[0] + crossed[1] > 0)
        def _():
            y, chip = local_row // 4, jnp.where((local_row // 2) % 2 == xl, 0, 1)

            def add(tile):
                picked = pick_columns(tile, straight, crossed)
                acc_ref[local_col] += lax.dot_general(
                    a_ref[a],
                    picked,
                    (((0,), (0,)), ((), ())),
                    preferred_element_type=jnp.float32,
                )

            @pl.when(local_row % 2 == core)
            def _():
                add(own_ref[y, chip])

            @pl.when(local_row % 2 != core)
            def _():
                add(other_ref[y, chip])

        return carry

    lax.fori_loop(0, count, body, 0)

    def store(z, carry):
        mine_ref[z] = acc_ref[2 * z + xh].astype(jnp.bfloat16)
        theirs_ref[z] = acc_ref[2 * z + 1 - xh].astype(jnp.bfloat16)
        return carry

    lax.fori_loop(0, N_Z, store, 0)


def update_kernel(parts_ref, mass_ref, resid_ref, projector_ref, update_ref, sums_ref):
    def body(i, total):
        return total + parts_ref[i].astype(jnp.float32)

    resid = resid_ref[...].astype(jnp.float32)
    full = mass_ref[...] * resid
    full = lax.fori_loop(0, parts_ref.shape[0], body, full)
    update = full - jnp.dot(
        full, projector_ref[...], precision=EXACT, preferred_element_type=jnp.float32
    )
    update_ref[...] = update
    sums_ref[0:1, :] = jnp.sum(update * resid, axis=0, keepdims=True)
    sums_ref[1:2, :] = jnp.sum(update * update, axis=0, keepdims=True)


def shape(dims, dtype=jnp.bfloat16):
    return jax.ShapeDtypeStruct(dims, dtype)


def step(parts, mass_rows, resid, projector):
    return pl.pallas_call(
        update_kernel,
        out_shape=(shape(resid.shape, jnp.float32), shape((2, resid.shape[1]), jnp.float32)),
        in_specs=[VMEM] * 4,
        out_specs=(VMEM, VMEM),
        compiler_params=PARAMS,
    )(parts, mass_rows, resid, projector)


def sum_over(values, axes, count):
    spread = jnp.broadcast_to(values[None], (count,) + values.shape)
    return jnp.sum(lax.all_to_all(spread, axes, 0, 0, tiled=True), axis=0)


def shards(
    a_vals, a_place, a_count, p_cols, r_cols, null_layout, mass, p_now, res_p, rt_now, res_r
):
    z, xh, y, xl, core = (lax.axis_index(name) for name in AXES)
    row_id = z * N_XH + xh
    col_id = (y * N_XL + xl) * N_CORE + core
    where = jnp.stack([a_count[0, 0], xh, core, row_id, col_id, xl]).astype(jnp.int32)
    tile_vals = a_vals[0, 0]
    place = a_place[0, 0].reshape(-1)
    slots, height = tile_vals.shape[:2]
    width = res_p.shape[2]
    p_flat, r_flat = p_cols.reshape(-1), r_cols.reshape(-1)

    near = lax.ppermute(res_p, "xh", SWAP)
    p_rows = lax.all_gather(jnp.stack([res_p[0], near[0]]), "z", axis=0)
    near = lax.ppermute(res_r, "xl", SWAP)
    pair = jnp.stack([res_r[0], near[0]])
    r_own = lax.all_to_all(
        jnp.broadcast_to(pair[None], (N_Y,) + pair.shape), "y", 0, 0, tiled=True
    )
    r_other = lax.ppermute(r_own, "core", SWAP)

    r_mine, r_theirs = pl.pallas_call(
        restrict_kernel,
        out_shape=(shape((N_Z, height, width)),) * 2,
        in_specs=[SMEM] * 3 + [VMEM] * 3,
        out_specs=(VMEM, VMEM),
        scratch_shapes=[pltpu.VMEM((N_ROW, height, width), jnp.float32)],
        compiler_params=PARAMS,
    )(where, place, r_flat, tile_vals, r_own, r_other)
    r_near = lax.ppermute(r_theirs, "xh", SWAP)
    r_sum = (r_mine.astype(jnp.float32) + r_near.astype(jnp.float32)).astype(jnp.bfloat16)
    r_part = lax.psum_scatter(r_sum, "z", scatter_dimension=0, tiled=True)

    p_mine, p_theirs = pl.pallas_call(
        prolong_kernel,
        out_shape=(shape((HALF_COL, height, width)),) * 2,
        in_specs=[SMEM] * 3 + [VMEM] * 2,
        out_specs=(VMEM, VMEM),
        scratch_shapes=[pltpu.VMEM((N_COL, height, width), jnp.float32)],
        compiler_params=PARAMS,
    )(where, place, p_flat, tile_vals, p_rows)
    p_near = lax.ppermute(p_theirs, "core", SWAP)
    p_sum = (p_mine.astype(jnp.float32) + p_near.astype(jnp.float32)).astype(jnp.bfloat16)
    p_part = lax.all_to_all(p_sum, ("y", "xl"), 0, 0, tiled=True)

    component = jnp.tile(null_layout % NS, width // null_layout.shape[0])
    projector = (component[:, None] == component[None, :]).astype(jnp.float32) * (NS / width)
    mass_rows = mass[0][:, None]
    update_p, sums_p = step(p_part, mass_rows, res_p[0], projector)
    update_r, sums_r = step(r_part, mass_rows, res_r[0], projector)
    sums = jnp.sum(jnp.concatenate([sums_p, sums_r]), axis=1)
    sums = jnp.pad(sums[None], ((0, 0), (0, width - sums.shape[0])))
    sums = sum_over(sums, ("y", "xl", "core"), N_COL)
    sums = sum_over(sums, ("z", "xh"), N_ROW)[0]
    alpha_p = sums[0] / (sums[1] + EPSILON)
    alpha_r = sums[2] / (sums[3] + EPSILON)
    resid_p, resid_r = res_p[0].astype(jnp.float32), res_r[0].astype(jnp.float32)
    p_next = (p_now[0].astype(jnp.float32) + alpha_p * resid_p).astype(jnp.bfloat16)
    res_p_next = (resid_p - alpha_p * update_p).astype(jnp.bfloat16)
    rt_next = (rt_now[0].astype(jnp.float32) + alpha_r * resid_r).astype(jnp.bfloat16)
    res_r_next = (resid_r - alpha_r * update_r).astype(jnp.bfloat16)
    return (p_next[None], res_p_next[None], rt_next[None], res_r_next[None])


def solution(mesh):
    fine = Mesh(mesh.devices.reshape(SIZES), AXES)
    row, col = ("z", "xh"), ("y", "xl", "core")
    tiles = P(row + col, None, None)
    in_specs = (
        P(row, col, None, None, None),
        P(row, col, None, None),
        P(row, col),
        P(),
        P(),
        P(),
        P(row + col, None),
        tiles,
        tiles,
        tiles,
        tiles,
    )
    return jax.shard_map(
        shards, mesh=fine, in_specs=in_specs, out_specs=(tiles,) * 4, check_vma=False
    )
```

time: 836 us -> 237 us (0.28)
  waiting for transfers between devices: 639 us -> 77.4 us
  blocking collectives: 114 us -> 70.6 us
  starting transfers between devices: 0.34 us -> 42.8 us
  local copies, waits for them, and re-layouts: 34.5 us -> 5.9 us
  matrix products: 26.4 us -> 0 us
  Pallas kernels: 0 us -> 13.3 us
    reduce_scatter x2 -> x1, waiting for transfers between devices: 470 us -> 48.8 us  [shards(): r_part = lax.psum_scatter(r_sum, 'z', scatter_dimension=0, tiled=True)]
    all_gather x2 -> x1, waiting for transfers between devices: 168 us -> 16.3 us  [shards(): p_rows = lax.all_gather(jnp.stack([res_p[0], near[0]]), 'z', axis=0)]
    psum x1 -> x0, blocking collectives: 114 us -> none  [shards(): across_p, square_p = lax.psum((across_p, square_p), ('row', 'col'))]
    all_to_all x0 -> x3, blocking collectives: none -> 70.6 us  [the longest x2 43.7 us: sum_over(): return jnp.sum(lax.all_to_all(spread, axes, 0, 0, tiled=True), axis=0)]
    ppermute x0 -> x5, starting transfers between devices: none -> 36.2 us  [the longest x1 11.6 us: shards(): r_other = lax.ppermute(r_own, 'core', SWAP)]
    dot_general x8 -> x0, matrix products: 26.4 us -> none  [the longest x2 7.99 us: pick_blocks(): jnp.einsum('ats,axty->axsy', matched, split_tiles, preferred_element_type...]
    pallas_call x0 -> x4, Pallas kernels: none -> 13.3 us  [the longest x1 6.12 us: shards(): pl.pallas_call(restrict_kernel, out_shape=(shape((N_Z, height, width)),)...]
    gather x8 -> x0, local copies, waits for them, and re-layouts: 13.1 us -> none  [the longest x2 5.47 us: shards(): restrict_rows[local_row]]
  transfers between devices with their start and end apart: 4 -> 8, of which waited for: 4 -> 5; matrix products, arithmetic and copies ran while one was open for 7% -> 3% of each run, Pallas kernels for 0% -> 5%
where the time goes in v1:
time: 237 us; the launch traced here: 236 us
  waiting for transfers between devices  77.4 us (33%)
  blocking collectives  70.6 us (30%)
  starting transfers between devices  42.8 us (18%)
  between operations  17.6 us (7%)
  Pallas kernels  13.3 us (6%)
  other arithmetic  8.82 us (4%)
  local copies, waits for them, and re-layouts  5.9 us (2%)
    reduce_scatter x1, waiting for transfers between devices, shards(): r_part = lax.psum_scatter(r_sum, 'z', scatter_dimension=0, tiled=True)  48.8 us
    all_to_all x2, blocking collectives, sum_over(): return jnp.sum(lax.all_to_all(spread, axes, 0, 0, tiled=True), axis=0)  43.7 us
    all_to_all x1, blocking collectives, shards(): lax.all_to_all(jnp.broadcast_to(pair[None], (N_Y,) + pair.shape), 'y', 0,...  26.8 us
    all_gather x1, waiting for transfers between devices, shards(): p_rows = lax.all_gather(jnp.stack([res_p[0], near[0]]), 'z', axis=0)  16.3 us
    ppermute x1, starting transfers between devices, shards(): r_other = lax.ppermute(r_own, 'core', SWAP)  11.6 us
    ppermute x1, starting transfers between devices, shards(): p_near = lax.ppermute(p_theirs, 'core', SWAP)  8.99 us
    ppermute x1, waiting for transfers between devices, shards(): r_near = lax.ppermute(r_theirs, 'xh', SWAP)  8.46 us
    ppermute x1, starting transfers between devices, shards(): r_near = lax.ppermute(r_theirs, 'xh', SWAP)  6.87 us
  transfers between devices with their start and end apart: 8, of which 5 were waited for; matrix products, arithmetic and copies ran while one was open for 3% of the time, Pallas kernels for 5%

profile of v1, /device:TPU:1, one launch (start us, length us, event | category | flops | bytes accessed | tf_op | source)
XLA Modules:
  0.0 236.3 jit_solution(5892541513430910416)
XLA Ops:
  7.2 0.0 copy-start.10
  7.2 0.0 copy-start.8
  7.2 0.0 all-gather.3.cloned.1.call-start
  7.2 5.5 %collective-permute-start = (bf16[1,256,128]{2,1,0:T(8,128)(2,1)}, bf16[1,256,128]{2,1,0:T(8,128)(2,1)S(1)}, u32[]{:S(2)}, u32[]{:S(2)}) collective-permute-start(bf16[1,256,128]{2,1,0:T(8,128)(2,1)} %param.19), channel_id=1, source_target_pairs={{0,32},{32,0},{1,33},{33,1},{2,34},{34,2},{3,35},{35,3},{4,36},{36... | collective-permute-start | bytes 196616 | tf_op jit(solution)/shard_map/ppermute | solution.py:178
  12.7 1.9 collective-permute-done
  14.6 1.5 pad_maximum_fusion
  16.1 0.0 all-gather.3.cloned.1.call-update
  16.1 3.3 %collective-permute-start.2 = (bf16[1,256,128]{2,1,0:T(8,128)(2,1)}, bf16[1,256,128]{2,1,0:T(8,128)(2,1)S(1)}, u32[]{:S(2)}, u32[]{:S(2)}) collective-permute-start(bf16[1,256,128]{2,1,0:T(8,128)(2,1)} %param.21), channel_id=1, source_target_pairs={{0,2},{2,0},{1,3},{3,1},{4,6},{6,4},{5,7},{7,5},{8,10},{10,8},{9,1... | collective-permute-start | bytes 196616 | tf_op jit(solution)/shard_map/ppermute | solution.py:180
  19.5 1.9 collective-permute-done.2
  21.4 0.9 pad_maximum_fusion.1
  22.2 0.2 broadcast_in_dim.14
  22.4 26.8 %all_to_all.20.own_ref = bf16[8,2,256,128]{3,2,1,0:T(8,128)(2,1)S(1)} all-to-all(bf16[8,2,256,128]{3,2,1,0:T(8,128)(2,1)S(1)} %broadcast_in_dim.14), channel_id=1, replica_groups=mesh['z'=12,'xh'=2,'y'=8,'xl'=2,'core'=2] {'y'}, dimensions={0} | all-to-all | bytes 2097152 | tf_op jit(solution)/shard_map/all_to_all | solution.py:182
  49.3 11.6 %collective-permute-start.3 = (bf16[8,2,256,128]{3,2,1,0:T(8,128)(2,1)S(1)}, bf16[8,2,256,128]{3,2,1,0:T(8,128)(2,1)S(1)}, u32[]{:S(2)}, u32[]{:S(2)}) collective-permute-start(bf16[8,2,256,128]{3,2,1,0:T(8,128)(2,1)S(1)} %all_to_all.20.own_ref), channel_id=1, source_target_pairs={{0,1},{1,0},{2,3},{3,2},{4,5},{5,4},{6,7},{7,6},{8,9},{9,8},{10,11... | collective-permute-start | bytes 3145736 | tf_op jit(solution)/shard_map/ppermute | solution.py:185
  61.5 0.0 copy-done.10
  61.5 0.1 reshape_squeeze.3.place_ref
  61.6 0.0 copy-done.8
  61.6 0.2 copy.27
  61.8 0.2 reshape.41.cols_ref
  62.0 0.1 stack.29.where_ref
  62.1 16.3 %all-gather.3.cloned.1.call-done = bf16[24,256,128]{2,1,0:T(8,128)(2,1)} async-done(((bf16[2,256,128]{2,1,0:T(8,128)(2,1)}), bf16[24,256,128]{2,1,0:T(8,128)(2,1)}) %all-gather.3.cloned.1.call-update) | async-done | bytes 1572880 | tf_op jit(solution)/shard_map/all_gather | solution.py:179
  78.4 0.0 copy-start
  78.4 1.4 copy-done
  79.8 6.1 %shard_map.138 = (bf16[16,256,128]{2,1,0:T(8,128)(2,1)S(1)}, bf16[16,256,128]{2,1,0:T(8,128)(2,1)}) custom-call(s32[6]{0:T(128)S(1)} %stack.29.where_ref, s32[64]{0:T(128)S(1)} %reshape_squeeze.3.place_ref, s32[1536]{0:T(1024)S(1)} %reshape.41.cols_ref, bf16[32,256,256]{2,1,0:T(8,128)(2,1)} %bitcast.29, bf16[12,2,256,128]{3,2,1,0:T(8,128)(2,1)S(1)} %bitcast.26), custom_call_target="tpu_custom_call" | custom-call | tf_op jit(solution)/shard_map/pallas_call | solution.py:199
  85.9 9.0 %collective-permute-start.1 = (bf16[16,256,128]{2,1,0:T(8,128)(2,1)}, bf16[16,256,128]{2,1,0:T(8,128)(2,1)}, u32[]{:S(2)}, u32[]{:S(2)}) collective-permute-start(bf16[16,256,128]{2,1,0:T(8,128)(2,1)} %get-tuple-element.13), channel_id=1, source_target_pairs={{0,1},{1,0},{2,3},{3,2},{4,5},{5,4},{6,7},{7,6},{8,9},{9,8},{10,11... | collective-permute-start | bytes 3145736 | tf_op jit(solution)/shard_map/ppermute | solution.py:207
  94.9 0.9 copy.29
  95.8 0.2 reshape.42.cols_ref
  96.0 0.0 collective-permute-done.3.other_ref
  96.0 6.1 %shard_map.140 = (bf16[12,256,128]{2,1,0:T(8,128)(2,1)S(1)}, bf16[12,256,128]{2,1,0:T(8,128)(2,1)}) custom-call(s32[6]{0:T(128)S(1)} %stack.29.where_ref, s32[64]{0:T(128)S(1)} %reshape_squeeze.3.place_ref, s32[1536]{0:T(1024)S(1)} %reshape.42.cols_ref, bf16[32,256,256]{2,1,0:T(8,128)(2,1)} %bitcast.30, bf16[8,2,256,128]{3,2,1,0:T(8,128)(2,1)S(1)} %all_to_all.20.own_ref, ...), custom_call_target="tpu_custom_call" | custom-call | tf_op jit(solution)/shard_map/pallas_call | solution.py:187
  102.2 0.0 copy-start.3
  102.2 0.9 copy-done.3
  103.1 6.9 %collective-permute-start.4 = (bf16[12,256,128]{2,1,0:T(8,128)(2,1)}, bf16[12,256,128]{2,1,0:T(8,128)(2,1)}, u32[]{:S(2)}, u32[]{:S(2)}) collective-permute-start(bf16[12,256,128]{2,1,0:T(8,128)(2,1)} %get-tuple-element.16), channel_id=1, source_target_pairs={{0,32},{32,0},{1,33},{33,1},{2,34},{34,2},{3,35},{35,3},{4,36},{36... | collective-permute-start | bytes 2359304 | tf_op jit(solution)/shard_map/ppermute | solution.py:195
  110.0 0.0 collective-permute-done.1
  110.0 0.0 copy-start.4
  110.0 2.6 %add_convert_fusion = bf16[16,256,128]{2,1,0:T(8,128)(2,1)} fusion(bf16[16,256,128]{2,1,0:T(8,128)(2,1)} %collective-permute-done.1, bf16[16,256,128]{2,1,0:T(8,128)(2,1)S(1)} %get-tuple-element.12), kind=kLoop, calls=%fused_computation | loop fusion | flops 2097152 | bytes 3145728 | tf_op jit(solution)/shard_map/convert_element_type | solution.py:208
  112.5 6.4 %all-to-all-start = ((bf16[16,256,128]{2,1,0:T(8,128)(2,1)}), bf16[16,256,128]{2,1,0:T(8,128)(2,1)S(1)}, u32[]{:S(2)}, u32[]{:S(2)}) async-start(bf16[16,256,128]{2,1,0:T(8,128)(2,1)} %add_convert_fusion), calls=%async_computation | async-start | bytes 2097152 | tf_op jit(solution)/shard_map/all_to_all | solution.py:209
  119.0 0.0 copy-start.9
  119.0 0.0 copy-start.11
  119.0 0.0 copy-start.1
  119.0 0.0 copy-start.2
  119.0 0.0 reduce-scatter.2.cloned.1.call-start
  119.1 8.5 %collective-permute-done.4 = bf16[12,256,128]{2,1,0:T(8,128)(2,1)} collective-permute-done((bf16[12,256,128]{2,1,0:T(8,128)(2,1)}, bf16[12,256,128]{2,1,0:T(8,128)(2,1)}, u32[]{:S(2)}, u32[]{:S(2)}) %collective-permute-start.4) | collective-permute-done | bytes 786464 | tf_op jit(solution)/shard_map/ppermute | solution.py:195
  127.5 0.0 copy-done.4
  127.5 2.2 add_convert_fusion.1
  129.8 0.0 reduce-scatter.2.cloned.1.call-update
  129.8 0.0 copy-done.9
  129.8 0.1 copy.28.mass_ref
  130.0 0.0 copy-done.11
  130.0 0.1 eq.17
  130.1 0.1 compare_select_fusion.projector_ref
  130.2 48.8 %reduce-scatter.2.cloned.1.call-done.parts_ref = bf16[1,256,128]{2,1,0:T(8,128)(2,1)} async-done(((bf16[12,256,128]{2,1,0:T(8,128)(2,1)}), bf16[1,256,128]{2,1,0:T(8,128)(2,1)}) %reduce-scatter.2.cloned.1.call-update) | async-done | bytes 65552 | tf_op jit(solution)/shard_map/reduce_scatter | solution.py:197
  179.0 0.0 copy-done.1
  179.0 0.8 copy-done.5
  179.8 0.3 shard_map.141
  180.2 0.0 all-to-all-done.parts_ref
  180.2 0.0 copy-done.2
  180.2 0.7 shard_map.139
  180.9 0.1 maximum_reduce_fusion
  181.1 23.9 %all_to_all.21 = f32[32,1,128]{2,1,0:T(1,128)S(1)} all-to-all(f32[32,1,128]{2,1,0:T(1,128)S(1)} %broadcast_in_dim.34), channel_id=1, replica_groups=mesh['z'=12,'xh'=2,'y'=8,'xl'=2,'core'=2] {'y','xl','core'}, dimensions={0} | all-to-all | bytes 32768 | tf_op jit(solution)/shard_map/all_to_all | solution.py:162
  205.0 19.8 %all_to_all.22 = f32[24,1,128]{2,1,0:T(1,128)S(1)} all-to-all(f32[24,1,128]{2,1,0:T(1,128)S(1)} %broadcast_in_dim.35), channel_id=1, replica_groups=mesh['z'=12,'xh'=2,'y'=8,'xl'=2,'core'=2] {'z','xh'}, dimensions={0} | all-to-all | bytes 24576 | tf_op jit(solution)/shard_map/all_to_all | solution.py:162
  224.9 0.6 fusion.3
  228.1 0.7 fusion
  228.7 0.0 copy-done.6
  228.8 0.0 copy-done.7
  228.8 0.7 add_convert_fusion.2
  (10 shorter events, 0.1 us)
Async XLA Ops:
  7.2 54.3 %copy-start.10 = (s32[1,1,2,32]{3,2,1,0:T(2,128)S(1)}, s32[1,1,2,32]{3,2,1,0:T(2,128)}, u32[]{:S(2)}) copy-start(s32[1,1,2,32]{3,2,1,0:T(2,128)} %param.12) | copy-start | bytes 772
  7.2 54.4 %copy-start.8 = (s32[768,2]{0,1:T(2,128)S(1)}, s32[768,2]{0,1:T(2,128)}, u32[]{:S(2)}) copy-start(s32[768,2]{0,1:T(2,128)} %param.14) | copy-start | bytes 18436
  7.2 71.2 %all-gather.3.cloned.1.call-start = ((), (), s32[]{:S(2)}) async-start(), calls=%async_computation.6 | async-start | bytes 1703936 | tf_op jit(solution)/shard_map/all_gather | solution.py:179
  7.2 7.3 %collective-permute-start = (bf16[1,256,128]{2,1,0:T(8,128)(2,1)}, bf16[1,256,128]{2,1,0:T(8,128)(2,1)S(1)}, u32[]{:S(2)}, u32[]{:S(2)}) collective-permute-start(bf16[1,256,128]{2,1,0:T(8,128)(2,1)} %param.19), channel_id=1, source_target_pairs={{0,32},{32,0},{1,33},{33,1},{2,34},{34,2},{3,35},{35,3},{4,36},{36... | collective-permute-start | bytes 196616 | tf_op jit(solution)/shard_map/ppermute | solution.py:178
  16.1 5.2 %collective-permute-start.2 = (bf16[1,256,128]{2,1,0:T(8,128)(2,1)}, bf16[1,256,128]{2,1,0:T(8,128)(2,1)S(1)}, u32[]{:S(2)}, u32[]{:S(2)}) collective-permute-start(bf16[1,256,128]{2,1,0:T(8,128)(2,1)} %param.21), channel_id=1, source_target_pairs={{0,2},{2,0},{1,3},{3,1},{4,6},{6,4},{5,7},{7,5},{8,10},{10,8},{9,1... | collective-permute-start | bytes 196616 | tf_op jit(solution)/shard_map/ppermute | solution.py:180
  49.3 46.8 %collective-permute-start.3 = (bf16[8,2,256,128]{3,2,1,0:T(8,128)(2,1)S(1)}, bf16[8,2,256,128]{3,2,1,0:T(8,128)(2,1)S(1)}, u32[]{:S(2)}, u32[]{:S(2)}) collective-permute-start(bf16[8,2,256,128]{3,2,1,0:T(8,128)(2,1)S(1)} %all_to_all.20.own_ref), channel_id=1, source_target_pairs={{0,1},{1,0},{2,3},{3,2},{4,5},{5,4},{6,7},{7,6},{8,9},{9,8},{10,11... | collective-permute-start | bytes 3145736 | tf_op jit(solution)/shard_map/ppermute | solution.py:185
  78.4 1.4 copy-start
  85.9 24.0 %collective-permute-start.1 = (bf16[16,256,128]{2,1,0:T(8,128)(2,1)}, bf16[16,256,128]{2,1,0:T(8,128)(2,1)}, u32[]{:S(2)}, u32[]{:S(2)}) collective-permute-start(bf16[16,256,128]{2,1,0:T(8,128)(2,1)} %get-tuple-element.13), channel_id=1, source_target_pairs={{0,1},{1,0},{2,3},{3,2},{4,5},{5,4},{6,7},{7,6},{8,9},{9,8},{10,11... | collective-permute-start | bytes 3145736 | tf_op jit(solution)/shard_map/ppermute | solution.py:207
  102.2 0.9 copy-start.3
  103.1 24.5 %collective-permute-start.4 = (bf16[12,256,128]{2,1,0:T(8,128)(2,1)}, bf16[12,256,128]{2,1,0:T(8,128)(2,1)}, u32[]{:S(2)}, u32[]{:S(2)}) collective-permute-start(bf16[12,256,128]{2,1,0:T(8,128)(2,1)} %get-tuple-element.16), channel_id=1, source_target_pairs={{0,32},{32,0},{1,33},{33,1},{2,34},{34,2},{3,35},{35,3},{4,36},{36... | collective-permute-start | bytes 2359304 | tf_op jit(solution)/shard_map/ppermute | solution.py:195
  110.0 17.6 %copy-start.4 = (bf16[12,256,128]{2,1,0:T(8,128)(2,1)S(1)}, bf16[12,256,128]{2,1,0:T(8,128)(2,1)}, u32[]{:S(2)}) copy-start(bf16[12,256,128]{2,1,0:T(8,128)(2,1)} %copy-done.3) | copy-start | bytes 2359300
  112.5 67.6 %all-to-all-start = ((bf16[16,256,128]{2,1,0:T(8,128)(2,1)}), bf16[16,256,128]{2,1,0:T(8,128)(2,1)S(1)}, u32[]{:S(2)}, u32[]{:S(2)}) async-start(bf16[16,256,128]{2,1,0:T(8,128)(2,1)} %add_convert_fusion), calls=%async_computation | async-start | bytes 2097152 | tf_op jit(solution)/shard_map/all_to_all | solution.py:209
  119.0 10.8 %copy-start.9 = (f32[1,256]{1,0:T(1,128)S(1)}, f32[1,256]{1,0:T(1,128)}, u32[]{:S(2)}) copy-start(f32[1,256]{1,0:T(1,128)} %param.17) | copy-start | bytes 3076
  119.0 11.0 %copy-start.11 = (s32[64]{0:T(128)S(1)}, s32[64]{0:T(128)}, u32[]{:S(2)}) copy-start(s32[64]{0:T(128)} %param.16) | copy-start | bytes 772
  119.0 60.0 %copy-start.1 = (bf16[1,256,128]{2,1,0:T(8,128)(2,1)S(1)}, bf16[1,256,128]{2,1,0:T(8,128)(2,1)}, u32[]{:S(2)}) copy-start(bf16[1,256,128]{2,1,0:T(8,128)(2,1)} %param.21) | copy-start | bytes 196612
  119.0 61.2 %copy-start.2 = (bf16[1,256,128]{2,1,0:T(8,128)(2,1)S(1)}, bf16[1,256,128]{2,1,0:T(8,128)(2,1)}, u32[]{:S(2)}) copy-start(bf16[1,256,128]{2,1,0:T(8,128)(2,1)} %param.19) | copy-start | bytes 196612
  119.0 60.0 %reduce-scatter.2.cloned.1.call-start = ((), (), s32[]{:S(2)}) async-start(), calls=%async_computation.5 | async-start | bytes 851968 | tf_op jit(solution)/shard_map/reduce_scatter | solution.py:197
  129.8 99.0 %copy-start.6 = (bf16[1,256,128]{2,1,0:T(8,128)(2,1)S(1)}, bf16[1,256,128]{2,1,0:T(8,128)(2,1)}, u32[]{:S(2)}) copy-start(bf16[1,256,128]{2,1,0:T(8,128)(2,1)} %param.20) | copy-start | bytes 196612
  129.8 99.0 %copy-start.7 = (bf16[1,256,128]{2,1,0:T(8,128)(2,1)S(1)}, bf16[1,256,128]{2,1,0:T(8,128)(2,1)}, u32[]{:S(2)}) copy-start(bf16[1,256,128]{2,1,0:T(8,128)(2,1)} %param.18) | copy-start | bytes 196612
  179.0 0.8 copy-start.5
Sparse Core Ops, SparseCore 0:
  16.2 62.1 all-gather.2
  129.9 49.0 reduce-scatter.1

commit v2 on v1

v2 whole, which is shorter than its diff:
```python
import functools

import jax
import jax.numpy as jnp
from jax import lax
from jax.experimental import pallas as pl
from jax.experimental.pallas import tpu as pltpu
from jax.sharding import Mesh
from jax.sharding import PartitionSpec as P

NS = 4
EPSILON = 1e-06
EXACT = lax.Precision.HIGHEST

SIZES = (12, 2, 8, 2, 2)
AXES = ("z", "xh", "y", "xl", "core")
N_Z, N_XH, N_Y, N_XL, N_CORE = SIZES
N_ROW, N_COL = N_Z * N_XH, N_Y * N_XL * N_CORE
HALF_COL = N_COL // 2
SWAP = ((0, 1), (1, 0))

VMEM = pl.BlockSpec(memory_space=pltpu.VMEM)
SMEM = pl.BlockSpec(memory_space=pltpu.SMEM)
COST = pl.CostEstimate(flops=2**29, bytes_accessed=12 * 2**20, transcendentals=0)
MIB = 2**20


def pick_columns(tile, straight, crossed):
    block = tile.shape[1] // 2
    lane = lax.broadcasted_iota(jnp.int32, tile.shape, 1)
    left = lane < block
    wide = tile.astype(jnp.float32)
    turned = pltpu.roll(wide, block, 1)
    as_is = jnp.where(left, straight[0], straight[1]) != 0
    other = jnp.where(left, crossed[0], crossed[1]) != 0
    picked = jnp.where(as_is, wide, jnp.where(other, turned, 0.0))
    return picked.astype(jnp.bfloat16)


def matches(cols_ref, source, target):
    s0, s1 = cols_ref[2 * source], cols_ref[2 * source + 1]
    t0, t1 = cols_ref[2 * target], cols_ref[2 * target + 1]
    flag = lambda same: same.astype(jnp.int32)
    return (flag(s0 == t0), flag(s1 == t1)), (flag(s1 == t0), flag(s0 == t1))


def clear(acc_ref):
    def body(i, carry):
        acc_ref[i] = jnp.zeros(acc_ref.shape[1:], acc_ref.dtype)
        return carry

    lax.fori_loop(0, acc_ref.shape[0], body, 0)


def each_match(where_ref, place_ref, cols_ref, slots, turn, product):
    count, row_id, col_id = where_ref[0], where_ref[3], where_ref[4]

    def body(a, carry):
        local_row, local_col = place_ref[a], place_ref[slots + a]
        tile_row = row_id * N_COL + local_row
        tile_col = local_col * N_COL + col_id
        source, target = (tile_row, tile_col) if turn else (tile_col, tile_row)
        straight, crossed = matches(cols_ref, source, target)

        @pl.when(straight[0] + straight[1] + crossed[0] + crossed[1] > 0)
        def _():
            product(a, local_row, local_col, straight, crossed)

        return carry

    lax.fori_loop(0, count, body, 0)


def fetch(tile_ref, choices):
    for holds, ref, index in choices:

        @pl.when(holds)
        def _(ref=ref, index=index):
            tile_ref[...] = ref[index]


def prolong_kernel(
    where_ref,
    place_ref,
    cols_ref,
    a_ref,
    own_ref,
    up_ref,
    down_ref,
    near_own_ref,
    near_up_ref,
    near_down_ref,
    mine_ref,
    theirs_low_ref,
    theirs_high_ref,
    acc_ref,
    tile_ref,
):
    xh, core, z = where_ref[1], where_ref[2], where_ref[5]
    clear(acc_ref)

    def product(a, local_row, local_col, straight, crossed):
        here = lax.rem(local_col, N_XH) == xh
        ahead = lax.rem(local_col // N_XH - z + N_Z, N_Z)
        third = lax.rem(ahead, 3)
        choices = []
        for side, refs in (
            (here, (own_ref, up_ref, down_ref)),
            (jnp.logical_not(here), (near_own_ref, near_up_ref, near_down_ref)),
        ):
            for k, offset in enumerate((0, 1, -1)):
                index = lax.rem(ahead - offset + N_Z, N_Z) // 3
                choices.append((side & (third == k), refs[k], index))
        fetch(tile_ref, choices)
        picked = pick_columns(tile_ref[...], straight, crossed)
        acc_ref[local_row] += jnp.dot(a_ref[a], picked, preferred_element_type=jnp.float32)

    each_match(where_ref, place_ref, cols_ref, a_ref.shape[0], False, product)

    def store(q, carry):
        mine_ref[q] = acc_ref[2 * q + core].astype(jnp.bfloat16)
        return carry

    lax.fori_loop(0, HALF_COL, store, 0)

    def store_theirs(q, carry):
        theirs_low_ref[q] = acc_ref[2 * q + 1 - core].astype(jnp.bfloat16)
        theirs_high_ref[q] = acc_ref[HALF_COL + 2 * q + 1 - core].astype(jnp.bfloat16)
        return carry

    lax.fori_loop(0, HALF_COL // 2, store_theirs, 0)


def restrict_kernel(
    where_ref,
    place_ref,
    cols_ref,
    a_ref,
    own_ref,
    other_ref,
    mine_ref,
    theirs_ref,
    after_ref,
    acc_ref,
    tile_ref,
):
    for i in range(where_ref.shape[0]):
        after_ref[i] = where_ref[i]
    xh, core, z = where_ref[1], where_ref[2], where_ref[5]
    clear(acc_ref)

    def product(a, local_row, local_col, straight, crossed):
        here = lax.rem(local_row, N_CORE) == core
        index = local_row // N_CORE
        fetch(tile_ref, [(here, own_ref, index), (jnp.logical_not(here), other_ref, index)])
        picked = pick_columns(tile_ref[...], straight, crossed)
        acc_ref[local_col] += lax.dot_general(
            a_ref[a], picked, (((0,), (0,)), ((), ())), preferred_element_type=jnp.float32
        )

    each_match(where_ref, place_ref, cols_ref, a_ref.shape[0], True, product)

    def store(q, carry):
        owner = 3 * lax.rem(q, 4) + lax.rem(z + q // 4, 3)
        mine_ref[q] = acc_ref[2 * owner + xh].astype(jnp.bfloat16)
        theirs_ref[q] = acc_ref[2 * owner + 1 - xh].astype(jnp.bfloat16)
        return carry

    lax.fori_loop(0, N_Z, store, 0)


def wide_sum(refs, index):
    total = refs[0][index].astype(jnp.float32)
    for ref in refs[1:]:
        total += ref[index].astype(jnp.float32)
    return total.astype(jnp.bfloat16)


def pair_kernel(mine_ref, near_low_ref, near_high_ref, sum_ref):
    half = near_low_ref.shape[0]

    def body(i, carry):
        for start, near_ref in ((0, near_low_ref), (half, near_high_ref)):
            total = mine_ref[start + i].astype(jnp.float32) + near_ref[i].astype(jnp.float32)
            sum_ref[start + i] = total.astype(jnp.bfloat16)
        return carry

    lax.fori_loop(0, half, body, 0)


def thirds_kernel(mine_ref, near_ref, own_ref, up_ref, down_ref):
    def body(i, carry):
        for third, ref in enumerate((own_ref, up_ref, down_ref)):
            ref[i] = wide_sum((mine_ref, near_ref), 4 * third + i)
        return carry

    lax.fori_loop(0, 4, body, 0)


def quarters_kernel(where_ref, own_ref, up_ref, down_ref, *quarter_refs):
    quarter = where_ref[5] // 3
    for i, ref in enumerate(quarter_refs):
        ref[...] = wide_sum((own_ref, up_ref, down_ref), lax.rem(quarter + i, 4))


def update_kernel(mass_ref, resid_ref, projector_ref, *refs):
    update_ref, sums_ref = refs[-2:]
    resid = resid_ref[...].astype(jnp.float32)
    full = mass_ref[...] * resid
    for parts_ref in refs[:-2]:
        if len(parts_ref.shape) == 2:
            full += parts_ref[...].astype(jnp.float32)
        else:
            add = lambda i, total, ref=parts_ref: total + ref[i].astype(jnp.float32)
            full = lax.fori_loop(0, parts_ref.shape[0], add, full)
    update = full - jnp.dot(
        full, projector_ref[...], precision=EXACT, preferred_element_type=jnp.float32
    )
    update_ref[...] = update
    sums_ref[0:1, :] = jnp.sum(update * resid, axis=0, keepdims=True)
    sums_ref[1:2, :] = jnp.sum(update * update, axis=0, keepdims=True)


def shape(dims, dtype=jnp.bfloat16):
    return jax.ShapeDtypeStruct(dims, dtype)


def on_device(kernel, out_shape, scalars, *operands, scratch=(), cost=None, scalars_out=0, mib=6):
    count = len(out_shape)
    return pl.pallas_call(
        kernel,
        out_shape=out_shape,
        in_specs=[SMEM] * len(scalars) + [VMEM] * len(operands),
        out_specs=(VMEM,) * (count - scalars_out) + (SMEM,) * scalars_out,
        scratch_shapes=scratch,
        cost_estimate=cost,
        compiler_params=pltpu.CompilerParams(vmem_limit_bytes=mib * MIB),
    )(*scalars, *operands)


def after(array, *earlier):
    return pl.pallas_call(
        lambda *refs: None,
        out_shape=shape(array.shape, array.dtype),
        in_specs=[pl.BlockSpec(memory_space=pl.ANY)] * (1 + len(earlier)),
        out_specs=pl.BlockSpec(memory_space=pl.ANY),
        input_output_aliases={0: 0},
        compiler_params=pltpu.CompilerParams(vmem_limit_bytes=MIB),
    )(array, *earlier)


def step(parts, mass_rows, resid, projector):
    return on_device(
        update_kernel,
        (shape(resid.shape, jnp.float32), shape((2, resid.shape[1]), jnp.float32)),
        (),
        mass_rows,
        resid,
        projector,
        *parts,
    )


def turned(array, axis, by):
    size = lax.axis_size(axis)
    return lax.ppermute(array, axis, [((i + by) % size, i) for i in range(size)])


def gather(tile, axes, count):
    copies = jnp.broadcast_to(tile, (count,) + tile.shape[1:])
    return lax.all_to_all(copies, axes, 0, 0, tiled=True)


def final_kernel(
    sums_ref,
    p_now_ref,
    res_p_ref,
    update_p_ref,
    rt_now_ref,
    res_r_ref,
    update_r_ref,
    p_next_ref,
    res_p_next_ref,
    rt_next_ref,
    res_r_next_ref,
):
    sums = jnp.sum(sums_ref[...], axis=0)
    alpha_p = sums[0:1, 0:1] / (sums[0:1, 1:2] + EPSILON)
    alpha_r = sums[0:1, 2:3] / (sums[0:1, 3:4] + EPSILON)
    for alpha, now_ref, res_ref, update_ref, next_ref, res_next_ref in (
        (alpha_p, p_now_ref, res_p_ref, update_p_ref, p_next_ref, res_p_next_ref),
        (alpha_r, rt_now_ref, res_r_ref, update_r_ref, rt_next_ref, res_r_next_ref),
    ):
        resid = res_ref[...].astype(jnp.float32)
        next_ref[...] = (now_ref[...].astype(jnp.float32) + alpha * resid).astype(jnp.bfloat16)
        res_next_ref[...] = (resid - alpha * update_ref[...]).astype(jnp.bfloat16)


def shards(
    a_vals, a_place, a_count, p_cols, r_cols, null_layout, mass, p_now, res_p, rt_now, res_r
):
    z, xh, y, xl, core = (lax.axis_index(name) for name in AXES)
    row_id = z * N_XH + xh
    col_id = (y * N_XL + xl) * N_CORE + core
    where = jnp.stack([a_count[0, 0], xh, core, row_id, col_id, z]).astype(jnp.int32)
    tile_vals = a_vals[0, 0]
    place = a_place[0, 0].reshape(-1)
    height, width = res_p.shape[1:]
    p_flat, r_flat = p_cols.reshape(-1), r_cols.reshape(-1)
    tile = shape((height, width))
    tile_scratch = pltpu.VMEM((height, width), jnp.bfloat16)

    r_own = gather(res_r, ("y", "xl"), HALF_COL)
    own = jnp.concatenate([res_p] + [turned(res_p, "z", by) for by in (3, 6, 9)])
    thirds = (own, turned(own, "z", 1), turned(own, "z", -1))
    near = tuple(turned(third, "xh", 1) for third in thirds)
    r_own = after(r_own, *thirds[1:])
    r_other = turned(r_own, "core", 1)

    r_mine, r_theirs, where_then = on_device(
        restrict_kernel,
        (shape((N_Z, height, width)),) * 2 + (shape(where.shape, jnp.int32),),
        (where, place, r_flat),
        tile_vals,
        r_own,
        r_other,
        scratch=[pltpu.VMEM((N_ROW, height, width), jnp.float32), tile_scratch],
        cost=COST,
        mib=18,
        scalars_out=1,
    )
    r_near = turned(r_theirs, "xh", 1)
    p_mine, p_low, p_high = on_device(
        prolong_kernel,
        (shape((HALF_COL, height, width)),) + (shape((HALF_COL // 2, height, width)),) * 2,
        (where_then, place, p_flat),
        tile_vals,
        *thirds,
        *near,
        scratch=[pltpu.VMEM((N_COL, height, width), jnp.float32), tile_scratch],
        cost=COST,
        mib=18,
    )
    p_near = (turned(p_low, "core", 1), turned(p_high, "core", 1))

    r_thirds = on_device(thirds_kernel, (shape((4, height, width)),) * 3, (), r_mine, r_near)
    r_quarters = on_device(
        quarters_kernel,
        (tile,) * 4,
        (where,),
        r_thirds[0],
        turned(r_thirds[1], "z", -1),
        turned(r_thirds[2], "z", 1),
    )
    r_parts = [r_quarters[0]]
    r_parts += [turned(r_quarters[i], "z", -3 * i) for i in (1, 2, 3)]
    p_mine = after(p_mine, r_thirds[0])
    (p_sum,) = on_device(pair_kernel, (shape((HALF_COL, height, width)),), (), p_mine, *p_near)
    p_parts = [lax.all_to_all(p_sum, ("y", "xl"), 0, 0, tiled=True)]

    component = jnp.tile(null_layout % NS, width // null_layout.shape[0])
    projector = (component[:, None] == component[None, :]).astype(jnp.float32) * (NS / width)
    mass_rows = mass[0][:, None]
    update_p, sums_p = step(p_parts, mass_rows, res_p[0], projector)
    update_r, sums_r = step(r_parts, mass_rows, res_r[0], projector)
    sums = jnp.sum(jnp.concatenate([sums_p, sums_r]), axis=1)
    sums = jnp.pad(sums[None, None], ((0, 0), (0, 0), (0, width - sums.shape[0])))
    sums = gather(sums, ("xh", "xl", "core"), N_XH * N_XL * N_CORE)
    sums = gather(jnp.sum(sums, axis=0, keepdims=True), ("z", "y"), N_Z * N_Y)
    outs = on_device(
        final_kernel,
        (tile,) * 4,
        (),
        sums,
        p_now[0],
        res_p[0],
        update_p,
        rt_now[0],
        res_r[0],
        update_r,
    )
    return tuple(out[None] for out in outs)


def solution(mesh):
    fine = Mesh(mesh.devices.reshape(SIZES), AXES)
    row, col = ("z", "xh"), ("y", "xl", "core")
    tiles = P(row + col, None, None)
    in_specs = (
        P(row, col, None, None, None),
        P(row, col, None, None),
        P(row, col),
        P(),
        P(),
        P(),
        P(row + col, None),
        tiles,
        tiles,
        tiles,
        tiles,
    )
    return jax.shard_map(
        shards, mesh=fine, in_specs=in_specs, out_specs=(tiles,) * 4, check_vma=False
    )
```

time: 237 us -> 184 us (0.78)
  starting transfers between devices: 42.8 us -> 94 us
  waiting for transfers between devices: 77.4 us -> 27.7 us
  blocking collectives: 70.6 us -> 35.4 us
  between operations: 17.6 us -> 1.71 us
  other arithmetic: 8.82 us -> 0.23 us
  local copies, waits for them, and re-layouts: 5.9 us -> 11.1 us
    reduce_scatter x1 -> x0, waiting for transfers between devices: 48.8 us -> none  [shards(): r_part = lax.psum_scatter(r_sum, 'z', scatter_dimension=0, tiled=True)]
    ppermute x5 -> x17, starting transfers between devices: 36.2 us -> 78.2 us  [turned(): lax.ppermute(array, axis, [((i + by) % size, i) for i in range(size)])]
    all_to_all x3 -> x2, blocking collectives: 70.6 us -> 35.4 us  [gather(): return lax.all_to_all(copies, axes, 0, 0, tiled=True)]
    all_gather x1 -> x0, waiting for transfers between devices: 16.3 us -> none  [shards(): p_rows = lax.all_gather(jnp.stack([res_p[0], near[0]]), 'z', axis=0)]
    ppermute x5 -> x17, waiting for transfers between devices: 12.2 us -> 27.7 us  [turned(): lax.ppermute(array, axis, [((i + by) % size, i) for i in range(size)])]
    all_to_all x1 -> x2, starting transfers between devices: 6.42 us -> 15.8 us  [the longest x1 8.68 us: gather(): return lax.all_to_all(copies, axes, 0, 0, tiled=True)]
    convert_element_type x3 -> x0, other arithmetic: 5.51 us -> none  [the longest x1 2.57 us: shards(): (p_mine.astype(jnp.float32) + p_near.astype(jnp.float32)).astype(jnp.bflo...]
    unnamed x26 -> x29, local copies, waits for them, and re-layouts: 4.24 us -> 7.53 us
  transfers between devices with their start and end apart: 8 -> 19, of which waited for: 5 -> 8; matrix products, arithmetic and copies ran while one was open for 3% -> 3% of each run, Pallas kernels for 5% -> 5%
where the time goes in v2:
time: 184 us; the launch traced here: 183 us
  starting transfers between devices  94 us (51%)
  blocking collectives  35.4 us (19%)
  waiting for transfers between devices  27.7 us (15%)
  Pallas kernels  12.7 us (7%)
  local copies, waits for them, and re-layouts  11.1 us (6%)
    ppermute x17, starting transfers between devices, turned(): lax.ppermute(array, axis, [((i + by) % size, i) for i in range(size)])  78.2 us
    all_to_all x2, blocking collectives, gather(): return lax.all_to_all(copies, axes, 0, 0, tiled=True)  35.4 us
    ppermute x17, waiting for transfers between devices, turned(): lax.ppermute(array, axis, [((i + by) % size, i) for i in range(size)])  27.7 us
    pallas_call x8, Pallas kernels, on_device(): pl.pallas_call(kernel, out_shape=out_shape, in_specs=[SMEM] * len(scalars...  12.7 us
    all_to_all x1, starting transfers between devices, gather(): return lax.all_to_all(copies, axes, 0, 0, tiled=True)  8.68 us
    unnamed x29, local copies, waits for them, and re-layouts  7.53 us
    all_to_all x1, starting transfers between devices, shards(): p_parts = [lax.all_to_all(p_sum, ('y', 'xl'), 0, 0, tiled=True)]  7.07 us
  transfers between devices with their start and end apart: 19, of which 8 were waited for; matrix products, arithmetic and copies ran while one was open for 3% of the time, Pallas kernels for 5%

profile of v2, /device:TPU:1, one launch (start us, length us, event | category | flops | bytes accessed | tf_op | source)
XLA Modules:
  0.0 182.7 jit_solution(159318383530078397)
XLA Ops:
  0.7 2.0 %broadcast_in_dim.36 = bf16[16,256,128]{2,1,0:T(8,128)(2,1)} broadcast(bf16[256,128]{1,0:T(8,128)(2,1)} %bitcast.25), dimensions={1,2} | broadcast | bytes 1114112 | tf_op jit(solution)/shard_map/broadcast_in_dim | solution.py:270
  2.7 8.7 %all-to-all-start = ((bf16[16,256,128]{2,1,0:T(8,128)(2,1)}), bf16[16,256,128]{2,1,0:T(8,128)(2,1)S(1)}, u32[]{:S(2)}, u32[]{:S(2)}) async-start(bf16[16,256,128]{2,1,0:T(8,128)(2,1)} %broadcast_in_dim.36), calls=%async_computation | async-start | bytes 2097152 | tf_op jit(solution)/shard_map/all_to_all | solution.py:271
  11.4 14.3 %collective-permute-start = (bf16[1,256,128]{2,1,0:T(8,128)(2,1)}, bf16[1,256,128]{2,1,0:T(8,128)(2,1)S(1)}, u32[]{:S(2)}, u32[]{:S(2)}) collective-permute-start(bf16[1,256,128]{2,1,0:T(8,128)(2,1)} %param.19), channel_id=1, source_target_pairs={{192,0},{256,64},{320,128},{384,192},{448,256},{512,320},{576,384}... | collective-permute-start | bytes 196616 | tf_op jit(solution)/shard_map/ppermute | solution.py:266
  25.7 2.5 %collective-permute-start.1 = (bf16[1,256,128]{2,1,0:T(8,128)(2,1)}, bf16[1,256,128]{2,1,0:T(8,128)(2,1)S(1)}, u32[]{:S(2)}, u32[]{:S(2)}) collective-permute-start(bf16[1,256,128]{2,1,0:T(8,128)(2,1)} %param.19), channel_id=1, source_target_pairs={{384,0},{448,64},{512,128},{576,192},{640,256},{704,320},{0,384},{... | collective-permute-start | bytes 196616 | tf_op jit(solution)/shard_map/ppermute | solution.py:266
  28.2 5.8 %collective-permute-start.2 = (bf16[1,256,128]{2,1,0:T(8,128)(2,1)}, bf16[1,256,128]{2,1,0:T(8,128)(2,1)S(1)}, u32[]{:S(2)}, u32[]{:S(2)}) collective-permute-start(bf16[1,256,128]{2,1,0:T(8,128)(2,1)} %param.19), channel_id=1, source_target_pairs={{576,0},{640,64},{704,128},{0,192},{64,256},{128,320},{192,384},{2... | collective-permute-start | bytes 196616 | tf_op jit(solution)/shard_map/ppermute | solution.py:266
  34.0 1.5 constant_dynamic-update-slice_fusion.3
  35.4 0.0 collective-permute-done
  35.4 0.6 constant_dynamic-update-slice_fusion.2
  36.1 1.8 collective-permute-done.1
  37.9 0.6 constant_dynamic-update-slice_fusion.1
  38.5 0.6 constant_dynamic-update-slice_fusion.own_ref
  39.1 8.4 %collective-permute-start.3 = (bf16[4,256,128]{2,1,0:T(8,128)(2,1)}, bf16[4,256,128]{2,1,0:T(8,128)(2,1)S(1)}, u32[]{:S(2)}, u32[]{:S(2)}) collective-permute-start(bf16[4,256,128]{2,1,0:T(8,128)(2,1)} %constant_dynamic-update-slice_fusion.own_ref), channel_id=1, source_target_pairs={{64,0},{128,64},{192,128},{256,192},{320,256},{384,320},{448,384},... | collective-permute-start | bytes 786440 | tf_op jit(solution)/shard_map/ppermute | solution.py:266
  47.5 1.9 %collective-permute-start.4 = (bf16[4,256,128]{2,1,0:T(8,128)(2,1)}, bf16[4,256,128]{2,1,0:T(8,128)(2,1)S(1)}, u32[]{:S(2)}, u32[]{:S(2)}) collective-permute-start(bf16[4,256,128]{2,1,0:T(8,128)(2,1)} %constant_dynamic-update-slice_fusion.own_ref), channel_id=1, source_target_pairs={{704,0},{0,64},{64,128},{128,192},{192,256},{256,320},{320,384},{3... | collective-permute-start | bytes 786440 | tf_op jit(solution)/shard_map/ppermute | solution.py:266
  49.4 3.0 %collective-permute-done.3.refs_1_.up_ref = bf16[4,256,128]{2,1,0:T(8,128)(2,1)S(1)} collective-permute-done((bf16[4,256,128]{2,1,0:T(8,128)(2,1)}, bf16[4,256,128]{2,1,0:T(8,128)(2,1)S(1)}, u32[]{:S(2)}, u32[]{:S(2)}) %collective-permute-start.3) | collective-permute-done | bytes 262176 | tf_op jit(solution)/shard_map/ppermute | solution.py:266
  52.5 4.9 %collective-permute-done.4.refs_2_.down_ref = bf16[4,256,128]{2,1,0:T(8,128)(2,1)S(1)} collective-permute-done((bf16[4,256,128]{2,1,0:T(8,128)(2,1)}, bf16[4,256,128]{2,1,0:T(8,128)(2,1)S(1)}, u32[]{:S(2)}, u32[]{:S(2)}) %collective-permute-start.4) | collective-permute-done | bytes 262176 | tf_op jit(solution)/shard_map/ppermute | solution.py:266
  57.4 4.2 %collective-permute-start.5 = (bf16[16,256,128]{2,1,0:T(8,128)(2,1)S(1)}, bf16[16,256,128]{2,1,0:T(8,128)(2,1)S(1)}, u32[]{:S(2)}, u32[]{:S(2)}) collective-permute-start(bf16[16,256,128]{2,1,0:T(8,128)(2,1)S(1)} %shard_map.138.own_ref), channel_id=1, source_target_pairs={{1,0},{0,1},{3,2},{2,3},{5,4},{4,5},{7,6},{6,7},{9,8},{8,9},{11,10... | collective-permute-start | bytes 3145736 | tf_op jit(solution)/shard_map/ppermute | solution.py:266
  62.3 0.1 reshape_squeeze.3.place_ref
  62.4 0.2 copy.25
  62.5 0.2 reshape.24.cols_ref
  62.8 0.1 stack.23.where_ref
  62.9 4.3 %collective-permute-start.6 = (bf16[4,256,128]{2,1,0:T(8,128)(2,1)}, bf16[4,256,128]{2,1,0:T(8,128)(2,1)}, u32[]{:S(2)}, u32[]{:S(2)}) collective-permute-start(bf16[4,256,128]{2,1,0:T(8,128)(2,1)} %constant_dynamic-update-slice_fusion.own_ref), channel_id=1, source_target_pairs={{32,0},{0,32},{33,1},{1,33},{34,2},{2,34},{35,3},{3,35},{36,4},{4,... | collective-permute-start | bytes 786440 | tf_op jit(solution)/shard_map/ppermute | solution.py:266
  67.2 2.4 %collective-permute-start.7 = (bf16[4,256,128]{2,1,0:T(8,128)(2,1)S(1)}, bf16[4,256,128]{2,1,0:T(8,128)(2,1)}, u32[]{:S(2)}, u32[]{:S(2)}) collective-permute-start(bf16[4,256,128]{2,1,0:T(8,128)(2,1)S(1)} %collective-permute-done.3.refs_1_.up_ref), channel_id=1, source_target_pairs={{32,0},{0,32},{33,1},{1,33},{34,2},{2,34},{35,3},{3,35},{36,4},{4,... | collective-permute-start | bytes 786440 | tf_op jit(solution)/shard_map/ppermute | solution.py:266
  69.7 4.4 %collective-permute-start.8 = (bf16[4,256,128]{2,1,0:T(8,128)(2,1)S(1)}, bf16[4,256,128]{2,1,0:T(8,128)(2,1)}, u32[]{:S(2)}, u32[]{:S(2)}) collective-permute-start(bf16[4,256,128]{2,1,0:T(8,128)(2,1)S(1)} %collective-permute-done.4.refs_2_.down_ref), channel_id=1, source_target_pairs={{32,0},{0,32},{33,1},{1,33},{34,2},{2,34},{35,3},{3,35},{36,4},{4,... | collective-permute-start | bytes 786440 | tf_op jit(solution)/shard_map/ppermute | solution.py:266
  74.0 0.0 collective-permute-done.5.other_ref
  74.0 0.0 copy-start
  74.1 2.2 %copy-done = bf16[1,1,32,256,256]{4,3,2,1,0:T(8,128)(2,1)S(1)} copy-done((bf16[1,1,32,256,256]{4,3,2,1,0:T(8,128)(2,1)S(1)}, bf16[1,1,32,256,256]{4,3,2,1,0:T(8,128)(2,1)}, u32[]{:S(2)}) %copy-start) | copy-done | bytes 4194328
  76.2 4.1 %shard_map.139 = (bf16[12,256,128]{2,1,0:T(8,128)(2,1)S(1)}, bf16[12,256,128]{2,1,0:T(8,128)(2,1)}, s32[6]{0:T(128)S(1)}) custom-call(s32[6]{0:T(128)S(1)} %stack.23.where_ref, s32[64]{0:T(128)S(1)} %reshape_squeeze.3.place_ref, s32[1536]{0:T(1024)S(1)} %reshape.24.cols_ref, bf16[32,256,256]{2,1,0:T(8,128)(2,1)S(1)} %bitcast.21, ...), custom_call_target="tpu_custom_call" | custom-call | flops 536870912 | bytes 12582912 | tf_op jit(solution)/shard_map/pallas_call | solution.py:230
  80.4 2.7 %collective-permute-start.9 = (bf16[12,256,128]{2,1,0:T(8,128)(2,1)}, bf16[12,256,128]{2,1,0:T(8,128)(2,1)S(1)}, u32[]{:S(2)}, u32[]{:S(2)}) collective-permute-start(bf16[12,256,128]{2,1,0:T(8,128)(2,1)} %get-tuple-element.28), channel_id=1, source_target_pairs={{32,0},{0,32},{33,1},{1,33},{34,2},{2,34},{35,3},{3,35},{36,4},{4,... | collective-permute-start | bytes 2359304 | tf_op jit(solution)/shard_map/ppermute | solution.py:266
  83.1 0.2 copy.26
  83.3 0.2 reshape.25.cols_ref
  83.5 0.0 collective-permute-done.7.near_up_ref
  83.5 2.2 %collective-permute-done.8.near_down_ref = bf16[4,256,128]{2,1,0:T(8,128)(2,1)} collective-permute-done((bf16[4,256,128]{2,1,0:T(8,128)(2,1)S(1)}, bf16[4,256,128]{2,1,0:T(8,128)(2,1)}, u32[]{:S(2)}, u32[]{:S(2)}) %collective-permute-start.8) | collective-permute-done | bytes 262176 | tf_op jit(solution)/shard_map/ppermute | solution.py:266
  85.7 2.2 %copy-done.1 = bf16[1,1,32,256,256]{4,3,2,1,0:T(8,128)(2,1)S(1)} copy-done((bf16[1,1,32,256,256]{4,3,2,1,0:T(8,128)(2,1)S(1)}, bf16[1,1,32,256,256]{4,3,2,1,0:T(8,128)(2,1)}, u32[]{:S(2)}) %copy-start.1) | copy-done | bytes 4194328
  87.9 3.7 %shard_map.140 = (bf16[16,256,128]{2,1,0:T(8,128)(2,1)S(1)}, bf16[8,256,128]{2,1,0:T(8,128)(2,1)S(1)}, bf16[8,256,128]{2,1,0:T(8,128)(2,1)S(1)}) custom-call(s32[6]{0:T(128)S(1)} %get-tuple-element.25.where_ref, s32[64]{0:T(128)S(1)} %reshape_squeeze.3.place_ref, s32[1536]{0:T(1024)S(1)} %reshape.25.cols_ref, bf16[32,256,256]{2,1,0:T(8,128)(2,1)S(1)} %bitcast.22, ...), custom_call_target="tpu_custom_call" | custom-call | flops 536870912 | bytes 12582912 | tf_op jit(solution)/shard_map/pallas_call | solution.py:230
  91.7 2.7 %collective-permute-start.10 = (bf16[8,256,128]{2,1,0:T(8,128)(2,1)S(1)}, bf16[8,256,128]{2,1,0:T(8,128)(2,1)S(1)}, u32[]{:S(2)}, u32[]{:S(2)}) collective-permute-start(bf16[8,256,128]{2,1,0:T(8,128)(2,1)S(1)} %get-tuple-element.30), channel_id=1, source_target_pairs={{1,0},{0,1},{3,2},{2,3},{5,4},{4,5},{7,6},{6,7},{9,8},{8,9},{11,10... | collective-permute-start | bytes 1572872 | tf_op jit(solution)/shard_map/ppermute | solution.py:266
  94.4 1.9 %collective-permute-start.11 = (bf16[8,256,128]{2,1,0:T(8,128)(2,1)S(1)}, bf16[8,256,128]{2,1,0:T(8,128)(2,1)S(1)}, u32[]{:S(2)}, u32[]{:S(2)}) collective-permute-start(bf16[8,256,128]{2,1,0:T(8,128)(2,1)S(1)} %get-tuple-element.31), channel_id=1, source_target_pairs={{1,0},{0,1},{3,2},{2,3},{5,4},{4,5},{7,6},{6,7},{9,8},{8,9},{11,10... | collective-permute-start | bytes 1572872 | tf_op jit(solution)/shard_map/ppermute | solution.py:266
  96.3 6.8 %collective-permute-done.9.near_ref = bf16[12,256,128]{2,1,0:T(8,128)(2,1)S(1)} collective-permute-done((bf16[12,256,128]{2,1,0:T(8,128)(2,1)}, bf16[12,256,128]{2,1,0:T(8,128)(2,1)S(1)}, u32[]{:S(2)}, u32[]{:S(2)}) %collective-permute-start.9) | collective-permute-done | bytes 786464 | tf_op jit(solution)/shard_map/ppermute | solution.py:266
  103.1 0.9 shard_map.141
  104.0 0.0 copy-start.2
  104.0 0.0 copy-start.4
  104.0 0.0 copy-start.5
  104.1 0.0 collective-permute-done.11.near_high_ref
  104.1 1.3 shard_map.143
  105.3 7.1 %all-to-all-start.1 = ((bf16[16,256,128]{2,1,0:T(8,128)(2,1)}), bf16[16,256,128]{2,1,0:T(8,128)(2,1)S(1)}, u32[]{:S(2)}, u32[]{:S(2)}) async-start(bf16[16,256,128]{2,1,0:T(8,128)(2,1)} %shard_map.143), calls=%async_computation.1 | async-start | bytes 2097152 | tf_op jit(solution)/shard_map/all_to_all | solution.py:359
  112.4 1.9 %collective-permute-start.12 = (bf16[4,256,128]{2,1,0:T(8,128)(2,1)}, bf16[4,256,128]{2,1,0:T(8,128)(2,1)S(1)}, u32[]{:S(2)}, u32[]{:S(2)}) collective-permute-start(bf16[4,256,128]{2,1,0:T(8,128)(2,1)} %get-tuple-element.33), channel_id=1, source_target_pairs={{704,0},{0,64},{64,128},{128,192},{192,256},{256,320},{320,384},{3... | collective-permute-start | bytes 786440 | tf_op jit(solution)/shard_map/ppermute | solution.py:266
  114.3 4.6 %collective-permute-start.13 = (bf16[4,256,128]{2,1,0:T(8,128)(2,1)}, bf16[4,256,128]{2,1,0:T(8,128)(2,1)S(1)}, u32[]{:S(2)}, u32[]{:S(2)}) collective-permute-start(bf16[4,256,128]{2,1,0:T(8,128)(2,1)} %copy-done.6), channel_id=1, source_target_pairs={{64,0},{128,64},{192,128},{256,192},{320,256},{384,320},{448,384},... | collective-permute-start | bytes 786440 | tf_op jit(solution)/shard_map/ppermute | solution.py:266
  119.0 0.1 eq.17
  119.0 3.6 %collective-permute-done.12.up_ref = bf16[4,256,128]{2,1,0:T(8,128)(2,1)S(1)} collective-permute-done((bf16[4,256,128]{2,1,0:T(8,128)(2,1)}, bf16[4,256,128]{2,1,0:T(8,128)(2,1)S(1)}, u32[]{:S(2)}, u32[]{:S(2)}) %collective-permute-start.12) | collective-permute-done | bytes 262176 | tf_op jit(solution)/shard_map/ppermute | solution.py:266
  122.6 1.0 collective-permute-done.13.down_ref
  123.6 0.7 shard_map.145
  124.3 6.4 %collective-permute-start.14 = (bf16[256,128]{1,0:T(8,128)(2,1)S(1)}, bf16[256,128]{1,0:T(8,128)(2,1)S(1)}, u32[]{:S(2)}, u32[]{:S(2)}) collective-permute-start(bf16[256,128]{1,0:T(8,128)(2,1)S(1)} %get-tuple-element.36), channel_id=1, source_target_pairs={{576,0},{640,64},{704,128},{0,192},{64,256},{128,320},{192,384},{2... | collective-permute-start | bytes 196616 | tf_op jit(solution)/shard_map/ppermute | solution.py:266
  130.7 4.3 %collective-permute-start.15 = (bf16[256,128]{1,0:T(8,128)(2,1)S(1)}, bf16[256,128]{1,0:T(8,128)(2,1)S(1)}, u32[]{:S(2)}, u32[]{:S(2)}) collective-permute-start(bf16[256,128]{1,0:T(8,128)(2,1)S(1)} %get-tuple-element.37), channel_id=1, source_target_pairs={{384,0},{448,64},{512,128},{576,192},{640,256},{704,320},{0,384},{... | collective-permute-start | bytes 196616 | tf_op jit(solution)/shard_map/ppermute | solution.py:266
  135.0 5.5 %collective-permute-start.16 = (bf16[256,128]{1,0:T(8,128)(2,1)S(1)}, bf16[256,128]{1,0:T(8,128)(2,1)S(1)}, u32[]{:S(2)}, u32[]{:S(2)}) collective-permute-start(bf16[256,128]{1,0:T(8,128)(2,1)S(1)} %get-tuple-element.38), channel_id=1, source_target_pairs={{192,0},{256,64},{320,128},{384,192},{448,256},{512,320},{576,384}... | collective-permute-start | bytes 196616 | tf_op jit(solution)/shard_map/ppermute | solution.py:266
  140.5 0.1 compare_select_fusion.projector_ref
  140.6 0.1 copy.27.mass_ref
  140.8 0.0 collective-permute-done.14.refs_1_
  140.8 4.4 %collective-permute-done.15.refs_2_ = bf16[256,128]{1,0:T(8,128)(2,1)S(1)} collective-permute-done((bf16[256,128]{1,0:T(8,128)(2,1)S(1)}, bf16[256,128]{1,0:T(8,128)(2,1)S(1)}, u32[]{:S(2)}, u32[]{:S(2)}) %collective-permute-start.15) | collective-permute-done | bytes 65568 | tf_op jit(solution)/shard_map/ppermute | solution.py:266
  145.1 0.3 shard_map.146
  145.5 0.0 all-to-all-done.1.refs_0_
  145.5 0.7 shard_map.144
  146.2 0.1 maximum_reduce_fusion
  146.4 8.4 %all_to_all.20 = f32[8,1,128]{2,1,0:T(1,128)S(1)} all-to-all(f32[8,1,128]{2,1,0:T(1,128)S(1)} %broadcast_in_dim.39), channel_id=1, replica_groups=mesh['z'=12,'xh'=2,'y'=8,'xl'=2,'core'=2] {'xh','xl','core'}, dimensions={0} | all-to-all | bytes 8192 | tf_op jit(solution)/shard_map/all_to_all | solution.py:271
  154.8 27.0 %all_to_all.21.sums_ref = f32[96,1,128]{2,1,0:T(1,128)S(1)} all-to-all(f32[96,1,128]{2,1,0:T(1,128)S(1)} %broadcast_in_dim.40), channel_id=1, replica_groups=mesh['z'=12,'xh'=2,'y'=8,'xl'=2,'core'=2] {'z','y'}, dimensions={0} | all-to-all | bytes 98304 | tf_op jit(solution)/shard_map/all_to_all | solution.py:271
  181.8 1.0 shard_map.147
  (31 shorter events, 0.1 us)
Async XLA Ops:
  0.6 61.6 %copy-start.10 = (s32[1,1,2,32]{3,2,1,0:T(2,128)S(1)}, s32[1,1,2,32]{3,2,1,0:T(2,128)}, u32[]{:S(2)}) copy-start(s32[1,1,2,32]{3,2,1,0:T(2,128)} %param.12) | copy-start | bytes 772
  0.6 61.7 %copy-start.7 = (s32[768,2]{0,1:T(2,128)S(1)}, s32[768,2]{0,1:T(2,128)}, u32[]{:S(2)}) copy-start(s32[768,2]{0,1:T(2,128)} %param.15) | copy-start | bytes 18436
  2.7 54.7 %all-to-all-start = ((bf16[16,256,128]{2,1,0:T(8,128)(2,1)}), bf16[16,256,128]{2,1,0:T(8,128)(2,1)S(1)}, u32[]{:S(2)}, u32[]{:S(2)}) async-start(bf16[16,256,128]{2,1,0:T(8,128)(2,1)} %broadcast_in_dim.36), calls=%async_computation | async-start | bytes 2097152 | tf_op jit(solution)/shard_map/all_to_all | solution.py:271
  11.4 24.1 %collective-permute-start = (bf16[1,256,128]{2,1,0:T(8,128)(2,1)}, bf16[1,256,128]{2,1,0:T(8,128)(2,1)S(1)}, u32[]{:S(2)}, u32[]{:S(2)}) collective-permute-start(bf16[1,256,128]{2,1,0:T(8,128)(2,1)} %param.19), channel_id=1, source_target_pairs={{192,0},{256,64},{320,128},{384,192},{448,256},{512,320},{576,384}... | collective-permute-start | bytes 196616 | tf_op jit(solution)/shard_map/ppermute | solution.py:266
  25.7 12.2 %collective-permute-start.1 = (bf16[1,256,128]{2,1,0:T(8,128)(2,1)}, bf16[1,256,128]{2,1,0:T(8,128)(2,1)S(1)}, u32[]{:S(2)}, u32[]{:S(2)}) collective-permute-start(bf16[1,256,128]{2,1,0:T(8,128)(2,1)} %param.19), channel_id=1, source_target_pairs={{384,0},{448,64},{512,128},{576,192},{640,256},{704,320},{0,384},{... | collective-permute-start | bytes 196616 | tf_op jit(solution)/shard_map/ppermute | solution.py:266
  28.2 10.3 %collective-permute-start.2 = (bf16[1,256,128]{2,1,0:T(8,128)(2,1)}, bf16[1,256,128]{2,1,0:T(8,128)(2,1)S(1)}, u32[]{:S(2)}, u32[]{:S(2)}) collective-permute-start(bf16[1,256,128]{2,1,0:T(8,128)(2,1)} %param.19), channel_id=1, source_target_pairs={{576,0},{640,64},{704,128},{0,192},{64,256},{128,320},{192,384},{2... | collective-permute-start | bytes 196616 | tf_op jit(solution)/shard_map/ppermute | solution.py:266
  39.1 13.4 %collective-permute-start.3 = (bf16[4,256,128]{2,1,0:T(8,128)(2,1)}, bf16[4,256,128]{2,1,0:T(8,128)(2,1)S(1)}, u32[]{:S(2)}, u32[]{:S(2)}) collective-permute-start(bf16[4,256,128]{2,1,0:T(8,128)(2,1)} %constant_dynamic-update-slice_fusion.own_ref), channel_id=1, source_target_pairs={{64,0},{128,64},{192,128},{256,192},{320,256},{384,320},{448,384},... | collective-permute-start | bytes 786440 | tf_op jit(solution)/shard_map/ppermute | solution.py:266
  47.5 9.9 %collective-permute-start.4 = (bf16[4,256,128]{2,1,0:T(8,128)(2,1)}, bf16[4,256,128]{2,1,0:T(8,128)(2,1)S(1)}, u32[]{:S(2)}, u32[]{:S(2)}) collective-permute-start(bf16[4,256,128]{2,1,0:T(8,128)(2,1)} %constant_dynamic-update-slice_fusion.own_ref), channel_id=1, source_target_pairs={{704,0},{0,64},{64,128},{128,192},{192,256},{256,320},{320,384},{3... | collective-permute-start | bytes 786440 | tf_op jit(solution)/shard_map/ppermute | solution.py:266
  57.4 25.7 %copy-start.8 = (s32[768,2]{0,1:T(2,128)S(1)}, s32[768,2]{0,1:T(2,128)}, u32[]{:S(2)}) copy-start(s32[768,2]{0,1:T(2,128)} %param.14) | copy-start | bytes 18436
  57.4 16.6 %collective-permute-start.5 = (bf16[16,256,128]{2,1,0:T(8,128)(2,1)S(1)}, bf16[16,256,128]{2,1,0:T(8,128)(2,1)S(1)}, u32[]{:S(2)}, u32[]{:S(2)}) collective-permute-start(bf16[16,256,128]{2,1,0:T(8,128)(2,1)S(1)} %shard_map.138.own_ref), channel_id=1, source_target_pairs={{1,0},{0,1},{3,2},{2,3},{5,4},{4,5},{7,6},{6,7},{9,8},{8,9},{11,10... | collective-permute-start | bytes 3145736 | tf_op jit(solution)/shard_map/ppermute | solution.py:266
  62.9 20.6 %collective-permute-start.6 = (bf16[4,256,128]{2,1,0:T(8,128)(2,1)}, bf16[4,256,128]{2,1,0:T(8,128)(2,1)}, u32[]{:S(2)}, u32[]{:S(2)}) collective-permute-start(bf16[4,256,128]{2,1,0:T(8,128)(2,1)} %constant_dynamic-update-slice_fusion.own_ref), channel_id=1, source_target_pairs={{32,0},{0,32},{33,1},{1,33},{34,2},{2,34},{35,3},{3,35},{36,4},{4,... | collective-permute-start | bytes 786440 | tf_op jit(solution)/shard_map/ppermute | solution.py:266
  67.2 16.3 %collective-permute-start.7 = (bf16[4,256,128]{2,1,0:T(8,128)(2,1)S(1)}, bf16[4,256,128]{2,1,0:T(8,128)(2,1)}, u32[]{:S(2)}, u32[]{:S(2)}) collective-permute-start(bf16[4,256,128]{2,1,0:T(8,128)(2,1)S(1)} %collective-permute-done.3.refs_1_.up_ref), channel_id=1, source_target_pairs={{32,0},{0,32},{33,1},{1,33},{34,2},{2,34},{35,3},{3,35},{36,4},{4,... | collective-permute-start | bytes 786440 | tf_op jit(solution)/shard_map/ppermute | solution.py:266
  69.7 16.1 %collective-permute-start.8 = (bf16[4,256,128]{2,1,0:T(8,128)(2,1)S(1)}, bf16[4,256,128]{2,1,0:T(8,128)(2,1)}, u32[]{:S(2)}, u32[]{:S(2)}) collective-permute-start(bf16[4,256,128]{2,1,0:T(8,128)(2,1)S(1)} %collective-permute-done.4.refs_2_.down_ref), channel_id=1, source_target_pairs={{32,0},{0,32},{33,1},{1,33},{34,2},{2,34},{35,3},{3,35},{36,4},{4,... | collective-permute-start | bytes 786440 | tf_op jit(solution)/shard_map/ppermute | solution.py:266
  74.0 2.2 %copy-start = (bf16[1,1,32,256,256]{4,3,2,1,0:T(8,128)(2,1)S(1)}, bf16[1,1,32,256,256]{4,3,2,1,0:T(8,128)(2,1)}, u32[]{:S(2)}) copy-start(bf16[1,1,32,256,256]{4,3,2,1,0:T(8,128)(2,1)} %param.11) | copy-start | bytes 12582916
  80.4 22.8 %collective-permute-start.9 = (bf16[12,256,128]{2,1,0:T(8,128)(2,1)}, bf16[12,256,128]{2,1,0:T(8,128)(2,1)S(1)}, u32[]{:S(2)}, u32[]{:S(2)}) collective-permute-start(bf16[12,256,128]{2,1,0:T(8,128)(2,1)} %get-tuple-element.28), channel_id=1, source_target_pairs={{32,0},{0,32},{33,1},{1,33},{34,2},{2,34},{35,3},{3,35},{36,4},{4,... | collective-permute-start | bytes 2359304 | tf_op jit(solution)/shard_map/ppermute | solution.py:266
  85.7 2.2 %copy-start.1 = (bf16[1,1,32,256,256]{4,3,2,1,0:T(8,128)(2,1)S(1)}, bf16[1,1,32,256,256]{4,3,2,1,0:T(8,128)(2,1)}, u32[]{:S(2)}) copy-start(bf16[1,1,32,256,256]{4,3,2,1,0:T(8,128)(2,1)} %param.11) | copy-start | bytes 12582916
  91.7 12.4 %collective-permute-start.10 = (bf16[8,256,128]{2,1,0:T(8,128)(2,1)S(1)}, bf16[8,256,128]{2,1,0:T(8,128)(2,1)S(1)}, u32[]{:S(2)}, u32[]{:S(2)}) collective-permute-start(bf16[8,256,128]{2,1,0:T(8,128)(2,1)S(1)} %get-tuple-element.30), channel_id=1, source_target_pairs={{1,0},{0,1},{3,2},{2,3},{5,4},{4,5},{7,6},{6,7},{9,8},{8,9},{11,10... | collective-permute-start | bytes 1572872 | tf_op jit(solution)/shard_map/ppermute | solution.py:266
  94.4 9.7 %collective-permute-start.11 = (bf16[8,256,128]{2,1,0:T(8,128)(2,1)S(1)}, bf16[8,256,128]{2,1,0:T(8,128)(2,1)S(1)}, u32[]{:S(2)}, u32[]{:S(2)}) collective-permute-start(bf16[8,256,128]{2,1,0:T(8,128)(2,1)S(1)} %get-tuple-element.31), channel_id=1, source_target_pairs={{1,0},{0,1},{3,2},{2,3},{5,4},{4,5},{7,6},{6,7},{9,8},{8,9},{11,10... | collective-permute-start | bytes 1572872 | tf_op jit(solution)/shard_map/ppermute | solution.py:266
  104.0 1.3 copy-start.6
  104.0 14.9 %copy-start.11 = (s32[64]{0:T(128)S(1)}, s32[64]{0:T(128)}, u32[]{:S(2)}) copy-start(s32[64]{0:T(128)} %param.16) | copy-start | bytes 772
  104.0 36.6 %copy-start.9 = (f32[1,256]{1,0:T(1,128)S(1)}, f32[1,256]{1,0:T(1,128)}, u32[]{:S(2)}) copy-start(f32[1,256]{1,0:T(1,128)} %param.17) | copy-start | bytes 3076
  104.0 41.1 %copy-start.3 = (bf16[1,256,128]{2,1,0:T(8,128)(2,1)S(1)}, bf16[1,256,128]{2,1,0:T(8,128)(2,1)}, u32[]{:S(2)}) copy-start(bf16[1,256,128]{2,1,0:T(8,128)(2,1)} %param.21) | copy-start | bytes 196612
  104.0 41.5 %copy-start.2 = (bf16[1,256,128]{2,1,0:T(8,128)(2,1)S(1)}, bf16[1,256,128]{2,1,0:T(8,128)(2,1)}, u32[]{:S(2)}) copy-start(bf16[1,256,128]{2,1,0:T(8,128)(2,1)} %param.19) | copy-start | bytes 196612
  104.0 77.8 %copy-start.4 = (bf16[1,256,128]{2,1,0:T(8,128)(2,1)S(1)}, bf16[1,256,128]{2,1,0:T(8,128)(2,1)}, u32[]{:S(2)}) copy-start(bf16[1,256,128]{2,1,0:T(8,128)(2,1)} %param.18) | copy-start | bytes 196612
  104.0 77.8 %copy-start.5 = (bf16[1,256,128]{2,1,0:T(8,128)(2,1)S(1)}, bf16[1,256,128]{2,1,0:T(8,128)(2,1)}, u32[]{:S(2)}) copy-start(bf16[1,256,128]{2,1,0:T(8,128)(2,1)} %param.20) | copy-start | bytes 196612
  105.3 40.1 %all-to-all-start.1 = ((bf16[16,256,128]{2,1,0:T(8,128)(2,1)}), bf16[16,256,128]{2,1,0:T(8,128)(2,1)S(1)}, u32[]{:S(2)}, u32[]{:S(2)}) async-start(bf16[16,256,128]{2,1,0:T(8,128)(2,1)} %shard_map.143), calls=%async_computation.1 | async-start | bytes 2097152 | tf_op jit(solution)/shard_map/all_to_all | solution.py:359
  112.4 10.2 %collective-permute-start.12 = (bf16[4,256,128]{2,1,0:T(8,128)(2,1)}, bf16[4,256,128]{2,1,0:T(8,128)(2,1)S(1)}, u32[]{:S(2)}, u32[]{:S(2)}) collective-permute-start(bf16[4,256,128]{2,1,0:T(8,128)(2,1)} %get-tuple-element.33), channel_id=1, source_target_pairs={{704,0},{0,64},{64,128},{128,192},{192,256},{256,320},{320,384},{3... | collective-permute-start | bytes 786440 | tf_op jit(solution)/shard_map/ppermute | solution.py:266
  114.3 9.3 %collective-permute-start.13 = (bf16[4,256,128]{2,1,0:T(8,128)(2,1)}, bf16[4,256,128]{2,1,0:T(8,128)(2,1)S(1)}, u32[]{:S(2)}, u32[]{:S(2)}) collective-permute-start(bf16[4,256,128]{2,1,0:T(8,128)(2,1)} %copy-done.6), channel_id=1, source_target_pairs={{64,0},{128,64},{192,128},{256,192},{320,256},{384,320},{448,384},... | collective-permute-start | bytes 786440 | tf_op jit(solution)/shard_map/ppermute | solution.py:266
  124.3 16.5 %collective-permute-start.14 = (bf16[256,128]{1,0:T(8,128)(2,1)S(1)}, bf16[256,128]{1,0:T(8,128)(2,1)S(1)}, u32[]{:S(2)}, u32[]{:S(2)}) collective-permute-start(bf16[256,128]{1,0:T(8,128)(2,1)S(1)} %get-tuple-element.36), channel_id=1, source_target_pairs={{576,0},{640,64},{704,128},{0,192},{64,256},{128,320},{192,384},{2... | collective-permute-start | bytes 196616 | tf_op jit(solution)/shard_map/ppermute | solution.py:266
  130.7 14.4 %collective-permute-start.15 = (bf16[256,128]{1,0:T(8,128)(2,1)S(1)}, bf16[256,128]{1,0:T(8,128)(2,1)S(1)}, u32[]{:S(2)}, u32[]{:S(2)}) collective-permute-start(bf16[256,128]{1,0:T(8,128)(2,1)S(1)} %get-tuple-element.37), channel_id=1, source_target_pairs={{384,0},{448,64},{512,128},{576,192},{640,256},{704,320},{0,384},{... | collective-permute-start | bytes 196616 | tf_op jit(solution)/shard_map/ppermute | solution.py:266
  135.0 10.1 %collective-permute-start.16 = (bf16[256,128]{1,0:T(8,128)(2,1)S(1)}, bf16[256,128]{1,0:T(8,128)(2,1)S(1)}, u32[]{:S(2)}, u32[]{:S(2)}) collective-permute-start(bf16[256,128]{1,0:T(8,128)(2,1)S(1)} %get-tuple-element.38), channel_id=1, source_target_pairs={{192,0},{256,64},{320,128},{384,192},{448,256},{512,320},{576,384}... | collective-permute-start | bytes 196616 | tf_op jit(solution)/shard_map/ppermute | solution.py:266

commit v3 on v2

--- a/solution.py
+++ b/solution.py
@@ -20,6 +20,7 @@
 SWAP = ((0, 1), (1, 0))
 
 VMEM = pl.BlockSpec(memory_space=pltpu.VMEM)
+HBM = pl.BlockSpec(memory_space=pltpu.HBM)
 SMEM = pl.BlockSpec(memory_space=pltpu.SMEM)
 COST = pl.CostEstimate(flops=2**29, bytes_accessed=12 * 2**20, transcendentals=0)
 MIB = 2**20
@@ -52,70 +53,77 @@
     lax.fori_loop(0, acc_ref.shape[0], body, 0)
 
 
-def each_match(where_ref, place_ref, cols_ref, slots, turn, product):
+def each_match(where_ref, place_ref, cols_ref, a_ref, turn, choose, scratch, product):
+    acc_ref, held_ref, tiles_ref, held_sems, tile_sems = scratch
     count, row_id, col_id = where_ref[0], where_ref[3], where_ref[4]
-
-    def body(a, carry):
-        local_row, local_col = place_ref[a], place_ref[slots + a]
-        tile_row = row_id * N_COL + local_row
-        tile_col = local_col * N_COL + col_id
-        source, target = (tile_row, tile_col) if turn else (tile_col, tile_row)
-        straight, crossed = matches(cols_ref, source, target)
-
-        @pl.when(straight[0] + straight[1] + crossed[0] + crossed[1] > 0)
+    slots = a_ref.shape[0]
+    hold = lambda a: pltpu.make_async_copy(a_ref.at[a], held_ref.at[a], held_sems.at[a])
+    take = lambda a, ref, index: pltpu.make_async_copy(
+        ref.at[index], tiles_ref.at[a], tile_sems.at[a]
+    )
+
+    def each(act):
+        def body(a, carry):
+            local_row, local_col = place_ref[a], place_ref[slots + a]
+            tile_row = row_id * N_COL + local_row
+            tile_col = local_col * N_COL + col_id
+            source, target = (tile_row, tile_col) if turn else (tile_col, tile_row)
+            straight, crossed = matches(cols_ref, source, target)
+
+            @pl.when(straight[0] + straight[1] + crossed[0] + crossed[1] > 0)
+            def _():
+                act(a, local_row, local_col, straight, crossed)
+
+            return carry
+
+        lax.fori_loop(0, count, body, 0)
+
+    def start(a, local_row, local_col, straight, crossed):
+        hold(a).start()
+        here, own_ref, other_ref, index = choose(local_row, local_col)
+
+        @pl.when(here)
         def _():
-            product(a, local_row, local_col, straight, crossed)
-
-        return carry
-
-    lax.fori_loop(0, count, body, 0)
-
-
-def fetch(tile_ref, choices):
-    for holds, ref, index in choices:
-
-        @pl.when(holds)
-        def _(ref=ref, index=index):
-            tile_ref[...] = ref[index]
+            take(a, own_ref, index).start()
+
+        @pl.when(jnp.logical_not(here))
+        def _():
+            take(a, other_ref, index).start()
+
+    def finish(a, local_row, local_col, straight, crossed):
+        here, own_ref, other_ref, index = choose(local_row, local_col)
+        take(a, own_ref, index).wait()
+        picked = pick_columns(tiles_ref[a], straight, crossed)
+        hold(a).wait()
+        product(held_ref[a], picked, local_row, local_col)
+
+    each(start)
+    clear(acc_ref)
+    each(finish)
 
 
 def prolong_kernel(
     where_ref,
     place_ref,
     cols_ref,
+    own_ref,
+    other_ref,
     a_ref,
-    own_ref,
-    up_ref,
-    down_ref,
-    near_own_ref,
-    near_up_ref,
-    near_down_ref,
     mine_ref,
     theirs_low_ref,
     theirs_high_ref,
-    acc_ref,
-    tile_ref,
+    *scratch,
 ):
-    xh, core, z = where_ref[1], where_ref[2], where_ref[5]
-    clear(acc_ref)
-
-    def product(a, local_row, local_col, straight, crossed):
-        here = lax.rem(local_col, N_XH) == xh
-        ahead = lax.rem(local_col // N_XH - z + N_Z, N_Z)
-        third = lax.rem(ahead, 3)
-        choices = []
-        for side, refs in (
-            (here, (own_ref, up_ref, down_ref)),
-            (jnp.logical_not(here), (near_own_ref, near_up_ref, near_down_ref)),
-        ):
-            for k, offset in enumerate((0, 1, -1)):
-                index = lax.rem(ahead - offset + N_Z, N_Z) // 3
-                choices.append((side & (third == k), refs[k], index))
-        fetch(tile_ref, choices)
-        picked = pick_columns(tile_ref[...], straight, crossed)
-        acc_ref[local_row] += jnp.dot(a_ref[a], picked, preferred_element_type=jnp.float32)
-
-    each_match(where_ref, place_ref, cols_ref, a_ref.shape[0], False, product)
+    xh, core = where_ref[1], where_ref[2]
+    acc_ref = scratch[0]
+
+    def choose(local_row, local_col):
+        return lax.rem(local_col, N_XH) == xh, own_ref, other_ref, local_col // N_XH
+
+    def product(block, picked, local_row, local_col):
+        acc_ref[local_row] += jnp.dot(block, picked, preferred_element_type=jnp.float32)
+
+    each_match(where_ref, place_ref, cols_ref, a_ref, False, choose, scratch, product)
 
     def store(q, carry):
         mine_ref[q] = acc_ref[2 * q + core].astype(jnp.bfloat16)
@@ -135,30 +143,28 @@
     where_ref,
     place_ref,
     cols_ref,
-    a_ref,
     own_ref,
     other_ref,
+    a_ref,
     mine_ref,
     theirs_ref,
     after_ref,
-    acc_ref,
-    tile_ref,
+    *scratch,
 ):
     for i in range(where_ref.shape[0]):
         after_ref[i] = where_ref[i]
     xh, core, z = where_ref[1], where_ref[2], where_ref[5]
-    clear(acc_ref)
-
-    def product(a, local_row, local_col, straight, crossed):
-        here = lax.rem(local_row, N_CORE) == core
-        index = local_row // N_CORE
-        fetch(tile_ref, [(here, own_ref, index), (jnp.logical_not(here), other_ref, index)])
-        picked = pick_columns(tile_ref[...], straight, crossed)
+    acc_ref = scratch[0]
+
+    def choose(local_row, local_col):
+        return lax.rem(local_row, N_CORE) == core, own_ref, other_ref, local_row // N_CORE
+
+    def product(block, picked, local_row, local_col):
         acc_ref[local_col] += lax.dot_general(
-            a_ref[a], picked, (((0,), (0,)), ((), ())), preferred_element_type=jnp.float32
+            block, picked, (((0,), (0,)), ((), ())), preferred_element_type=jnp.float32
         )
 
-    each_match(where_ref, place_ref, cols_ref, a_ref.shape[0], True, product)
+    each_match(where_ref, place_ref, cols_ref, a_ref, True, choose, scratch, product)
 
     def store(q, carry):
         owner = 3 * lax.rem(q, 4) + lax.rem(z + q // 4, 3)
@@ -225,17 +231,19 @@
     return jax.ShapeDtypeStruct(dims, dtype)
 
 
-def on_device(kernel, out_shape, scalars, *operands, scratch=(), cost=None, scalars_out=0, mib=6):
+def on_device(
+    kernel, out_shape, scalars, *operands, left=(), scratch=(), cost=None, scalars_out=0, mib=6
+):
     count = len(out_shape)
     return pl.pallas_call(
         kernel,
         out_shape=out_shape,
-        in_specs=[SMEM] * len(scalars) + [VMEM] * len(operands),
+        in_specs=[SMEM] * len(scalars) + [VMEM] * len(operands) + [HBM] * len(left),
         out_specs=(VMEM,) * (count - scalars_out) + (SMEM,) * scalars_out,
         scratch_shapes=scratch,
         cost_estimate=cost,
         compiler_params=pltpu.CompilerParams(vmem_limit_bytes=mib * MIB),
-    )(*scalars, *operands)
+    )(*scalars, *operands, *left)
 
 
 def after(array, *earlier):
@@ -308,25 +316,28 @@
     height, width = res_p.shape[1:]
     p_flat, r_flat = p_cols.reshape(-1), r_cols.reshape(-1)
     tile = shape((height, width))
-    tile_scratch = pltpu.VMEM((height, width), jnp.bfloat16)
+    slots = tile_vals.shape[0]
+    scratch = (
+        pltpu.VMEM(tile_vals.shape, jnp.bfloat16),
+        pltpu.VMEM((slots, height, width), jnp.bfloat16),
+        pltpu.SemaphoreType.DMA((slots,)),
+        pltpu.SemaphoreType.DMA((slots,)),
+    )
 
     r_own = gather(res_r, ("y", "xl"), HALF_COL)
-    own = jnp.concatenate([res_p] + [turned(res_p, "z", by) for by in (3, 6, 9)])
-    thirds = (own, turned(own, "z", 1), turned(own, "z", -1))
-    near = tuple(turned(third, "xh", 1) for third in thirds)
-    r_own = after(r_own, *thirds[1:])
+    p_own = lax.all_gather(res_p, "z", axis=0, tiled=True)
+    p_other = turned(p_own, "xh", 1)
+    r_own = after(r_own, p_own)
     r_other = turned(r_own, "core", 1)
 
     r_mine, r_theirs, where_then = on_device(
         restrict_kernel,
         (shape((N_Z, height, width)),) * 2 + (shape(where.shape, jnp.int32),),
         (where, place, r_flat),
-        tile_vals,
-        r_own,
-        r_other,
-        scratch=[pltpu.VMEM((N_ROW, height, width), jnp.float32), tile_scratch],
+        left=(r_own, r_other, tile_vals),
+        scratch=[pltpu.VMEM((N_ROW, height, width), jnp.float32), *scratch],
         cost=COST,
-        mib=18,
+        mib=48,
         scalars_out=1,
     )
     r_near = turned(r_theirs, "xh", 1)
@@ -334,12 +345,10 @@
         prolong_kernel,
         (shape((HALF_COL, height, width)),) + (shape((HALF_COL // 2, height, width)),) * 2,
         (where_then, place, p_flat),
-        tile_vals,
-        *thirds,
-        *near,
-        scratch=[pltpu.VMEM((N_COL, height, width), jnp.float32), tile_scratch],
+        left=(p_own, p_other, tile_vals),
+        scratch=[pltpu.VMEM((N_COL, height, width), jnp.float32), *scratch],
         cost=COST,
-        mib=18,
+        mib=48,
     )
     p_near = (turned(p_low, "core", 1), turned(p_high, "core", 1))
 

time: 184 us -> 171 us (0.929)
  blocking collectives: 35.4 us -> 68.8 us
  starting transfers between devices: 94 us -> 62.8 us
  waiting for transfers between devices: 27.7 us -> 18.9 us
  local copies, waits for them, and re-layouts: 11.1 us -> 4.25 us
    ppermute x17 -> x10, starting transfers between devices: 78.2 us -> 44.6 us  [turned(): lax.ppermute(array, axis, [((i + by) % size, i) for i in range(size)])]
    all_gather x0 -> x1, blocking collectives: none -> 33 us  [shards(): p_own = lax.all_gather(res_p, 'z', axis=0, tiled=True)]
    ppermute x17 -> x10, waiting for transfers between devices: 27.7 us -> 18.9 us  [turned(): lax.ppermute(array, axis, [((i + by) % size, i) for i in range(size)])]
    unnamed x29 -> x24, local copies, waits for them, and re-layouts: 7.53 us -> 1.3 us
    all_to_all x1, starting transfers between devices: 7.07 us -> 9.5 us  [shards(): p_parts = [lax.all_to_all(p_sum, ('y', 'xl'), 0, 0, tiled=True)]]
  transfers between devices with their start and end apart: 19 -> 12, of which waited for: 8 -> 6; matrix products, arithmetic and copies ran while one was open for 3% -> 1% of each run, Pallas kernels for 5% -> 6%
where the time goes in v3:
time: 171 us; the launch traced here: 170 us
  blocking collectives  68.8 us (40%)
  starting transfers between devices  62.8 us (37%)
  waiting for transfers between devices  18.9 us (11%)
  Pallas kernels  13.5 us (8%)
  local copies, waits for them, and re-layouts  4.25 us (2%)
    ppermute x10, starting transfers between devices, turned(): lax.ppermute(array, axis, [((i + by) % size, i) for i in range(size)])  44.6 us
    all_to_all x2, blocking collectives, gather(): return lax.all_to_all(copies, axes, 0, 0, tiled=True)  35.8 us
    all_gather x1, blocking collectives, shards(): p_own = lax.all_gather(res_p, 'z', axis=0, tiled=True)  33 us
    ppermute x10, waiting for transfers between devices, turned(): lax.ppermute(array, axis, [((i + by) % size, i) for i in range(size)])  18.9 us
    pallas_call x8, Pallas kernels, on_device(): pl.pallas_call(kernel, out_shape=out_shape, in_specs=[SMEM] * len(scalars...  13.5 us
    all_to_all x1, starting transfers between devices, shards(): p_parts = [lax.all_to_all(p_sum, ('y', 'xl'), 0, 0, tiled=True)]  9.5 us
    all_to_all x1, starting transfers between devices, gather(): return lax.all_to_all(copies, axes, 0, 0, tiled=True)  8.68 us
  transfers between devices with their start and end apart: 12, of which 6 were waited for; matrix products, arithmetic and copies ran while one was open for 1% of the time, Pallas kernels for 6%

profile of v3, /device:TPU:1, one launch (start us, length us, event | category | flops | bytes accessed | tf_op | source)
XLA Modules:
  0.0 170.2 jit_solution(16567764837867977481)
XLA Ops:
  0.6 0.0 copy-start.9
  0.6 0.0 copy-start.6
  0.7 2.1 %broadcast_in_dim.36 = bf16[16,256,128]{2,1,0:T(8,128)(2,1)} broadcast(bf16[256,128]{1,0:T(8,128)(2,1)} %bitcast.21), dimensions={1,2} | broadcast | bytes 1114112 | tf_op jit(solution)/shard_map/broadcast_in_dim | solution.py:278
  2.7 8.7 %all-to-all-start = ((bf16[16,256,128]{2,1,0:T(8,128)(2,1)}), bf16[16,256,128]{2,1,0:T(8,128)(2,1)S(1)}, u32[]{:S(2)}, u32[]{:S(2)}) async-start(bf16[16,256,128]{2,1,0:T(8,128)(2,1)} %broadcast_in_dim.36), calls=%async_computation | async-start | bytes 2097152 | tf_op jit(solution)/shard_map/all_to_all | solution.py:279
  11.4 33.0 %all_gather.3.refs_1_.own_ref = bf16[12,256,128]{2,1,0:T(8,128)(2,1)S(1)} all-gather(bf16[1,256,128]{2,1,0:T(8,128)(2,1)} %param.19), channel_id=1, replica_groups=mesh['z'=12,'xh'=2,'y'=8,'xl'=2,'core'=2] {'z'}, dimensions={0}, use_global_device_ids=true | all-gather | bytes 851968 | tf_op jit(solution)/shard_map/all_gather | solution.py:328
  44.4 0.0 all-to-all-done.refs_0_
  44.4 7.6 %collective-permute-start = (bf16[16,256,128]{2,1,0:T(8,128)(2,1)S(1)}, bf16[16,256,128]{2,1,0:T(8,128)(2,1)S(1)}, u32[]{:S(2)}, u32[]{:S(2)}) collective-permute-start(bf16[16,256,128]{2,1,0:T(8,128)(2,1)S(1)} %shard_map.138.own_ref), channel_id=1, source_target_pairs={{1,0},{0,1},{3,2},{2,3},{5,4},{4,5},{7,6},{6,7},{9,8},{8,9},{11,10... | collective-permute-start | bytes 3145736 | tf_op jit(solution)/shard_map/ppermute | solution.py:274
  52.0 4.4 %collective-permute-start.1 = (bf16[12,256,128]{2,1,0:T(8,128)(2,1)S(1)}, bf16[12,256,128]{2,1,0:T(8,128)(2,1)}, u32[]{:S(2)}, u32[]{:S(2)}) collective-permute-start(bf16[12,256,128]{2,1,0:T(8,128)(2,1)S(1)} %all_gather.3.refs_1_.own_ref), channel_id=1, source_target_pairs={{32,0},{0,32},{33,1},{1,33},{34,2},{2,34},{35,3},{3,35},{36,4},{4,... | collective-permute-start | bytes 2359304 | tf_op jit(solution)/shard_map/ppermute | solution.py:274
  57.0 0.0 copy-done.9
  57.0 0.1 reshape_squeeze.3.place_ref
  57.1 0.0 copy-done.6
  57.1 0.2 copy.29
  57.3 0.2 reshape.24.cols_ref
  57.5 0.1 stack.23.where_ref
  57.6 0.0 collective-permute-done.other_ref
  57.6 5.0 %shard_map.139 = (bf16[12,256,128]{2,1,0:T(8,128)(2,1)S(1)}, bf16[12,256,128]{2,1,0:T(8,128)(2,1)}, s32[6]{0:T(128)S(1)}) custom-call(s32[6]{0:T(128)S(1)} %stack.23.where_ref, s32[64]{0:T(128)S(1)} %reshape_squeeze.3.place_ref, s32[1536]{0:T(1024)S(1)} %reshape.24.cols_ref, bf16[16,256,128]{2,1,0:T(8,128)(2,1)S(1)} %shard_map.138.own_ref, ...), custom_call_target="tpu_custom_call" | custom-call | flops 536870912 | bytes 12582912 | tf_op jit(solution)/shard_map/pallas_call | solution.py:238
  62.6 0.0 copy-start
  62.6 0.9 copy-done
  63.5 4.8 %collective-permute-start.2 = (bf16[12,256,128]{2,1,0:T(8,128)(2,1)}, bf16[12,256,128]{2,1,0:T(8,128)(2,1)S(1)}, u32[]{:S(2)}, u32[]{:S(2)}) collective-permute-start(bf16[12,256,128]{2,1,0:T(8,128)(2,1)} %get-tuple-element.28), channel_id=1, source_target_pairs={{32,0},{0,32},{33,1},{1,33},{34,2},{2,34},{35,3},{3,35},{36,4},{4,... | collective-permute-start | bytes 2359304 | tf_op jit(solution)/shard_map/ppermute | solution.py:274
  68.3 0.0 copy-done.7
  68.3 0.2 copy.30
  68.5 0.2 reshape.25.cols_ref
  68.7 5.9 %collective-permute-done.1.other_ref = bf16[12,256,128]{2,1,0:T(8,128)(2,1)} collective-permute-done((bf16[12,256,128]{2,1,0:T(8,128)(2,1)S(1)}, bf16[12,256,128]{2,1,0:T(8,128)(2,1)}, u32[]{:S(2)}, u32[]{:S(2)}) %collective-permute-start.1) | collective-permute-done | bytes 786464 | tf_op jit(solution)/shard_map/ppermute | solution.py:274
  74.6 4.4 %shard_map.140 = (bf16[16,256,128]{2,1,0:T(8,128)(2,1)S(1)}, bf16[8,256,128]{2,1,0:T(8,128)(2,1)S(1)}, bf16[8,256,128]{2,1,0:T(8,128)(2,1)S(1)}) custom-call(s32[6]{0:T(128)S(1)} %get-tuple-element.25.where_ref, s32[64]{0:T(128)S(1)} %reshape_squeeze.3.place_ref, s32[1536]{0:T(1024)S(1)} %reshape.25.cols_ref, ...), custom_call_target="tpu_custom_call" | custom-call | flops 536870912 | bytes 12582912 | tf_op jit(solution)/shard_map/pallas_call | solution.py:238
  79.0 6.3 %collective-permute-start.3 = (bf16[8,256,128]{2,1,0:T(8,128)(2,1)S(1)}, bf16[8,256,128]{2,1,0:T(8,128)(2,1)S(1)}, u32[]{:S(2)}, u32[]{:S(2)}) collective-permute-start(bf16[8,256,128]{2,1,0:T(8,128)(2,1)S(1)} %get-tuple-element.30), channel_id=1, source_target_pairs={{1,0},{0,1},{3,2},{2,3},{5,4},{4,5},{7,6},{6,7},{9,8},{8,9},{11,10... | collective-permute-start | bytes 1572872 | tf_op jit(solution)/shard_map/ppermute | solution.py:274
  85.4 1.9 %collective-permute-start.4 = (bf16[8,256,128]{2,1,0:T(8,128)(2,1)S(1)}, bf16[8,256,128]{2,1,0:T(8,128)(2,1)S(1)}, u32[]{:S(2)}, u32[]{:S(2)}) collective-permute-start(bf16[8,256,128]{2,1,0:T(8,128)(2,1)S(1)} %get-tuple-element.31), channel_id=1, source_target_pairs={{1,0},{0,1},{3,2},{2,3},{5,4},{4,5},{7,6},{6,7},{9,8},{8,9},{11,10... | collective-permute-start | bytes 1572872 | tf_op jit(solution)/shard_map/ppermute | solution.py:274
  87.3 2.4 %collective-permute-done.2.near_ref = bf16[12,256,128]{2,1,0:T(8,128)(2,1)S(1)} collective-permute-done((bf16[12,256,128]{2,1,0:T(8,128)(2,1)}, bf16[12,256,128]{2,1,0:T(8,128)(2,1)S(1)}, u32[]{:S(2)}, u32[]{:S(2)}) %collective-permute-start.2) | collective-permute-done | bytes 786464 | tf_op jit(solution)/shard_map/ppermute | solution.py:274
  89.7 0.0 copy-done.1
  89.7 0.2 shard_map.141
  89.9 0.0 copy-start.10
  89.9 0.0 copy-start.8
  89.9 0.0 copy-start.2
  89.9 0.0 copy-start.3
  90.0 0.0 copy-start.4
  90.0 0.0 copy-start.5
  90.0 0.0 collective-permute-done.3.near_low_ref
  90.0 0.0 collective-permute-done.4.near_high_ref
  90.0 1.3 shard_map.143
  91.3 9.5 %all-to-all-start.1 = ((bf16[16,256,128]{2,1,0:T(8,128)(2,1)}), bf16[16,256,128]{2,1,0:T(8,128)(2,1)S(1)}, u32[]{:S(2)}, u32[]{:S(2)}) async-start(bf16[16,256,128]{2,1,0:T(8,128)(2,1)} %shard_map.143), calls=%async_computation.1 | async-start | bytes 2097152 | tf_op jit(solution)/shard_map/all_to_all | solution.py:368
  100.8 1.9 %collective-permute-start.5 = (bf16[4,256,128]{2,1,0:T(8,128)(2,1)S(1)}, bf16[4,256,128]{2,1,0:T(8,128)(2,1)S(1)}, u32[]{:S(2)}, u32[]{:S(2)}) collective-permute-start(bf16[4,256,128]{2,1,0:T(8,128)(2,1)S(1)} %get-tuple-element.33), channel_id=1, source_target_pairs={{704,0},{0,64},{64,128},{128,192},{192,256},{256,320},{320,384},{3... | collective-permute-start | bytes 786440 | tf_op jit(solution)/shard_map/ppermute | solution.py:274
  102.7 4.6 %collective-permute-start.6 = (bf16[4,256,128]{2,1,0:T(8,128)(2,1)S(1)}, bf16[4,256,128]{2,1,0:T(8,128)(2,1)S(1)}, u32[]{:S(2)}, u32[]{:S(2)}) collective-permute-start(bf16[4,256,128]{2,1,0:T(8,128)(2,1)S(1)} %get-tuple-element.34), channel_id=1, source_target_pairs={{64,0},{128,64},{192,128},{256,192},{320,256},{384,320},{448,384},... | collective-permute-start | bytes 786440 | tf_op jit(solution)/shard_map/ppermute | solution.py:274
  107.3 0.0 copy-done.10
  107.4 0.1 eq.17
  107.4 3.2 %collective-permute-done.5.up_ref = bf16[4,256,128]{2,1,0:T(8,128)(2,1)S(1)} collective-permute-done((bf16[4,256,128]{2,1,0:T(8,128)(2,1)S(1)}, bf16[4,256,128]{2,1,0:T(8,128)(2,1)S(1)}, u32[]{:S(2)}, u32[]{:S(2)}) %collective-permute-start.5) | collective-permute-done | bytes 262176 | tf_op jit(solution)/shard_map/ppermute | solution.py:274
  110.6 0.9 collective-permute-done.6.down_ref
  111.5 0.7 shard_map.145
  112.2 3.8 %collective-permute-start.7 = (bf16[256,128]{1,0:T(8,128)(2,1)S(1)}, bf16[256,128]{1,0:T(8,128)(2,1)S(1)}, u32[]{:S(2)}, u32[]{:S(2)}) collective-permute-start(bf16[256,128]{1,0:T(8,128)(2,1)S(1)} %get-tuple-element.36), channel_id=1, source_target_pairs={{576,0},{640,64},{704,128},{0,192},{64,256},{128,320},{192,384},{2... | collective-permute-start | bytes 196616 | tf_op jit(solution)/shard_map/ppermute | solution.py:274
  116.0 6.1 %collective-permute-start.8 = (bf16[256,128]{1,0:T(8,128)(2,1)S(1)}, bf16[256,128]{1,0:T(8,128)(2,1)S(1)}, u32[]{:S(2)}, u32[]{:S(2)}) collective-permute-start(bf16[256,128]{1,0:T(8,128)(2,1)S(1)} %get-tuple-element.37), channel_id=1, source_target_pairs={{384,0},{448,64},{512,128},{576,192},{640,256},{704,320},{0,384},{... | collective-permute-start | bytes 196616 | tf_op jit(solution)/shard_map/ppermute | solution.py:274
  122.1 3.3 %collective-permute-start.9 = (bf16[256,128]{1,0:T(8,128)(2,1)S(1)}, bf16[256,128]{1,0:T(8,128)(2,1)S(1)}, u32[]{:S(2)}, u32[]{:S(2)}) collective-permute-start(bf16[256,128]{1,0:T(8,128)(2,1)S(1)} %get-tuple-element.38), channel_id=1, source_target_pairs={{192,0},{256,64},{320,128},{384,192},{448,256},{512,320},{576,384}... | collective-permute-start | bytes 196616 | tf_op jit(solution)/shard_map/ppermute | solution.py:274
  125.4 0.1 compare_select_fusion.projector_ref
  125.5 0.0 copy-done.8
  125.5 0.1 copy.31.mass_ref
  125.6 0.0 collective-permute-done.7.refs_1_
  125.6 1.9 %collective-permute-done.8.refs_2_ = bf16[256,128]{1,0:T(8,128)(2,1)S(1)} collective-permute-done((bf16[256,128]{1,0:T(8,128)(2,1)S(1)}, bf16[256,128]{1,0:T(8,128)(2,1)S(1)}, u32[]{:S(2)}, u32[]{:S(2)}) %collective-permute-start.8) | collective-permute-done | bytes 65568 | tf_op jit(solution)/shard_map/ppermute | solution.py:274
  127.5 4.6 %collective-permute-done.9.refs_3_ = bf16[256,128]{1,0:T(8,128)(2,1)S(1)} collective-permute-done((bf16[256,128]{1,0:T(8,128)(2,1)S(1)}, bf16[256,128]{1,0:T(8,128)(2,1)S(1)}, u32[]{:S(2)}, u32[]{:S(2)}) %collective-permute-start.9) | collective-permute-done | bytes 65568 | tf_op jit(solution)/shard_map/ppermute | solution.py:274
  132.1 0.0 copy-done.2
  132.1 0.3 shard_map.146
  132.4 0.0 all-to-all-done.1.refs_0_
  132.5 0.7 shard_map.144
  133.2 0.1 maximum_reduce_fusion
  133.3 9.0 %all_to_all.20 = f32[8,1,128]{2,1,0:T(1,128)S(1)} all-to-all(f32[8,1,128]{2,1,0:T(1,128)S(1)} %broadcast_in_dim.39), channel_id=1, replica_groups=mesh['z'=12,'xh'=2,'y'=8,'xl'=2,'core'=2] {'xh','xl','core'}, dimensions={0} | all-to-all | bytes 8192 | tf_op jit(solution)/shard_map/all_to_all | solution.py:279
  142.4 26.9 %all_to_all.21.sums_ref = f32[96,1,128]{2,1,0:T(1,128)S(1)} all-to-all(f32[96,1,128]{2,1,0:T(1,128)S(1)} %broadcast_in_dim.40), channel_id=1, replica_groups=mesh['z'=12,'xh'=2,'y'=8,'xl'=2,'core'=2] {'z','y'}, dimensions={0} | all-to-all | bytes 98304 | tf_op jit(solution)/shard_map/all_to_all | solution.py:279
  169.2 0.0 copy-done.4
  169.2 1.0 shard_map.147
  (12 shorter events, 0.1 us)
Async XLA Ops:
  0.6 56.4 %copy-start.9 = (s32[1,1,2,32]{3,2,1,0:T(2,128)S(1)}, s32[1,1,2,32]{3,2,1,0:T(2,128)}, u32[]{:S(2)}) copy-start(s32[1,1,2,32]{3,2,1,0:T(2,128)} %param.12) | copy-start | bytes 772
  0.6 56.4 %copy-start.6 = (s32[768,2]{0,1:T(2,128)S(1)}, s32[768,2]{0,1:T(2,128)}, u32[]{:S(2)}) copy-start(s32[768,2]{0,1:T(2,128)} %param.15) | copy-start | bytes 18436
  2.7 41.7 %all-to-all-start = ((bf16[16,256,128]{2,1,0:T(8,128)(2,1)}), bf16[16,256,128]{2,1,0:T(8,128)(2,1)S(1)}, u32[]{:S(2)}, u32[]{:S(2)}) async-start(bf16[16,256,128]{2,1,0:T(8,128)(2,1)} %broadcast_in_dim.36), calls=%async_computation | async-start | bytes 2097152 | tf_op jit(solution)/shard_map/all_to_all | solution.py:279
  44.4 23.9 %copy-start.7 = (s32[768,2]{0,1:T(2,128)S(1)}, s32[768,2]{0,1:T(2,128)}, u32[]{:S(2)}) copy-start(s32[768,2]{0,1:T(2,128)} %param.14) | copy-start | bytes 18436
  44.4 13.2 %collective-permute-start = (bf16[16,256,128]{2,1,0:T(8,128)(2,1)S(1)}, bf16[16,256,128]{2,1,0:T(8,128)(2,1)S(1)}, u32[]{:S(2)}, u32[]{:S(2)}) collective-permute-start(bf16[16,256,128]{2,1,0:T(8,128)(2,1)S(1)} %shard_map.138.own_ref), channel_id=1, source_target_pairs={{1,0},{0,1},{3,2},{2,3},{5,4},{4,5},{7,6},{6,7},{9,8},{8,9},{11,10... | collective-permute-start | bytes 3145736 | tf_op jit(solution)/shard_map/ppermute | solution.py:274
  52.0 22.7 %collective-permute-start.1 = (bf16[12,256,128]{2,1,0:T(8,128)(2,1)S(1)}, bf16[12,256,128]{2,1,0:T(8,128)(2,1)}, u32[]{:S(2)}, u32[]{:S(2)}) collective-permute-start(bf16[12,256,128]{2,1,0:T(8,128)(2,1)S(1)} %all_gather.3.refs_1_.own_ref), channel_id=1, source_target_pairs={{32,0},{0,32},{33,1},{1,33},{34,2},{2,34},{35,3},{3,35},{36,4},{4,... | collective-permute-start | bytes 2359304 | tf_op jit(solution)/shard_map/ppermute | solution.py:274
  62.6 0.9 copy-start
  63.5 26.2 %copy-start.1 = (bf16[12,256,128]{2,1,0:T(8,128)(2,1)S(1)}, bf16[12,256,128]{2,1,0:T(8,128)(2,1)}, u32[]{:S(2)}) copy-start(bf16[12,256,128]{2,1,0:T(8,128)(2,1)} %copy-done) | copy-start | bytes 2359300
  63.5 26.2 %collective-permute-start.2 = (bf16[12,256,128]{2,1,0:T(8,128)(2,1)}, bf16[12,256,128]{2,1,0:T(8,128)(2,1)S(1)}, u32[]{:S(2)}, u32[]{:S(2)}) collective-permute-start(bf16[12,256,128]{2,1,0:T(8,128)(2,1)} %get-tuple-element.28), channel_id=1, source_target_pairs={{32,0},{0,32},{33,1},{1,33},{34,2},{2,34},{35,3},{3,35},{36,4},{4,... | collective-permute-start | bytes 2359304 | tf_op jit(solution)/shard_map/ppermute | solution.py:274
  79.0 10.9 %collective-permute-start.3 = (bf16[8,256,128]{2,1,0:T(8,128)(2,1)S(1)}, bf16[8,256,128]{2,1,0:T(8,128)(2,1)S(1)}, u32[]{:S(2)}, u32[]{:S(2)}) collective-permute-start(bf16[8,256,128]{2,1,0:T(8,128)(2,1)S(1)} %get-tuple-element.30), channel_id=1, source_target_pairs={{1,0},{0,1},{3,2},{2,3},{5,4},{4,5},{7,6},{6,7},{9,8},{8,9},{11,10... | collective-permute-start | bytes 1572872 | tf_op jit(solution)/shard_map/ppermute | solution.py:274
  85.4 4.6 %collective-permute-start.4 = (bf16[8,256,128]{2,1,0:T(8,128)(2,1)S(1)}, bf16[8,256,128]{2,1,0:T(8,128)(2,1)S(1)}, u32[]{:S(2)}, u32[]{:S(2)}) collective-permute-start(bf16[8,256,128]{2,1,0:T(8,128)(2,1)S(1)} %get-tuple-element.31), channel_id=1, source_target_pairs={{1,0},{0,1},{3,2},{2,3},{5,4},{4,5},{7,6},{6,7},{9,8},{8,9},{11,10... | collective-permute-start | bytes 1572872 | tf_op jit(solution)/shard_map/ppermute | solution.py:274
  89.9 17.4 %copy-start.10 = (s32[64]{0:T(128)S(1)}, s32[64]{0:T(128)}, u32[]{:S(2)}) copy-start(s32[64]{0:T(128)} %param.16) | copy-start | bytes 772
  89.9 35.6 %copy-start.8 = (f32[1,256]{1,0:T(1,128)S(1)}, f32[1,256]{1,0:T(1,128)}, u32[]{:S(2)}) copy-start(f32[1,256]{1,0:T(1,128)} %param.17) | copy-start | bytes 3076
  89.9 42.2 %copy-start.2 = (bf16[1,256,128]{2,1,0:T(8,128)(2,1)S(1)}, bf16[1,256,128]{2,1,0:T(8,128)(2,1)}, u32[]{:S(2)}) copy-start(bf16[1,256,128]{2,1,0:T(8,128)(2,1)} %param.21) | copy-start | bytes 196612
  89.9 42.5 %copy-start.3 = (bf16[1,256,128]{2,1,0:T(8,128)(2,1)S(1)}, bf16[1,256,128]{2,1,0:T(8,128)(2,1)}, u32[]{:S(2)}) copy-start(bf16[1,256,128]{2,1,0:T(8,128)(2,1)} %param.19) | copy-start | bytes 196612
  90.0 79.3 %copy-start.4 = (bf16[1,256,128]{2,1,0:T(8,128)(2,1)S(1)}, bf16[1,256,128]{2,1,0:T(8,128)(2,1)}, u32[]{:S(2)}) copy-start(bf16[1,256,128]{2,1,0:T(8,128)(2,1)} %param.18) | copy-start | bytes 196612
  90.0 79.3 %copy-start.5 = (bf16[1,256,128]{2,1,0:T(8,128)(2,1)S(1)}, bf16[1,256,128]{2,1,0:T(8,128)(2,1)}, u32[]{:S(2)}) copy-start(bf16[1,256,128]{2,1,0:T(8,128)(2,1)} %param.20) | copy-start | bytes 196612
  91.3 41.1 %all-to-all-start.1 = ((bf16[16,256,128]{2,1,0:T(8,128)(2,1)}), bf16[16,256,128]{2,1,0:T(8,128)(2,1)S(1)}, u32[]{:S(2)}, u32[]{:S(2)}) async-start(bf16[16,256,128]{2,1,0:T(8,128)(2,1)} %shard_map.143), calls=%async_computation.1 | async-start | bytes 2097152 | tf_op jit(solution)/shard_map/all_to_all | solution.py:368
  100.8 9.8 %collective-permute-start.5 = (bf16[4,256,128]{2,1,0:T(8,128)(2,1)S(1)}, bf16[4,256,128]{2,1,0:T(8,128)(2,1)S(1)}, u32[]{:S(2)}, u32[]{:S(2)}) collective-permute-start(bf16[4,256,128]{2,1,0:T(8,128)(2,1)S(1)} %get-tuple-element.33), channel_id=1, source_target_pairs={{704,0},{0,64},{64,128},{128,192},{192,256},{256,320},{320,384},{3... | collective-permute-start | bytes 786440 | tf_op jit(solution)/shard_map/ppermute | solution.py:274
  102.7 8.8 %collective-permute-start.6 = (bf16[4,256,128]{2,1,0:T(8,128)(2,1)S(1)}, bf16[4,256,128]{2,1,0:T(8,128)(2,1)S(1)}, u32[]{:S(2)}, u32[]{:S(2)}) collective-permute-start(bf16[4,256,128]{2,1,0:T(8,128)(2,1)S(1)} %get-tuple-element.34), channel_id=1, source_target_pairs={{64,0},{128,64},{192,128},{256,192},{320,256},{384,320},{448,384},... | collective-permute-start | bytes 786440 | tf_op jit(solution)/shard_map/ppermute | solution.py:274
  112.2 13.4 %collective-permute-start.7 = (bf16[256,128]{1,0:T(8,128)(2,1)S(1)}, bf16[256,128]{1,0:T(8,128)(2,1)S(1)}, u32[]{:S(2)}, u32[]{:S(2)}) collective-permute-start(bf16[256,128]{1,0:T(8,128)(2,1)S(1)} %get-tuple-element.36), channel_id=1, source_target_pairs={{576,0},{640,64},{704,128},{0,192},{64,256},{128,320},{192,384},{2... | collective-permute-start | bytes 196616 | tf_op jit(solution)/shard_map/ppermute | solution.py:274
  116.0 11.5 %collective-permute-start.8 = (bf16[256,128]{1,0:T(8,128)(2,1)S(1)}, bf16[256,128]{1,0:T(8,128)(2,1)S(1)}, u32[]{:S(2)}, u32[]{:S(2)}) collective-permute-start(bf16[256,128]{1,0:T(8,128)(2,1)S(1)} %get-tuple-element.37), channel_id=1, source_target_pairs={{384,0},{448,64},{512,128},{576,192},{640,256},{704,320},{0,384},{... | collective-permute-start | bytes 196616 | tf_op jit(solution)/shard_map/ppermute | solution.py:274
  122.1 10.0 %collective-permute-start.9 = (bf16[256,128]{1,0:T(8,128)(2,1)S(1)}, bf16[256,128]{1,0:T(8,128)(2,1)S(1)}, u32[]{:S(2)}, u32[]{:S(2)}) collective-permute-start(bf16[256,128]{1,0:T(8,128)(2,1)S(1)} %get-tuple-element.38), channel_id=1, source_target_pairs={{192,0},{256,64},{320,128},{384,192},{448,256},{512,320},{576,384}... | collective-permute-start | bytes 196616 | tf_op jit(solution)/shard_map/ppermute | solution.py:274

commit v4 on v3

--- a/solution.py
+++ b/solution.py
@@ -26,16 +26,19 @@
 MIB = 2**20
 
 
-def pick_columns(tile, straight, crossed):
-    block = tile.shape[1] // 2
-    lane = lax.broadcasted_iota(jnp.int32, tile.shape, 1)
-    left = lane < block
-    wide = tile.astype(jnp.float32)
-    turned = pltpu.roll(wide, block, 1)
-    as_is = jnp.where(left, straight[0], straight[1]) != 0
-    other = jnp.where(left, crossed[0], crossed[1]) != 0
-    picked = jnp.where(as_is, wide, jnp.where(other, turned, 0.0))
-    return picked.astype(jnp.bfloat16)
+def add_columns(acc_ref, index, whole, straight, crossed):
+    block = whole.shape[1] // 2
+    left = lax.broadcasted_iota(jnp.int32, (1, whole.shape[1]), 1) < block
+
+    @pl.when(straight[0] + straight[1] > 0)
+    def _():
+        keep = jnp.where(left, straight[0], straight[1]) != 0
+        acc_ref[index] += jnp.where(keep, whole, 0.0)
+
+    @pl.when(crossed[0] + crossed[1] > 0)
+    def _():
+        keep = jnp.where(left, crossed[0], crossed[1]) != 0
+        acc_ref[index] += jnp.where(keep, pltpu.roll(whole, block, 1), 0.0)
 
 
 def matches(cols_ref, source, target):
@@ -93,9 +96,8 @@
     def finish(a, local_row, local_col, straight, crossed):
         here, own_ref, other_ref, index = choose(local_row, local_col)
         take(a, own_ref, index).wait()
-        picked = pick_columns(tiles_ref[a], straight, crossed)
         hold(a).wait()
-        product(held_ref[a], picked, local_row, local_col)
+        product(held_ref[a], tiles_ref[a], local_row, local_col, straight, crossed)
 
     each(start)
     clear(acc_ref)
@@ -120,8 +122,9 @@
     def choose(local_row, local_col):
         return lax.rem(local_col, N_XH) == xh, own_ref, other_ref, local_col // N_XH
 
-    def product(block, picked, local_row, local_col):
-        acc_ref[local_row] += jnp.dot(block, picked, preferred_element_type=jnp.float32)
+    def product(block, tile, local_row, local_col, straight, crossed):
+        whole = jnp.dot(block, tile, preferred_element_type=jnp.float32)
+        add_columns(acc_ref, local_row, whole, straight, crossed)
 
     each_match(where_ref, place_ref, cols_ref, a_ref, False, choose, scratch, product)
 
@@ -146,33 +149,35 @@
     own_ref,
     other_ref,
     a_ref,
-    mine_ref,
-    theirs_ref,
+    own_third_ref,
+    up_third_ref,
+    down_third_ref,
     after_ref,
     *scratch,
 ):
     for i in range(where_ref.shape[0]):
         after_ref[i] = where_ref[i]
-    xh, core, z = where_ref[1], where_ref[2], where_ref[5]
+    core, z = where_ref[2], where_ref[5]
     acc_ref = scratch[0]
 
     def choose(local_row, local_col):
         return lax.rem(local_row, N_CORE) == core, own_ref, other_ref, local_row // N_CORE
 
-    def product(block, picked, local_row, local_col):
-        acc_ref[local_col] += lax.dot_general(
-            block, picked, (((0,), (0,)), ((), ())), preferred_element_type=jnp.float32
+    def product(block, tile, local_row, local_col, straight, crossed):
+        whole = lax.dot_general(
+            block, tile, (((0,), (0,)), ((), ())), preferred_element_type=jnp.float32
         )
+        add_columns(acc_ref, local_col, whole, straight, crossed)
 
     each_match(where_ref, place_ref, cols_ref, a_ref, True, choose, scratch, product)
 
     def store(q, carry):
-        owner = 3 * lax.rem(q, 4) + lax.rem(z + q // 4, 3)
-        mine_ref[q] = acc_ref[2 * owner + xh].astype(jnp.bfloat16)
-        theirs_ref[q] = acc_ref[2 * owner + 1 - xh].astype(jnp.bfloat16)
+        for third, ref in enumerate((own_third_ref, up_third_ref, down_third_ref)):
+            owner = 3 * (q // N_XH) + lax.rem(z + third, 3)
+            ref[q] = acc_ref[N_XH * owner + lax.rem(q, N_XH)].astype(jnp.bfloat16)
         return carry
 
-    lax.fori_loop(0, N_Z, store, 0)
+    lax.fori_loop(0, N_ROW // 3, store, 0)
 
 
 def wide_sum(refs, index):
@@ -194,19 +199,19 @@
     lax.fori_loop(0, half, body, 0)
 
 
-def thirds_kernel(mine_ref, near_ref, own_ref, up_ref, down_ref):
-    def body(i, carry):
-        for third, ref in enumerate((own_ref, up_ref, down_ref)):
-            ref[i] = wide_sum((mine_ref, near_ref), 4 * third + i)
-        return carry
-
-    lax.fori_loop(0, 4, body, 0)
-
-
 def quarters_kernel(where_ref, own_ref, up_ref, down_ref, *quarter_refs):
     quarter = where_ref[5] // 3
     for i, ref in enumerate(quarter_refs):
-        ref[...] = wide_sum((own_ref, up_ref, down_ref), lax.rem(quarter + i, 4))
+        for x in range(N_XH):
+            index = N_XH * lax.rem(quarter + i, 4) + x
+            ref[x] = wide_sum((own_ref, up_ref, down_ref), index)
+
+
+def halves_kernel(where_ref, *refs):
+    quarter_refs, (mine_ref, theirs_ref) = refs[:-2], refs[-2:]
+    xh = where_ref[1]
+    mine_ref[...] = wide_sum(quarter_refs, xh)
+    theirs_ref[...] = wide_sum(quarter_refs, 1 - xh)
 
 
 def update_kernel(mass_ref, resid_ref, projector_ref, *refs):
@@ -271,6 +276,8 @@
 
 def turned(array, axis, by):
     size = lax.axis_size(axis)
+    if by % size == 0:
+        return array
     return lax.ppermute(array, axis, [((i + by) % size, i) for i in range(size)])
 
 
@@ -330,9 +337,9 @@
     r_own = after(r_own, p_own)
     r_other = turned(r_own, "core", 1)
 
-    r_mine, r_theirs, where_then = on_device(
+    *r_thirds, where_then = on_device(
         restrict_kernel,
-        (shape((N_Z, height, width)),) * 2 + (shape(where.shape, jnp.int32),),
+        (shape((N_ROW // 3, height, width)),) * 3 + (shape(where.shape, jnp.int32),),
         (where, place, r_flat),
         left=(r_own, r_other, tile_vals),
         scratch=[pltpu.VMEM((N_ROW, height, width), jnp.float32), *scratch],
@@ -340,7 +347,7 @@
         mib=48,
         scalars_out=1,
     )
-    r_near = turned(r_theirs, "xh", 1)
+    r_thirds = (r_thirds[0], turned(r_thirds[1], "z", -1), turned(r_thirds[2], "z", 1))
     p_mine, p_low, p_high = on_device(
         prolong_kernel,
         (shape((HALF_COL, height, width)),) + (shape((HALF_COL // 2, height, width)),) * 2,
@@ -352,18 +359,13 @@
     )
     p_near = (turned(p_low, "core", 1), turned(p_high, "core", 1))
 
-    r_thirds = on_device(thirds_kernel, (shape((4, height, width)),) * 3, (), r_mine, r_near)
     r_quarters = on_device(
-        quarters_kernel,
-        (tile,) * 4,
-        (where,),
-        r_thirds[0],
-        turned(r_thirds[1], "z", -1),
-        turned(r_thirds[2], "z", 1),
-    )
-    r_parts = [r_quarters[0]]
-    r_parts += [turned(r_quarters[i], "z", -3 * i) for i in (1, 2, 3)]
-    p_mine = after(p_mine, r_thirds[0])
+        quarters_kernel, (shape((N_XH, height, width)),) * 4, (where,), *r_thirds
+    )
+    r_quarters = [turned(quarter, "z", -3 * i) for i, quarter in enumerate(r_quarters)]
+    r_mine, r_theirs = on_device(halves_kernel, (tile,) * 2, (where,), *r_quarters)
+    r_parts = (r_mine, turned(r_theirs, "xh", 1))
+    p_mine = after(p_mine, r_quarters[0])
     (p_sum,) = on_device(pair_kernel, (shape((HALF_COL, height, width)),), (), p_mine, *p_near)
     p_parts = [lax.all_to_all(p_sum, ("y", "xl"), 0, 0, tiled=True)]
 

time: 171 us -> 170 us (level)
  blocking collectives: 68.8 us -> 71.5 us
    all_to_all x2, blocking collectives: 35.8 us -> 38.5 us  [gather(): return lax.all_to_all(copies, axes, 0, 0, tiled=True)]
  transfers between devices with their start and end apart: 12 -> 12, of which waited for: 6 -> 4; matrix products, arithmetic and copies ran while one was open for 1% -> 1% of each run, Pallas kernels for 6% -> 6%
where the time goes in v4:
time: 170 us
  blocking collectives  71.5 us (42%)
  starting transfers between devices  62.4 us (37%)
  waiting for transfers between devices  17.9 us (11%)
  Pallas kernels  12.7 us (7%)
  local copies, waits for them, and re-layouts  3.34 us (2%)
    ppermute x10, starting transfers between devices, turned(): lax.ppermute(array, axis, [((i + by) % size, i) for i in range(size)])  45.3 us
    all_to_all x2, blocking collectives, gather(): return lax.all_to_all(copies, axes, 0, 0, tiled=True)  38.5 us
    all_gather x1, blocking collectives, shards(): p_own = lax.all_gather(res_p, 'z', axis=0, tiled=True)  33 us
    ppermute x10, waiting for transfers between devices, turned(): lax.ppermute(array, axis, [((i + by) % size, i) for i in range(size)])  17.9 us
    pallas_call x8, Pallas kernels, on_device(): pl.pallas_call(kernel, out_shape=out_shape, in_specs=[SMEM] * len(scalars...  12.7 us
    all_to_all x1, starting transfers between devices, gather(): return lax.all_to_all(copies, axes, 0, 0, tiled=True)  8.68 us
    all_to_all x1, starting transfers between devices, shards(): p_parts = [lax.all_to_all(p_sum, ('y', 'xl'), 0, 0, tiled=True)]  8.44 us
  transfers between devices with their start and end apart: 12, of which 4 were waited for; matrix products, arithmetic and copies ran while one was open for 1% of the time, Pallas kernels for 6%

profile of v4, /device:TPU:1, one launch (start us, length us, event | category | flops | bytes accessed | tf_op | source)
XLA Modules:
  0.0 169.7 jit_solution(13550462634737692463)
XLA Ops:
  0.6 0.0 copy-start.7
  0.6 0.0 copy-start.4
  0.7 0.0 copy-start.5
  0.7 2.0 %broadcast_in_dim.36 = bf16[16,256,128]{2,1,0:T(8,128)(2,1)} broadcast(bf16[256,128]{1,0:T(8,128)(2,1)} %bitcast.21), dimensions={1,2} | broadcast | bytes 1114112 | tf_op jit(solution)/shard_map/broadcast_in_dim | solution.py:285
  2.7 8.7 %all-to-all-start = ((bf16[16,256,128]{2,1,0:T(8,128)(2,1)}), bf16[16,256,128]{2,1,0:T(8,128)(2,1)S(1)}, u32[]{:S(2)}, u32[]{:S(2)}) async-start(bf16[16,256,128]{2,1,0:T(8,128)(2,1)} %broadcast_in_dim.36), calls=%async_computation | async-start | bytes 2097152 | tf_op jit(solution)/shard_map/all_to_all | solution.py:286
  11.4 33.0 %all_gather.3.refs_1_.own_ref = bf16[12,256,128]{2,1,0:T(8,128)(2,1)S(1)} all-gather(bf16[1,256,128]{2,1,0:T(8,128)(2,1)} %param.19), channel_id=1, replica_groups=mesh['z'=12,'xh'=2,'y'=8,'xl'=2,'core'=2] {'z'}, dimensions={0}, use_global_device_ids=true | all-gather | bytes 851968 | tf_op jit(solution)/shard_map/all_gather | solution.py:335
  44.4 0.0 all-to-all-done.refs_0_
  44.4 7.4 %collective-permute-start = (bf16[16,256,128]{2,1,0:T(8,128)(2,1)S(1)}, bf16[16,256,128]{2,1,0:T(8,128)(2,1)S(1)}, u32[]{:S(2)}, u32[]{:S(2)}) collective-permute-start(bf16[16,256,128]{2,1,0:T(8,128)(2,1)S(1)} %shard_map.138.own_ref), channel_id=1, source_target_pairs={{1,0},{0,1},{3,2},{2,3},{5,4},{4,5},{7,6},{6,7},{9,8},{8,9},{11,10... | collective-permute-start | bytes 3145736 | tf_op jit(solution)/shard_map/ppermute | solution.py:281
  51.8 4.4 %collective-permute-start.1 = (bf16[12,256,128]{2,1,0:T(8,128)(2,1)S(1)}, bf16[12,256,128]{2,1,0:T(8,128)(2,1)}, u32[]{:S(2)}, u32[]{:S(2)}) collective-permute-start(bf16[12,256,128]{2,1,0:T(8,128)(2,1)S(1)} %all_gather.3.refs_1_.own_ref), channel_id=1, source_target_pairs={{32,0},{0,32},{33,1},{1,33},{34,2},{2,34},{35,3},{3,35},{36,4},{4,... | collective-permute-start | bytes 2359304 | tf_op jit(solution)/shard_map/ppermute | solution.py:281
  56.8 0.0 copy-done.7
  56.9 0.1 reshape_squeeze.3.place_ref
  56.9 0.0 copy-done.4
  56.9 0.2 copy.29
  57.1 0.2 reshape.24.cols_ref
  57.4 0.0 copy-done.5
  57.4 0.2 copy.30
  57.6 0.2 reshape.25.cols_ref
  57.8 0.1 stack.23.where_ref
  57.9 0.0 collective-permute-done.other_ref
  57.9 4.2 %shard_map.139 = (bf16[8,256,128]{2,1,0:T(8,128)(2,1)S(1)}, bf16[8,256,128]{2,1,0:T(8,128)(2,1)S(1)}, bf16[8,256,128]{2,1,0:T(8,128)(2,1)S(1)}, s32[6]{0:T(128)S(1)}) custom-call(s32[6]{0:T(128)S(1)} %stack.23.where_ref, s32[64]{0:T(128)S(1)} %reshape_squeeze.3.place_ref, s32[1536]{0:T(1024)S(1)} %reshape.24.cols_ref, ...), custom_call_target="tpu_custom_call" | custom-call | flops 536870912 | bytes 12582912 | tf_op jit(solution)/shard_map/pallas_call | solution.py:243
  62.1 7.0 %collective-permute-start.2 = (bf16[8,256,128]{2,1,0:T(8,128)(2,1)S(1)}, bf16[8,256,128]{2,1,0:T(8,128)(2,1)S(1)}, u32[]{:S(2)}, u32[]{:S(2)}) collective-permute-start(bf16[8,256,128]{2,1,0:T(8,128)(2,1)S(1)} %get-tuple-element.28), channel_id=1, source_target_pairs={{704,0},{0,64},{64,128},{128,192},{192,256},{256,320},{320,384},{3... | collective-permute-start | bytes 1572872 | tf_op jit(solution)/shard_map/ppermute | solution.py:281
  69.1 8.7 %collective-permute-start.3 = (bf16[8,256,128]{2,1,0:T(8,128)(2,1)S(1)}, bf16[8,256,128]{2,1,0:T(8,128)(2,1)S(1)}, u32[]{:S(2)}, u32[]{:S(2)}) collective-permute-start(bf16[8,256,128]{2,1,0:T(8,128)(2,1)S(1)} %get-tuple-element.29), channel_id=1, source_target_pairs={{64,0},{128,64},{192,128},{256,192},{320,256},{384,320},{448,384},... | collective-permute-start | bytes 1572872 | tf_op jit(solution)/shard_map/ppermute | solution.py:281
  77.8 0.0 collective-permute-done.1.other_ref
  77.8 3.9 %shard_map.140 = (bf16[16,256,128]{2,1,0:T(8,128)(2,1)S(1)}, bf16[8,256,128]{2,1,0:T(8,128)(2,1)S(1)}, bf16[8,256,128]{2,1,0:T(8,128)(2,1)S(1)}) custom-call(s32[6]{0:T(128)S(1)} %get-tuple-element.25.where_ref, s32[64]{0:T(128)S(1)} %reshape_squeeze.3.place_ref, s32[1536]{0:T(1024)S(1)} %reshape.25.cols_ref, ...), custom_call_target="tpu_custom_call" | custom-call | flops 536870912 | bytes 12582912 | tf_op jit(solution)/shard_map/pallas_call | solution.py:243
  81.7 3.2 %collective-permute-start.4 = (bf16[8,256,128]{2,1,0:T(8,128)(2,1)S(1)}, bf16[8,256,128]{2,1,0:T(8,128)(2,1)S(1)}, u32[]{:S(2)}, u32[]{:S(2)}) collective-permute-start(bf16[8,256,128]{2,1,0:T(8,128)(2,1)S(1)} %get-tuple-element.31), channel_id=1, source_target_pairs={{1,0},{0,1},{3,2},{2,3},{5,4},{4,5},{7,6},{6,7},{9,8},{8,9},{11,10... | collective-permute-start | bytes 1572872 | tf_op jit(solution)/shard_map/ppermute | solution.py:281
  84.9 1.9 %collective-permute-start.5 = (bf16[8,256,128]{2,1,0:T(8,128)(2,1)S(1)}, bf16[8,256,128]{2,1,0:T(8,128)(2,1)S(1)}, u32[]{:S(2)}, u32[]{:S(2)}) collective-permute-start(bf16[8,256,128]{2,1,0:T(8,128)(2,1)S(1)} %get-tuple-element.32), channel_id=1, source_target_pairs={{1,0},{0,1},{3,2},{2,3},{5,4},{4,5},{7,6},{6,7},{9,8},{8,9},{11,10... | collective-permute-start | bytes 1572872 | tf_op jit(solution)/shard_map/ppermute | solution.py:281
  86.8 0.0 collective-permute-done.2.up_ref
  86.8 0.7 collective-permute-done.3.down_ref
  87.5 0.0 copy-start.8
  87.5 0.7 shard_map.141
  88.3 0.0 copy-start.6
  88.3 0.0 copy-start
  88.3 0.0 copy-start.1
  88.3 0.0 copy-start.2
  88.4 0.0 copy-start.3
  88.4 0.0 collective-permute-done.4.near_low_ref
  88.4 0.3 collective-permute-done.5.near_high_ref
  88.7 1.3 shard_map.143
  90.0 8.4 %all-to-all-start.1 = ((bf16[16,256,128]{2,1,0:T(8,128)(2,1)}), bf16[16,256,128]{2,1,0:T(8,128)(2,1)S(1)}, u32[]{:S(2)}, u32[]{:S(2)}) async-start(bf16[16,256,128]{2,1,0:T(8,128)(2,1)} %shard_map.143), calls=%async_computation.1 | async-start | bytes 2097152 | tf_op jit(solution)/shard_map/all_to_all | solution.py:370
  98.4 1.9 %collective-permute-start.6 = (bf16[2,256,128]{2,1,0:T(8,128)(2,1)S(1)}, bf16[2,256,128]{2,1,0:T(8,128)(2,1)S(1)}, u32[]{:S(2)}, u32[]{:S(2)}) collective-permute-start(bf16[2,256,128]{2,1,0:T(8,128)(2,1)S(1)} %get-tuple-element.34), channel_id=1, source_target_pairs={{576,0},{640,64},{704,128},{0,192},{64,256},{128,320},{192,384},{2... | collective-permute-start | bytes 393224 | tf_op jit(solution)/shard_map/ppermute | solution.py:281
  100.3 4.7 %collective-permute-start.7 = (bf16[2,256,128]{2,1,0:T(8,128)(2,1)S(1)}, bf16[2,256,128]{2,1,0:T(8,128)(2,1)S(1)}, u32[]{:S(2)}, u32[]{:S(2)}) collective-permute-start(bf16[2,256,128]{2,1,0:T(8,128)(2,1)S(1)} %get-tuple-element.35), channel_id=1, source_target_pairs={{384,0},{448,64},{512,128},{576,192},{640,256},{704,320},{0,384},{... | collective-permute-start | bytes 393224 | tf_op jit(solution)/shard_map/ppermute | solution.py:281
  105.0 3.6 %collective-permute-start.8 = (bf16[2,256,128]{2,1,0:T(8,128)(2,1)S(1)}, bf16[2,256,128]{2,1,0:T(8,128)(2,1)S(1)}, u32[]{:S(2)}, u32[]{:S(2)}) collective-permute-start(bf16[2,256,128]{2,1,0:T(8,128)(2,1)S(1)} %get-tuple-element.36), channel_id=1, source_target_pairs={{192,0},{256,64},{320,128},{384,192},{448,256},{512,320},{576,384}... | collective-permute-start | bytes 393224 | tf_op jit(solution)/shard_map/ppermute | solution.py:281
  108.6 0.0 copy-done.8
  108.7 0.1 eq.17
  108.8 13.1 %collective-permute-done.6.refs_1_ = bf16[2,256,128]{2,1,0:T(8,128)(2,1)S(1)} collective-permute-done((bf16[2,256,128]{2,1,0:T(8,128)(2,1)S(1)}, bf16[2,256,128]{2,1,0:T(8,128)(2,1)S(1)}, u32[]{:S(2)}, u32[]{:S(2)}) %collective-permute-start.6) | collective-permute-done | bytes 131104 | tf_op jit(solution)/shard_map/ppermute | solution.py:281
  121.8 0.0 collective-permute-done.7.refs_2_
  121.8 0.0 collective-permute-done.8.refs_3_
  121.8 0.6 shard_map.145
  122.5 2.5 %collective-permute-start.9 = (bf16[256,128]{1,0:T(8,128)(2,1)S(1)}, bf16[256,128]{1,0:T(8,128)(2,1)S(1)}, u32[]{:S(2)}, u32[]{:S(2)}) collective-permute-start(bf16[256,128]{1,0:T(8,128)(2,1)S(1)} %get-tuple-element.38), channel_id=1, source_target_pairs={{32,0},{0,32},{33,1},{1,33},{34,2},{2,34},{35,3},{3,35},{36,4},{4,... | collective-permute-start | bytes 196616 | tf_op jit(solution)/shard_map/ppermute | solution.py:281
  124.9 0.1 compare_select_fusion.projector_ref
  125.0 0.0 copy-done.6
  125.0 0.1 copy.31.mass_ref
  125.2 3.8 %collective-permute-done.9.refs_1_ = bf16[256,128]{1,0:T(8,128)(2,1)S(1)} collective-permute-done((bf16[256,128]{1,0:T(8,128)(2,1)S(1)}, bf16[256,128]{1,0:T(8,128)(2,1)S(1)}, u32[]{:S(2)}, u32[]{:S(2)}) %collective-permute-start.9) | collective-permute-done | bytes 65568 | tf_op jit(solution)/shard_map/ppermute | solution.py:281
  129.0 0.0 copy-done
  129.0 0.3 shard_map.146
  129.3 0.0 all-to-all-done.1.refs_0_
  129.3 0.0 copy-done.1
  129.3 0.7 shard_map.144
  130.1 0.1 maximum_reduce_fusion
  130.2 15.4 %all_to_all.20 = f32[8,1,128]{2,1,0:T(1,128)S(1)} all-to-all(f32[8,1,128]{2,1,0:T(1,128)S(1)} %broadcast_in_dim.39), channel_id=1, replica_groups=mesh['z'=12,'xh'=2,'y'=8,'xl'=2,'core'=2] {'xh','xl','core'}, dimensions={0} | all-to-all | bytes 8192 | tf_op jit(solution)/shard_map/all_to_all | solution.py:286
  145.7 23.1 %all_to_all.21.sums_ref = f32[96,1,128]{2,1,0:T(1,128)S(1)} all-to-all(f32[96,1,128]{2,1,0:T(1,128)S(1)} %broadcast_in_dim.40), channel_id=1, replica_groups=mesh['z'=12,'xh'=2,'y'=8,'xl'=2,'core'=2] {'z','y'}, dimensions={0} | all-to-all | bytes 98304 | tf_op jit(solution)/shard_map/all_to_all | solution.py:286
  168.8 0.0 copy-done.2
  168.8 0.0 copy-done.3
  168.8 1.0 shard_map.147
  (8 shorter events, 0.1 us)
Async XLA Ops:
  0.6 56.2 %copy-start.7 = (s32[1,1,2,32]{3,2,1,0:T(2,128)S(1)}, s32[1,1,2,32]{3,2,1,0:T(2,128)}, u32[]{:S(2)}) copy-start(s32[1,1,2,32]{3,2,1,0:T(2,128)} %param.12) | copy-start | bytes 772
  0.6 56.3 %copy-start.4 = (s32[768,2]{0,1:T(2,128)S(1)}, s32[768,2]{0,1:T(2,128)}, u32[]{:S(2)}) copy-start(s32[768,2]{0,1:T(2,128)} %param.15) | copy-start | bytes 18436
  0.7 56.7 %copy-start.5 = (s32[768,2]{0,1:T(2,128)S(1)}, s32[768,2]{0,1:T(2,128)}, u32[]{:S(2)}) copy-start(s32[768,2]{0,1:T(2,128)} %param.14) | copy-start | bytes 18436
  2.7 41.7 %all-to-all-start = ((bf16[16,256,128]{2,1,0:T(8,128)(2,1)}), bf16[16,256,128]{2,1,0:T(8,128)(2,1)S(1)}, u32[]{:S(2)}, u32[]{:S(2)}) async-start(bf16[16,256,128]{2,1,0:T(8,128)(2,1)} %broadcast_in_dim.36), calls=%async_computation | async-start | bytes 2097152 | tf_op jit(solution)/shard_map/all_to_all | solution.py:286
  44.4 13.5 %collective-permute-start = (bf16[16,256,128]{2,1,0:T(8,128)(2,1)S(1)}, bf16[16,256,128]{2,1,0:T(8,128)(2,1)S(1)}, u32[]{:S(2)}, u32[]{:S(2)}) collective-permute-start(bf16[16,256,128]{2,1,0:T(8,128)(2,1)S(1)} %shard_map.138.own_ref), channel_id=1, source_target_pairs={{1,0},{0,1},{3,2},{2,3},{5,4},{4,5},{7,6},{6,7},{9,8},{8,9},{11,10... | collective-permute-start | bytes 3145736 | tf_op jit(solution)/shard_map/ppermute | solution.py:281
  51.8 26.0 %collective-permute-start.1 = (bf16[12,256,128]{2,1,0:T(8,128)(2,1)S(1)}, bf16[12,256,128]{2,1,0:T(8,128)(2,1)}, u32[]{:S(2)}, u32[]{:S(2)}) collective-permute-start(bf16[12,256,128]{2,1,0:T(8,128)(2,1)S(1)} %all_gather.3.refs_1_.own_ref), channel_id=1, source_target_pairs={{32,0},{0,32},{33,1},{1,33},{34,2},{2,34},{35,3},{3,35},{36,4},{4,... | collective-permute-start | bytes 2359304 | tf_op jit(solution)/shard_map/ppermute | solution.py:281
  62.1 24.7 %collective-permute-start.2 = (bf16[8,256,128]{2,1,0:T(8,128)(2,1)S(1)}, bf16[8,256,128]{2,1,0:T(8,128)(2,1)S(1)}, u32[]{:S(2)}, u32[]{:S(2)}) collective-permute-start(bf16[8,256,128]{2,1,0:T(8,128)(2,1)S(1)} %get-tuple-element.28), channel_id=1, source_target_pairs={{704,0},{0,64},{64,128},{128,192},{192,256},{256,320},{320,384},{3... | collective-permute-start | bytes 1572872 | tf_op jit(solution)/shard_map/ppermute | solution.py:281
  69.1 18.5 %collective-permute-start.3 = (bf16[8,256,128]{2,1,0:T(8,128)(2,1)S(1)}, bf16[8,256,128]{2,1,0:T(8,128)(2,1)S(1)}, u32[]{:S(2)}, u32[]{:S(2)}) collective-permute-start(bf16[8,256,128]{2,1,0:T(8,128)(2,1)S(1)} %get-tuple-element.29), channel_id=1, source_target_pairs={{64,0},{128,64},{192,128},{256,192},{320,256},{384,320},{448,384},... | collective-permute-start | bytes 1572872 | tf_op jit(solution)/shard_map/ppermute | solution.py:281
  81.7 6.7 %collective-permute-start.4 = (bf16[8,256,128]{2,1,0:T(8,128)(2,1)S(1)}, bf16[8,256,128]{2,1,0:T(8,128)(2,1)S(1)}, u32[]{:S(2)}, u32[]{:S(2)}) collective-permute-start(bf16[8,256,128]{2,1,0:T(8,128)(2,1)S(1)} %get-tuple-element.31), channel_id=1, source_target_pairs={{1,0},{0,1},{3,2},{2,3},{5,4},{4,5},{7,6},{6,7},{9,8},{8,9},{11,10... | collective-permute-start | bytes 1572872 | tf_op jit(solution)/shard_map/ppermute | solution.py:281
  84.9 3.8 %collective-permute-start.5 = (bf16[8,256,128]{2,1,0:T(8,128)(2,1)S(1)}, bf16[8,256,128]{2,1,0:T(8,128)(2,1)S(1)}, u32[]{:S(2)}, u32[]{:S(2)}) collective-permute-start(bf16[8,256,128]{2,1,0:T(8,128)(2,1)S(1)} %get-tuple-element.32), channel_id=1, source_target_pairs={{1,0},{0,1},{3,2},{2,3},{5,4},{4,5},{7,6},{6,7},{9,8},{8,9},{11,10... | collective-permute-start | bytes 1572872 | tf_op jit(solution)/shard_map/ppermute | solution.py:281
  87.5 21.1 %copy-start.8 = (s32[64]{0:T(128)S(1)}, s32[64]{0:T(128)}, u32[]{:S(2)}) copy-start(s32[64]{0:T(128)} %param.16) | copy-start | bytes 772
  88.3 36.7 %copy-start.6 = (f32[1,256]{1,0:T(1,128)S(1)}, f32[1,256]{1,0:T(1,128)}, u32[]{:S(2)}) copy-start(f32[1,256]{1,0:T(1,128)} %param.17) | copy-start | bytes 3076
  88.3 40.7 %copy-start = (bf16[1,256,128]{2,1,0:T(8,128)(2,1)S(1)}, bf16[1,256,128]{2,1,0:T(8,128)(2,1)}, u32[]{:S(2)}) copy-start(bf16[1,256,128]{2,1,0:T(8,128)(2,1)} %param.21) | copy-start | bytes 196612
  88.3 41.0 %copy-start.1 = (bf16[1,256,128]{2,1,0:T(8,128)(2,1)S(1)}, bf16[1,256,128]{2,1,0:T(8,128)(2,1)}, u32[]{:S(2)}) copy-start(bf16[1,256,128]{2,1,0:T(8,128)(2,1)} %param.19) | copy-start | bytes 196612
  88.3 80.4 %copy-start.2 = (bf16[1,256,128]{2,1,0:T(8,128)(2,1)S(1)}, bf16[1,256,128]{2,1,0:T(8,128)(2,1)}, u32[]{:S(2)}) copy-start(bf16[1,256,128]{2,1,0:T(8,128)(2,1)} %param.18) | copy-start | bytes 196612
  88.4 80.4 %copy-start.3 = (bf16[1,256,128]{2,1,0:T(8,128)(2,1)S(1)}, bf16[1,256,128]{2,1,0:T(8,128)(2,1)}, u32[]{:S(2)}) copy-start(bf16[1,256,128]{2,1,0:T(8,128)(2,1)} %param.20) | copy-start | bytes 196612
  90.0 39.3 %all-to-all-start.1 = ((bf16[16,256,128]{2,1,0:T(8,128)(2,1)}), bf16[16,256,128]{2,1,0:T(8,128)(2,1)S(1)}, u32[]{:S(2)}, u32[]{:S(2)}) async-start(bf16[16,256,128]{2,1,0:T(8,128)(2,1)} %shard_map.143), calls=%async_computation.1 | async-start | bytes 2097152 | tf_op jit(solution)/shard_map/all_to_all | solution.py:370
  98.4 23.4 %collective-permute-start.6 = (bf16[2,256,128]{2,1,0:T(8,128)(2,1)S(1)}, bf16[2,256,128]{2,1,0:T(8,128)(2,1)S(1)}, u32[]{:S(2)}, u32[]{:S(2)}) collective-permute-start(bf16[2,256,128]{2,1,0:T(8,128)(2,1)S(1)} %get-tuple-element.34), channel_id=1, source_target_pairs={{576,0},{640,64},{704,128},{0,192},{64,256},{128,320},{192,384},{2... | collective-permute-start | bytes 393224 | tf_op jit(solution)/shard_map/ppermute | solution.py:281
  100.3 21.5 %collective-permute-start.7 = (bf16[2,256,128]{2,1,0:T(8,128)(2,1)S(1)}, bf16[2,256,128]{2,1,0:T(8,128)(2,1)S(1)}, u32[]{:S(2)}, u32[]{:S(2)}) collective-permute-start(bf16[2,256,128]{2,1,0:T(8,128)(2,1)S(1)} %get-tuple-element.35), channel_id=1, source_target_pairs={{384,0},{448,64},{512,128},{576,192},{640,256},{704,320},{0,384},{... | collective-permute-start | bytes 393224 | tf_op jit(solution)/shard_map/ppermute | solution.py:281
  105.0 16.8 %collective-permute-start.8 = (bf16[2,256,128]{2,1,0:T(8,128)(2,1)S(1)}, bf16[2,256,128]{2,1,0:T(8,128)(2,1)S(1)}, u32[]{:S(2)}, u32[]{:S(2)}) collective-permute-start(bf16[2,256,128]{2,1,0:T(8,128)(2,1)S(1)} %get-tuple-element.36), channel_id=1, source_target_pairs={{192,0},{256,64},{320,128},{384,192},{448,256},{512,320},{576,384}... | collective-permute-start | bytes 393224 | tf_op jit(solution)/shard_map/ppermute | solution.py:281
  122.5 6.5 %collective-permute-start.9 = (bf16[256,128]{1,0:T(8,128)(2,1)S(1)}, bf16[256,128]{1,0:T(8,128)(2,1)S(1)}, u32[]{:S(2)}, u32[]{:S(2)}) collective-permute-start(bf16[256,128]{1,0:T(8,128)(2,1)S(1)} %get-tuple-element.38), channel_id=1, source_target_pairs={{32,0},{0,32},{33,1},{1,33},{34,2},{2,34},{35,3},{3,35},{36,4},{4,... | collective-permute-start | bytes 196616 | tf_op jit(solution)/shard_map/ppermute | solution.py:281

commit v5 on v4

--- a/solution.py
+++ b/solution.py
@@ -26,26 +26,39 @@
 MIB = 2**20
 
 
-def add_columns(acc_ref, index, whole, straight, crossed):
-    block = whole.shape[1] // 2
-    left = lax.broadcasted_iota(jnp.int32, (1, whole.shape[1]), 1) < block
-
-    @pl.when(straight[0] + straight[1] > 0)
-    def _():
-        keep = jnp.where(left, straight[0], straight[1]) != 0
-        acc_ref[index] += jnp.where(keep, whole, 0.0)
-
-    @pl.when(crossed[0] + crossed[1] > 0)
-    def _():
-        keep = jnp.where(left, crossed[0], crossed[1]) != 0
-        acc_ref[index] += jnp.where(keep, pltpu.roll(whole, block, 1), 0.0)
-
-
 def matches(cols_ref, source, target):
     s0, s1 = cols_ref[2 * source], cols_ref[2 * source + 1]
     t0, t1 = cols_ref[2 * target], cols_ref[2 * target + 1]
-    flag = lambda same: same.astype(jnp.int32)
-    return (flag(s0 == t0), flag(s1 == t1)), (flag(s1 == t0), flag(s0 == t1))
+    flag = lambda same, bit: jnp.where(same, bit, 0)
+    return flag(s0 == t0, 1) + flag(s1 == t1, 2) + flag(s1 == t0, 4) + flag(s0 == t1, 8)
+
+
+def plan_kernel(where_ref, place_ref, p_cols_ref, r_cols_ref, p_plan_ref, r_plan_ref):
+    count, xh, core = where_ref[0], where_ref[1], where_ref[2]
+    row_id, col_id = where_ref[3], where_ref[4]
+    slots = place_ref.shape[0] // 2
+
+    def note(plan_ref, used, slot, target, index, blocks):
+        for field, value in enumerate((slot, target, index, blocks)):
+            plan_ref[field * slots + used] = value
+        return used + jnp.where(blocks != 0, 1, 0)
+
+    def body(a, used):
+        local_row, local_col = place_ref[a], place_ref[slots + a]
+        tile_row = row_id * N_COL + local_row
+        tile_col = local_col * N_COL + col_id
+        p_index = local_col // N_XH + jnp.where(lax.rem(local_col, N_XH) == xh, 0, N_Z)
+        r_index = local_row // N_CORE + jnp.where(lax.rem(local_row, N_CORE) == core, 0, HALF_COL)
+        p_blocks = matches(p_cols_ref, tile_col, tile_row)
+        r_blocks = matches(r_cols_ref, tile_row, tile_col)
+        return (
+            note(p_plan_ref, used[0], a, local_row, p_index, p_blocks),
+            note(r_plan_ref, used[1], a, local_col, r_index, r_blocks),
+        )
+
+    p_used, r_used = lax.fori_loop(0, count, body, (0, 0))
+    p_plan_ref[4 * slots] = p_used
+    r_plan_ref[4 * slots] = r_used
 
 
 def clear(acc_ref):
@@ -56,58 +69,61 @@
     lax.fori_loop(0, acc_ref.shape[0], body, 0)
 
 
-def each_match(where_ref, place_ref, cols_ref, a_ref, turn, choose, scratch, product):
+def add_columns(acc_ref, index, whole, blocks):
+    block = whole.shape[1] // 2
+    left = lax.broadcasted_iota(jnp.int32, (1, whole.shape[1]), 1) < block
+
+    @pl.when((blocks & 3) != 0)
+    def _():
+        keep = jnp.where(left, blocks & 1, blocks & 2) != 0
+        acc_ref[index] += jnp.where(keep, whole, 0.0)
+
+    @pl.when((blocks & 12) != 0)
+    def _():
+        keep = jnp.where(left, blocks & 4, blocks & 8) != 0
+        acc_ref[index] += jnp.where(keep, pltpu.roll(whole, block, 1), 0.0)
+
+
+def each_used(plan_ref, own_ref, other_ref, a_ref, scratch, product):
     acc_ref, held_ref, tiles_ref, held_sems, tile_sems = scratch
-    count, row_id, col_id = where_ref[0], where_ref[3], where_ref[4]
-    slots = a_ref.shape[0]
-    hold = lambda a: pltpu.make_async_copy(a_ref.at[a], held_ref.at[a], held_sems.at[a])
-    take = lambda a, ref, index: pltpu.make_async_copy(
-        ref.at[index], tiles_ref.at[a], tile_sems.at[a]
-    )
-
-    def each(act):
-        def body(a, carry):
-            local_row, local_col = place_ref[a], place_ref[slots + a]
-            tile_row = row_id * N_COL + local_row
-            tile_col = local_col * N_COL + col_id
-            source, target = (tile_row, tile_col) if turn else (tile_col, tile_row)
-            straight, crossed = matches(cols_ref, source, target)
-
-            @pl.when(straight[0] + straight[1] + crossed[0] + crossed[1] > 0)
-            def _():
-                act(a, local_row, local_col, straight, crossed)
-
-            return carry
-
-        lax.fori_loop(0, count, body, 0)
-
-    def start(a, local_row, local_col, straight, crossed):
-        hold(a).start()
-        here, own_ref, other_ref, index = choose(local_row, local_col)
-
-        @pl.when(here)
+    slots, own_count = a_ref.shape[0], own_ref.shape[0]
+    used = plan_ref[4 * slots]
+    hold = lambda k: pltpu.make_async_copy(
+        a_ref.at[plan_ref[k]], held_ref.at[k], held_sems.at[k]
+    )
+    take = lambda k, ref, index: pltpu.make_async_copy(
+        ref.at[index], tiles_ref.at[k], tile_sems.at[k]
+    )
+
+    def start(k, carry):
+        index = plan_ref[2 * slots + k]
+
+        @pl.when(index < own_count)
         def _():
-            take(a, own_ref, index).start()
-
-        @pl.when(jnp.logical_not(here))
+            take(k, own_ref, index).start()
+
+        @pl.when(index >= own_count)
         def _():
-            take(a, other_ref, index).start()
-
-    def finish(a, local_row, local_col, straight, crossed):
-        here, own_ref, other_ref, index = choose(local_row, local_col)
-        take(a, own_ref, index).wait()
-        hold(a).wait()
-        product(held_ref[a], tiles_ref[a], local_row, local_col, straight, crossed)
-
-    each(start)
+            take(k, other_ref, index - own_count).start()
+
+        hold(k).start()
+        return carry
+
+    def finish(k, carry):
+        take(k, own_ref, 0).wait()
+        hold(k).wait()
+        whole = product(held_ref[k], tiles_ref[k])
+        add_columns(acc_ref, plan_ref[slots + k], whole, plan_ref[3 * slots + k])
+        return carry
+
+    lax.fori_loop(0, used, start, 0)
     clear(acc_ref)
-    each(finish)
+    lax.fori_loop(0, used, finish, 0)
 
 
 def prolong_kernel(
     where_ref,
-    place_ref,
-    cols_ref,
+    plan_ref,
     own_ref,
     other_ref,
     a_ref,
@@ -116,17 +132,10 @@
     theirs_high_ref,
     *scratch,
 ):
-    xh, core = where_ref[1], where_ref[2]
+    core = where_ref[2]
     acc_ref = scratch[0]
-
-    def choose(local_row, local_col):
-        return lax.rem(local_col, N_XH) == xh, own_ref, other_ref, local_col // N_XH
-
-    def product(block, tile, local_row, local_col, straight, crossed):
-        whole = jnp.dot(block, tile, preferred_element_type=jnp.float32)
-        add_columns(acc_ref, local_row, whole, straight, crossed)
-
-    each_match(where_ref, place_ref, cols_ref, a_ref, False, choose, scratch, product)
+    product = functools.partial(jnp.dot, preferred_element_type=jnp.float32)
+    each_used(plan_ref, own_ref, other_ref, a_ref, scratch, product)
 
     def store(q, carry):
         mine_ref[q] = acc_ref[2 * q + core].astype(jnp.bfloat16)
@@ -144,8 +153,7 @@
 
 def restrict_kernel(
     where_ref,
-    place_ref,
-    cols_ref,
+    plan_ref,
     own_ref,
     other_ref,
     a_ref,
@@ -157,19 +165,14 @@
 ):
     for i in range(where_ref.shape[0]):
         after_ref[i] = where_ref[i]
-    core, z = where_ref[2], where_ref[5]
-    acc_ref = scratch[0]
-
-    def choose(local_row, local_col):
-        return lax.rem(local_row, N_CORE) == core, own_ref, other_ref, local_row // N_CORE
-
-    def product(block, tile, local_row, local_col, straight, crossed):
-        whole = lax.dot_general(
+    z, acc_ref = where_ref[5], scratch[0]
+
+    def product(block, tile):
+        return lax.dot_general(
             block, tile, (((0,), (0,)), ((), ())), preferred_element_type=jnp.float32
         )
-        add_columns(acc_ref, local_col, whole, straight, crossed)
-
-    each_match(where_ref, place_ref, cols_ref, a_ref, True, choose, scratch, product)
+
+    each_used(plan_ref, own_ref, other_ref, a_ref, scratch, product)
 
     def store(q, carry):
         for third, ref in enumerate((own_third_ref, up_third_ref, down_third_ref)):
@@ -199,19 +202,17 @@
     lax.fori_loop(0, half, body, 0)
 
 
-def quarters_kernel(where_ref, own_ref, up_ref, down_ref, *quarter_refs):
-    quarter = where_ref[5] // 3
+def thirds_kernel(where_ref, own_ref, up_ref, down_ref, mine_ref, theirs_ref):
+    quarter, xh = where_ref[5] // 3, where_ref[1]
+    for i in range(mine_ref.shape[0]):
+        index = N_XH * lax.rem(quarter + i, 4)
+        mine_ref[i] = wide_sum((own_ref, up_ref, down_ref), index + xh)
+        theirs_ref[i] = wide_sum((own_ref, up_ref, down_ref), index + 1 - xh)
+
+
+def halves_kernel(mine_ref, near_ref, *quarter_refs):
     for i, ref in enumerate(quarter_refs):
-        for x in range(N_XH):
-            index = N_XH * lax.rem(quarter + i, 4) + x
-            ref[x] = wide_sum((own_ref, up_ref, down_ref), index)
-
-
-def halves_kernel(where_ref, *refs):
-    quarter_refs, (mine_ref, theirs_ref) = refs[:-2], refs[-2:]
-    xh = where_ref[1]
-    mine_ref[...] = wide_sum(quarter_refs, xh)
-    theirs_ref[...] = wide_sum(quarter_refs, 1 - xh)
+        ref[...] = wide_sum((mine_ref, near_ref), i)
 
 
 def update_kernel(mass_ref, resid_ref, projector_ref, *refs):
@@ -336,11 +337,18 @@
     p_other = turned(p_own, "xh", 1)
     r_own = after(r_own, p_own)
     r_other = turned(r_own, "core", 1)
+    where = after(where, p_own)
+    p_plan, r_plan = on_device(
+        plan_kernel,
+        (shape((4 * slots + 8,), jnp.int32),) * 2,
+        (where, place, p_flat, r_flat),
+        scalars_out=2,
+    )
 
     *r_thirds, where_then = on_device(
         restrict_kernel,
         (shape((N_ROW // 3, height, width)),) * 3 + (shape(where.shape, jnp.int32),),
-        (where, place, r_flat),
+        (where, r_plan),
         left=(r_own, r_other, tile_vals),
         scratch=[pltpu.VMEM((N_ROW, height, width), jnp.float32), *scratch],
         cost=COST,
@@ -351,7 +359,7 @@
     p_mine, p_low, p_high = on_device(
         prolong_kernel,
         (shape((HALF_COL, height, width)),) + (shape((HALF_COL // 2, height, width)),) * 2,
-        (where_then, place, p_flat),
+        (where_then, p_plan),
         left=(p_own, p_other, tile_vals),
         scratch=[pltpu.VMEM((N_COL, height, width), jnp.float32), *scratch],
         cost=COST,
@@ -359,13 +367,13 @@
     )
     p_near = (turned(p_low, "core", 1), turned(p_high, "core", 1))
 
-    r_quarters = on_device(
-        quarters_kernel, (shape((N_XH, height, width)),) * 4, (where,), *r_thirds
-    )
-    r_quarters = [turned(quarter, "z", -3 * i) for i, quarter in enumerate(r_quarters)]
-    r_mine, r_theirs = on_device(halves_kernel, (tile,) * 2, (where,), *r_quarters)
-    r_parts = (r_mine, turned(r_theirs, "xh", 1))
-    p_mine = after(p_mine, r_quarters[0])
+    r_mine, r_theirs = on_device(
+        thirds_kernel, (shape((4, height, width)),) * 2, (where,), *r_thirds
+    )
+    r_near = turned(r_theirs, "xh", 1)
+    r_quarters = on_device(halves_kernel, (tile,) * 4, (), r_mine, r_near)
+    r_parts = [turned(quarter, "z", -3 * i) for i, quarter in enumerate(r_quarters)]
+    p_mine = after(p_mine, r_theirs)
     (p_sum,) = on_device(pair_kernel, (shape((HALF_COL, height, width)),), (), p_mine, *p_near)
     p_parts = [lax.all_to_all(p_sum, ("y", "xl"), 0, 0, tiled=True)]
 

time: 170 us -> 166 us (0.976)
  starting transfers between devices: 62.4 us -> 58.8 us
    ppermute x10, starting transfers between devices: 45.3 us -> 41.7 us  [turned(): lax.ppermute(array, axis, [((i + by) % size, i) for i in range(size)])]
    pallas_call x8 -> x9, Pallas kernels: 12.7 us -> 13.3 us  [on_device(): pl.pallas_call(kernel, out_shape=out_shape, in_specs=[SMEM] * len(scalars...]
  transfers between devices with their start and end apart: 12 -> 12, of which waited for: 4 -> 5; matrix products, arithmetic and copies ran while one was open for 1% -> 1% of each run, Pallas kernels for 6% -> 6%
where the time goes in v5:
time: 166 us
  blocking collectives  70.2 us (42%)
  starting transfers between devices  58.8 us (35%)
  waiting for transfers between devices  18.3 us (11%)
  Pallas kernels  13.3 us (8%)
  local copies, waits for them, and re-layouts  3.36 us (2%)
    ppermute x10, starting transfers between devices, turned(): lax.ppermute(array, axis, [((i + by) % size, i) for i in range(size)])  41.7 us
    all_to_all x2, blocking collectives, gather(): return lax.all_to_all(copies, axes, 0, 0, tiled=True)  37.2 us
    all_gather x1, blocking collectives, shards(): p_own = lax.all_gather(res_p, 'z', axis=0, tiled=True)  33 us
    ppermute x10, waiting for transfers between devices, turned(): lax.ppermute(array, axis, [((i + by) % size, i) for i in range(size)])  18.3 us
    pallas_call x9, Pallas kernels, on_device(): pl.pallas_call(kernel, out_shape=out_shape, in_specs=[SMEM] * len(scalars...  13.3 us
    all_to_all x1, starting transfers between devices, gather(): return lax.all_to_all(copies, axes, 0, 0, tiled=True)  8.68 us
    all_to_all x1, starting transfers between devices, shards(): p_parts = [lax.all_to_all(p_sum, ('y', 'xl'), 0, 0, tiled=True)]  8.37 us
  transfers between devices with their start and end apart: 12, of which 5 were waited for; matrix products, arithmetic and copies ran while one was open for 1% of the time, Pallas kernels for 6%

profile of v5, /device:TPU:1, one launch (start us, length us, event | category | flops | bytes accessed | tf_op | source)
XLA Modules:
  0.0 165.9 jit_solution(15725794569478744946)
XLA Ops:
  0.6 0.0 copy-start.7
  0.6 0.0 copy-start.4
  0.7 0.0 copy-start.5
  0.7 2.1 %broadcast_in_dim.36 = bf16[16,256,128]{2,1,0:T(8,128)(2,1)} broadcast(bf16[256,128]{1,0:T(8,128)(2,1)} %bitcast.21), dimensions={1,2} | broadcast | bytes 1114112 | tf_op jit(solution)/shard_map/broadcast_in_dim | solution.py:286
  2.7 8.7 %all-to-all-start = ((bf16[16,256,128]{2,1,0:T(8,128)(2,1)}), bf16[16,256,128]{2,1,0:T(8,128)(2,1)S(1)}, u32[]{:S(2)}, u32[]{:S(2)}) async-start(bf16[16,256,128]{2,1,0:T(8,128)(2,1)} %broadcast_in_dim.36), calls=%async_computation | async-start | bytes 2097152 | tf_op jit(solution)/shard_map/all_to_all | solution.py:287
  11.4 33.0 %all_gather.3.refs_1_.own_ref = bf16[12,256,128]{2,1,0:T(8,128)(2,1)S(1)} all-gather(bf16[1,256,128]{2,1,0:T(8,128)(2,1)} %param.19), channel_id=1, replica_groups=mesh['z'=12,'xh'=2,'y'=8,'xl'=2,'core'=2] {'z'}, dimensions={0}, use_global_device_ids=true | all-gather | bytes 851968 | tf_op jit(solution)/shard_map/all_gather | solution.py:336
  44.4 0.0 all-to-all-done.refs_0_
  44.4 7.4 %collective-permute-start = (bf16[16,256,128]{2,1,0:T(8,128)(2,1)S(1)}, bf16[16,256,128]{2,1,0:T(8,128)(2,1)S(1)}, u32[]{:S(2)}, u32[]{:S(2)}) collective-permute-start(bf16[16,256,128]{2,1,0:T(8,128)(2,1)S(1)} %shard_map.140.own_ref), channel_id=1, source_target_pairs={{1,0},{0,1},{3,2},{2,3},{5,4},{4,5},{7,6},{6,7},{9,8},{8,9},{11,10... | collective-permute-start | bytes 3145736 | tf_op jit(solution)/shard_map/ppermute | solution.py:282
  51.8 4.4 %collective-permute-start.1 = (bf16[12,256,128]{2,1,0:T(8,128)(2,1)S(1)}, bf16[12,256,128]{2,1,0:T(8,128)(2,1)}, u32[]{:S(2)}, u32[]{:S(2)}) collective-permute-start(bf16[12,256,128]{2,1,0:T(8,128)(2,1)S(1)} %all_gather.3.refs_1_.own_ref), channel_id=1, source_target_pairs={{32,0},{0,32},{33,1},{1,33},{34,2},{2,34},{35,3},{3,35},{36,4},{4,... | collective-permute-start | bytes 2359304 | tf_op jit(solution)/shard_map/ppermute | solution.py:282
  56.9 0.1 stack.23.refs_0_
  56.9 0.0 copy-done.7
  56.9 0.1 reshape_squeeze.3.place_ref
  57.0 0.0 copy-done.4
  57.0 0.2 copy.30
  57.2 0.2 reshape.24.p_cols_ref
  57.5 0.0 copy-done.5
  57.5 0.2 copy.31
  57.7 0.2 reshape.25.r_cols_ref
  57.9 1.7 %shard_map.139 = (s32[136]{0:T(256)S(1)}, s32[136]{0:T(256)S(1)}) custom-call(s32[6]{0:T(128)S(1)} %shard_map.138.where_ref, s32[64]{0:T(128)S(1)} %reshape_squeeze.3.place_ref, s32[1536]{0:T(1024)S(1)} %reshape.24.p_cols_ref, s32[1536]{0:T(1024)S(1)} %reshape.25.r_cols_ref), custom_call_target="tpu_custom_call" | custom-call | tf_op jit(solution)/shard_map/pallas_call | solution.py:244
  59.6 0.0 collective-permute-done.other_ref
  59.6 4.5 %shard_map.141 = (bf16[8,256,128]{2,1,0:T(8,128)(2,1)S(1)}, bf16[8,256,128]{2,1,0:T(8,128)(2,1)S(1)}, bf16[8,256,128]{2,1,0:T(8,128)(2,1)S(1)}, s32[6]{0:T(128)S(1)}) custom-call(s32[6]{0:T(128)S(1)} %shard_map.138.where_ref, s32[136]{0:T(256)S(1)} %get-tuple-element.27.plan_ref, bf16[16,256,128]{2,1,0:T(8,128)(2,1)S(1)} %shard_map.140.own_ref, ...), custom_call_target="tpu_custom_call" | custom-call | flops 536870912 | bytes 12582912 | tf_op jit(solution)/shard_map/pallas_call | solution.py:244
  64.1 1.9 %collective-permute-start.2 = (bf16[8,256,128]{2,1,0:T(8,128)(2,1)S(1)}, bf16[8,256,128]{2,1,0:T(8,128)(2,1)S(1)}, u32[]{:S(2)}, u32[]{:S(2)}) collective-permute-start(bf16[8,256,128]{2,1,0:T(8,128)(2,1)S(1)} %get-tuple-element.32), channel_id=1, source_target_pairs={{704,0},{0,64},{64,128},{128,192},{192,256},{256,320},{320,384},{3... | collective-permute-start | bytes 1572872 | tf_op jit(solution)/shard_map/ppermute | solution.py:282
  66.0 5.7 %collective-permute-start.3 = (bf16[8,256,128]{2,1,0:T(8,128)(2,1)S(1)}, bf16[8,256,128]{2,1,0:T(8,128)(2,1)S(1)}, u32[]{:S(2)}, u32[]{:S(2)}) collective-permute-start(bf16[8,256,128]{2,1,0:T(8,128)(2,1)S(1)} %get-tuple-element.33), channel_id=1, source_target_pairs={{64,0},{128,64},{192,128},{256,192},{320,256},{384,320},{448,384},... | collective-permute-start | bytes 1572872 | tf_op jit(solution)/shard_map/ppermute | solution.py:282
  71.7 2.8 %collective-permute-done.1.other_ref = bf16[12,256,128]{2,1,0:T(8,128)(2,1)} collective-permute-done((bf16[12,256,128]{2,1,0:T(8,128)(2,1)S(1)}, bf16[12,256,128]{2,1,0:T(8,128)(2,1)}, u32[]{:S(2)}, u32[]{:S(2)}) %collective-permute-start.1) | collective-permute-done | bytes 786464 | tf_op jit(solution)/shard_map/ppermute | solution.py:282
  74.5 3.1 %shard_map.142 = (bf16[16,256,128]{2,1,0:T(8,128)(2,1)S(1)}, bf16[8,256,128]{2,1,0:T(8,128)(2,1)S(1)}, bf16[8,256,128]{2,1,0:T(8,128)(2,1)S(1)}) custom-call(s32[6]{0:T(128)S(1)} %get-tuple-element.28.where_ref, s32[136]{0:T(256)S(1)} %get-tuple-element.29.plan_ref, bf16[12,256,128]{2,1,0:T(8,128)(2,1)S(1)} %all_gather.3.refs_1_.own_ref, ...), custom_call_target="tpu_custom_call" | custom-call | flops 536870912 | bytes 12582912 | tf_op jit(solution)/shard_map/pallas_call | solution.py:244
  77.6 2.9 %collective-permute-start.4 = (bf16[8,256,128]{2,1,0:T(8,128)(2,1)S(1)}, bf16[8,256,128]{2,1,0:T(8,128)(2,1)S(1)}, u32[]{:S(2)}, u32[]{:S(2)}) collective-permute-start(bf16[8,256,128]{2,1,0:T(8,128)(2,1)S(1)} %get-tuple-element.35), channel_id=1, source_target_pairs={{1,0},{0,1},{3,2},{2,3},{5,4},{4,5},{7,6},{6,7},{9,8},{8,9},{11,10... | collective-permute-start | bytes 1572872 | tf_op jit(solution)/shard_map/ppermute | solution.py:282
  80.5 1.9 %collective-permute-start.5 = (bf16[8,256,128]{2,1,0:T(8,128)(2,1)S(1)}, bf16[8,256,128]{2,1,0:T(8,128)(2,1)S(1)}, u32[]{:S(2)}, u32[]{:S(2)}) collective-permute-start(bf16[8,256,128]{2,1,0:T(8,128)(2,1)S(1)} %get-tuple-element.36), channel_id=1, source_target_pairs={{1,0},{0,1},{3,2},{2,3},{5,4},{4,5},{7,6},{6,7},{9,8},{8,9},{11,10... | collective-permute-start | bytes 1572872 | tf_op jit(solution)/shard_map/ppermute | solution.py:282
  82.4 0.0 collective-permute-done.2.up_ref
  82.4 0.0 collective-permute-done.3.down_ref
  82.4 0.7 shard_map.143
  83.2 0.0 copy-start.8
  83.2 0.0 copy-start.6
  83.2 0.0 copy-start
  83.2 0.0 copy-start.1
  83.3 0.0 copy-start.2
  83.3 0.0 copy-start.3
  83.3 0.0 collective-permute-done.4.near_low_ref
  83.3 1.0 collective-permute-done.5.near_high_ref
  84.3 1.3 shard_map.145
  85.6 8.4 %all-to-all-start.1 = ((bf16[16,256,128]{2,1,0:T(8,128)(2,1)}), bf16[16,256,128]{2,1,0:T(8,128)(2,1)S(1)}, u32[]{:S(2)}, u32[]{:S(2)}) async-start(bf16[16,256,128]{2,1,0:T(8,128)(2,1)} %shard_map.145), calls=%async_computation.1 | async-start | bytes 2097152 | tf_op jit(solution)/shard_map/all_to_all | solution.py:378
  93.9 5.6 %collective-permute-start.6 = (bf16[4,256,128]{2,1,0:T(8,128)(2,1)S(1)}, bf16[4,256,128]{2,1,0:T(8,128)(2,1)S(1)}, u32[]{:S(2)}, u32[]{:S(2)}) collective-permute-start(bf16[4,256,128]{2,1,0:T(8,128)(2,1)S(1)} %get-tuple-element.34.refs_1_), channel_id=1, source_target_pairs={{32,0},{0,32},{33,1},{1,33},{34,2},{2,34},{35,3},{3,35},{36,4},{4,... | collective-permute-start | bytes 786440 | tf_op jit(solution)/shard_map/ppermute | solution.py:282
  99.6 0.0 copy-done.8
  99.6 0.1 eq.17
  99.7 6.3 %collective-permute-done.6.near_ref = bf16[4,256,128]{2,1,0:T(8,128)(2,1)S(1)} collective-permute-done((bf16[4,256,128]{2,1,0:T(8,128)(2,1)S(1)}, bf16[4,256,128]{2,1,0:T(8,128)(2,1)S(1)}, u32[]{:S(2)}, u32[]{:S(2)}) %collective-permute-start.6) | collective-permute-done | bytes 262176 | tf_op jit(solution)/shard_map/ppermute | solution.py:282
  106.0 0.1 shard_map.147
  106.1 1.9 %collective-permute-start.7 = (bf16[256,128]{1,0:T(8,128)(2,1)S(1)}, bf16[256,128]{1,0:T(8,128)(2,1)S(1)}, u32[]{:S(2)}, u32[]{:S(2)}) collective-permute-start(bf16[256,128]{1,0:T(8,128)(2,1)S(1)} %get-tuple-element.40), channel_id=1, source_target_pairs={{576,0},{640,64},{704,128},{0,192},{64,256},{128,320},{192,384},{2... | collective-permute-start | bytes 196616 | tf_op jit(solution)/shard_map/ppermute | solution.py:282
  108.0 4.3 %collective-permute-start.8 = (bf16[256,128]{1,0:T(8,128)(2,1)S(1)}, bf16[256,128]{1,0:T(8,128)(2,1)S(1)}, u32[]{:S(2)}, u32[]{:S(2)}) collective-permute-start(bf16[256,128]{1,0:T(8,128)(2,1)S(1)} %get-tuple-element.41), channel_id=1, source_target_pairs={{384,0},{448,64},{512,128},{576,192},{640,256},{704,320},{0,384},{... | collective-permute-start | bytes 196616 | tf_op jit(solution)/shard_map/ppermute | solution.py:282
  112.3 5.6 %collective-permute-start.9 = (bf16[256,128]{1,0:T(8,128)(2,1)S(1)}, bf16[256,128]{1,0:T(8,128)(2,1)S(1)}, u32[]{:S(2)}, u32[]{:S(2)}) collective-permute-start(bf16[256,128]{1,0:T(8,128)(2,1)S(1)} %get-tuple-element.42), channel_id=1, source_target_pairs={{192,0},{256,64},{320,128},{384,192},{448,256},{512,320},{576,384}... | collective-permute-start | bytes 196616 | tf_op jit(solution)/shard_map/ppermute | solution.py:282
  117.9 0.1 compare_select_fusion.projector_ref
  118.0 0.0 copy-done.6
  118.0 0.1 copy.32.mass_ref
  118.2 0.0 collective-permute-done.7.refs_1_
  118.2 2.8 %collective-permute-done.8.refs_2_ = bf16[256,128]{1,0:T(8,128)(2,1)S(1)} collective-permute-done((bf16[256,128]{1,0:T(8,128)(2,1)S(1)}, bf16[256,128]{1,0:T(8,128)(2,1)S(1)}, u32[]{:S(2)}, u32[]{:S(2)}) %collective-permute-start.8) | collective-permute-done | bytes 65568 | tf_op jit(solution)/shard_map/ppermute | solution.py:282
  120.9 5.4 %collective-permute-done.9.refs_3_ = bf16[256,128]{1,0:T(8,128)(2,1)S(1)} collective-permute-done((bf16[256,128]{1,0:T(8,128)(2,1)S(1)}, bf16[256,128]{1,0:T(8,128)(2,1)S(1)}, u32[]{:S(2)}, u32[]{:S(2)}) %collective-permute-start.9) | collective-permute-done | bytes 65568 | tf_op jit(solution)/shard_map/ppermute | solution.py:282
  126.4 0.0 copy-done
  126.4 0.3 shard_map.148
  126.7 0.0 all-to-all-done.1.refs_0_
  126.7 0.0 copy-done.1
  126.7 0.7 shard_map.146
  127.5 0.1 maximum_reduce_fusion
  127.6 10.3 %all_to_all.20 = f32[8,1,128]{2,1,0:T(1,128)S(1)} all-to-all(f32[8,1,128]{2,1,0:T(1,128)S(1)} %broadcast_in_dim.39), channel_id=1, replica_groups=mesh['z'=12,'xh'=2,'y'=8,'xl'=2,'core'=2] {'xh','xl','core'}, dimensions={0} | all-to-all | bytes 8192 | tf_op jit(solution)/shard_map/all_to_all | solution.py:287
  137.9 27.0 %all_to_all.21.sums_ref = f32[96,1,128]{2,1,0:T(1,128)S(1)} all-to-all(f32[96,1,128]{2,1,0:T(1,128)S(1)} %broadcast_in_dim.40), channel_id=1, replica_groups=mesh['z'=12,'xh'=2,'y'=8,'xl'=2,'core'=2] {'z','y'}, dimensions={0} | all-to-all | bytes 98304 | tf_op jit(solution)/shard_map/all_to_all | solution.py:287
  164.9 0.0 copy-done.2
  164.9 1.0 shard_map.149
  (10 shorter events, 0.1 us)
Async XLA Ops:
  0.6 56.3 %copy-start.7 = (s32[1,1,2,32]{3,2,1,0:T(2,128)S(1)}, s32[1,1,2,32]{3,2,1,0:T(2,128)}, u32[]{:S(2)}) copy-start(s32[1,1,2,32]{3,2,1,0:T(2,128)} %param.12) | copy-start | bytes 772
  0.6 56.4 %copy-start.4 = (s32[768,2]{0,1:T(2,128)S(1)}, s32[768,2]{0,1:T(2,128)}, u32[]{:S(2)}) copy-start(s32[768,2]{0,1:T(2,128)} %param.14) | copy-start | bytes 18436
  0.7 56.8 %copy-start.5 = (s32[768,2]{0,1:T(2,128)S(1)}, s32[768,2]{0,1:T(2,128)}, u32[]{:S(2)}) copy-start(s32[768,2]{0,1:T(2,128)} %param.15) | copy-start | bytes 18436
  2.7 41.7 %all-to-all-start = ((bf16[16,256,128]{2,1,0:T(8,128)(2,1)}), bf16[16,256,128]{2,1,0:T(8,128)(2,1)S(1)}, u32[]{:S(2)}, u32[]{:S(2)}) async-start(bf16[16,256,128]{2,1,0:T(8,128)(2,1)} %broadcast_in_dim.36), calls=%async_computation | async-start | bytes 2097152 | tf_op jit(solution)/shard_map/all_to_all | solution.py:287
  44.4 15.2 %collective-permute-start = (bf16[16,256,128]{2,1,0:T(8,128)(2,1)S(1)}, bf16[16,256,128]{2,1,0:T(8,128)(2,1)S(1)}, u32[]{:S(2)}, u32[]{:S(2)}) collective-permute-start(bf16[16,256,128]{2,1,0:T(8,128)(2,1)S(1)} %shard_map.140.own_ref), channel_id=1, source_target_pairs={{1,0},{0,1},{3,2},{2,3},{5,4},{4,5},{7,6},{6,7},{9,8},{8,9},{11,10... | collective-permute-start | bytes 3145736 | tf_op jit(solution)/shard_map/ppermute | solution.py:282
  51.8 22.7 %collective-permute-start.1 = (bf16[12,256,128]{2,1,0:T(8,128)(2,1)S(1)}, bf16[12,256,128]{2,1,0:T(8,128)(2,1)}, u32[]{:S(2)}, u32[]{:S(2)}) collective-permute-start(bf16[12,256,128]{2,1,0:T(8,128)(2,1)S(1)} %all_gather.3.refs_1_.own_ref), channel_id=1, source_target_pairs={{32,0},{0,32},{33,1},{1,33},{34,2},{2,34},{35,3},{3,35},{36,4},{4,... | collective-permute-start | bytes 2359304 | tf_op jit(solution)/shard_map/ppermute | solution.py:282
  64.1 18.4 %collective-permute-start.2 = (bf16[8,256,128]{2,1,0:T(8,128)(2,1)S(1)}, bf16[8,256,128]{2,1,0:T(8,128)(2,1)S(1)}, u32[]{:S(2)}, u32[]{:S(2)}) collective-permute-start(bf16[8,256,128]{2,1,0:T(8,128)(2,1)S(1)} %get-tuple-element.32), channel_id=1, source_target_pairs={{704,0},{0,64},{64,128},{128,192},{192,256},{256,320},{320,384},{3... | collective-permute-start | bytes 1572872 | tf_op jit(solution)/shard_map/ppermute | solution.py:282
  66.0 16.4 %collective-permute-start.3 = (bf16[8,256,128]{2,1,0:T(8,128)(2,1)S(1)}, bf16[8,256,128]{2,1,0:T(8,128)(2,1)S(1)}, u32[]{:S(2)}, u32[]{:S(2)}) collective-permute-start(bf16[8,256,128]{2,1,0:T(8,128)(2,1)S(1)} %get-tuple-element.33), channel_id=1, source_target_pairs={{64,0},{128,64},{192,128},{256,192},{320,256},{384,320},{448,384},... | collective-permute-start | bytes 1572872 | tf_op jit(solution)/shard_map/ppermute | solution.py:282
  77.6 5.7 %collective-permute-start.4 = (bf16[8,256,128]{2,1,0:T(8,128)(2,1)S(1)}, bf16[8,256,128]{2,1,0:T(8,128)(2,1)S(1)}, u32[]{:S(2)}, u32[]{:S(2)}) collective-permute-start(bf16[8,256,128]{2,1,0:T(8,128)(2,1)S(1)} %get-tuple-element.35), channel_id=1, source_target_pairs={{1,0},{0,1},{3,2},{2,3},{5,4},{4,5},{7,6},{6,7},{9,8},{8,9},{11,10... | collective-permute-start | bytes 1572872 | tf_op jit(solution)/shard_map/ppermute | solution.py:282
  80.5 3.8 %collective-permute-start.5 = (bf16[8,256,128]{2,1,0:T(8,128)(2,1)S(1)}, bf16[8,256,128]{2,1,0:T(8,128)(2,1)S(1)}, u32[]{:S(2)}, u32[]{:S(2)}) collective-permute-start(bf16[8,256,128]{2,1,0:T(8,128)(2,1)S(1)} %get-tuple-element.36), channel_id=1, source_target_pairs={{1,0},{0,1},{3,2},{2,3},{5,4},{4,5},{7,6},{6,7},{9,8},{8,9},{11,10... | collective-permute-start | bytes 1572872 | tf_op jit(solution)/shard_map/ppermute | solution.py:282
  83.2 16.4 %copy-start.8 = (s32[64]{0:T(128)S(1)}, s32[64]{0:T(128)}, u32[]{:S(2)}) copy-start(s32[64]{0:T(128)} %param.16) | copy-start | bytes 772
  83.2 34.8 %copy-start.6 = (f32[1,256]{1,0:T(1,128)S(1)}, f32[1,256]{1,0:T(1,128)}, u32[]{:S(2)}) copy-start(f32[1,256]{1,0:T(1,128)} %param.17) | copy-start | bytes 3076
  83.2 43.2 %copy-start = (bf16[1,256,128]{2,1,0:T(8,128)(2,1)S(1)}, bf16[1,256,128]{2,1,0:T(8,128)(2,1)}, u32[]{:S(2)}) copy-start(bf16[1,256,128]{2,1,0:T(8,128)(2,1)} %param.21) | copy-start | bytes 196612
  83.2 43.5 %copy-start.1 = (bf16[1,256,128]{2,1,0:T(8,128)(2,1)S(1)}, bf16[1,256,128]{2,1,0:T(8,128)(2,1)}, u32[]{:S(2)}) copy-start(bf16[1,256,128]{2,1,0:T(8,128)(2,1)} %param.19) | copy-start | bytes 196612
  83.3 81.7 %copy-start.2 = (bf16[1,256,128]{2,1,0:T(8,128)(2,1)S(1)}, bf16[1,256,128]{2,1,0:T(8,128)(2,1)}, u32[]{:S(2)}) copy-start(bf16[1,256,128]{2,1,0:T(8,128)(2,1)} %param.18) | copy-start | bytes 196612
  83.3 81.7 %copy-start.3 = (bf16[1,256,128]{2,1,0:T(8,128)(2,1)S(1)}, bf16[1,256,128]{2,1,0:T(8,128)(2,1)}, u32[]{:S(2)}) copy-start(bf16[1,256,128]{2,1,0:T(8,128)(2,1)} %param.20) | copy-start | bytes 196612
  85.6 41.2 %all-to-all-start.1 = ((bf16[16,256,128]{2,1,0:T(8,128)(2,1)}), bf16[16,256,128]{2,1,0:T(8,128)(2,1)S(1)}, u32[]{:S(2)}, u32[]{:S(2)}) async-start(bf16[16,256,128]{2,1,0:T(8,128)(2,1)} %shard_map.145), calls=%async_computation.1 | async-start | bytes 2097152 | tf_op jit(solution)/shard_map/all_to_all | solution.py:378
  93.9 12.1 %collective-permute-start.6 = (bf16[4,256,128]{2,1,0:T(8,128)(2,1)S(1)}, bf16[4,256,128]{2,1,0:T(8,128)(2,1)S(1)}, u32[]{:S(2)}, u32[]{:S(2)}) collective-permute-start(bf16[4,256,128]{2,1,0:T(8,128)(2,1)S(1)} %get-tuple-element.34.refs_1_), channel_id=1, source_target_pairs={{32,0},{0,32},{33,1},{1,33},{34,2},{2,34},{35,3},{3,35},{36,4},{4,... | collective-permute-start | bytes 786440 | tf_op jit(solution)/shard_map/ppermute | solution.py:282
  106.1 12.1 %collective-permute-start.7 = (bf16[256,128]{1,0:T(8,128)(2,1)S(1)}, bf16[256,128]{1,0:T(8,128)(2,1)S(1)}, u32[]{:S(2)}, u32[]{:S(2)}) collective-permute-start(bf16[256,128]{1,0:T(8,128)(2,1)S(1)} %get-tuple-element.40), channel_id=1, source_target_pairs={{576,0},{640,64},{704,128},{0,192},{64,256},{128,320},{192,384},{2... | collective-permute-start | bytes 196616 | tf_op jit(solution)/shard_map/ppermute | solution.py:282
  108.0 12.9 %collective-permute-start.8 = (bf16[256,128]{1,0:T(8,128)(2,1)S(1)}, bf16[256,128]{1,0:T(8,128)(2,1)S(1)}, u32[]{:S(2)}, u32[]{:S(2)}) collective-permute-start(bf16[256,128]{1,0:T(8,128)(2,1)S(1)} %get-tuple-element.41), channel_id=1, source_target_pairs={{384,0},{448,64},{512,128},{576,192},{640,256},{704,320},{0,384},{... | collective-permute-start | bytes 196616 | tf_op jit(solution)/shard_map/ppermute | solution.py:282
  112.3 14.1 %collective-permute-start.9 = (bf16[256,128]{1,0:T(8,128)(2,1)S(1)}, bf16[256,128]{1,0:T(8,128)(2,1)S(1)}, u32[]{:S(2)}, u32[]{:S(2)}) collective-permute-start(bf16[256,128]{1,0:T(8,128)(2,1)S(1)} %get-tuple-element.42), channel_id=1, source_target_pairs={{192,0},{256,64},{320,128},{384,192},{448,256},{512,320},{576,384}... | collective-permute-start | bytes 196616 | tf_op jit(solution)/shard_map/ppermute | solution.py:282

commit v6 on v5

--- a/solution.py
+++ b/solution.py
@@ -27,8 +27,8 @@
 
 
 def matches(cols_ref, source, target):
-    s0, s1 = cols_ref[2 * source], cols_ref[2 * source + 1]
-    t0, t1 = cols_ref[2 * target], cols_ref[2 * target + 1]
+    s0, s1 = cols_ref[0, source], cols_ref[1, source]
+    t0, t1 = cols_ref[0, target], cols_ref[1, target]
     flag = lambda same, bit: jnp.where(same, bit, 0)
     return flag(s0 == t0, 1) + flag(s1 == t1, 2) + flag(s1 == t0, 4) + flag(s0 == t1, 8)
 
@@ -36,7 +36,7 @@
 def plan_kernel(where_ref, place_ref, p_cols_ref, r_cols_ref, p_plan_ref, r_plan_ref):
     count, xh, core = where_ref[0], where_ref[1], where_ref[2]
     row_id, col_id = where_ref[3], where_ref[4]
-    slots = place_ref.shape[0] // 2
+    slots = place_ref.shape[1]
 
     def note(plan_ref, used, slot, target, index, blocks):
         for field, value in enumerate((slot, target, index, blocks)):
@@ -44,7 +44,7 @@
         return used + jnp.where(blocks != 0, 1, 0)
 
     def body(a, used):
-        local_row, local_col = place_ref[a], place_ref[slots + a]
+        local_row, local_col = place_ref[0, a], place_ref[1, a]
         tile_row = row_id * N_COL + local_row
         tile_col = local_col * N_COL + col_id
         p_index = local_col // N_XH + jnp.where(lax.rem(local_col, N_XH) == xh, 0, N_Z)
@@ -84,7 +84,7 @@
         acc_ref[index] += jnp.where(keep, pltpu.roll(whole, block, 1), 0.0)
 
 
-def each_used(plan_ref, own_ref, other_ref, a_ref, scratch, product):
+def each_used(plan_ref, own_ref, other_ref, a_ref, scratch, product, whole):
     acc_ref, held_ref, tiles_ref, held_sems, tile_sems = scratch
     slots, own_count = a_ref.shape[0], own_ref.shape[0]
     used = plan_ref[4 * slots]
@@ -94,6 +94,12 @@
     take = lambda k, ref, index: pltpu.make_async_copy(
         ref.at[index], tiles_ref.at[k], tile_sems.at[k]
     )
+    large = []
+    if whole:
+        large.append(pltpu.make_async_copy(a_ref, held_ref, held_sems.at[0]))
+        for i, ref in enumerate((own_ref, other_ref)):
+            part = tiles_ref.at[pl.ds(i * own_count, own_count)]
+            large.append(pltpu.make_async_copy(ref, part, tile_sems.at[i]))
 
     def start(k, carry):
         index = plan_ref[2 * slots + k]
@@ -110,14 +116,25 @@
         return carry
 
     def finish(k, carry):
-        take(k, own_ref, 0).wait()
-        hold(k).wait()
-        whole = product(held_ref[k], tiles_ref[k])
-        add_columns(acc_ref, plan_ref[slots + k], whole, plan_ref[3 * slots + k])
-        return carry
-
-    lax.fori_loop(0, used, start, 0)
+        if whole:
+            held, tile = plan_ref[k], plan_ref[2 * slots + k]
+        else:
+            held, tile = k, k
+            take(k, own_ref, 0).wait()
+            hold(k).wait()
+        result = product(held_ref[held], tiles_ref[tile])
+        add_columns(acc_ref, plan_ref[slots + k], result, plan_ref[3 * slots + k])
+        return carry
+
+    if whole:
+        for copy in large:
+            copy.start()
+    else:
+        lax.fori_loop(0, used, start, 0)
     clear(acc_ref)
+    if whole:
+        for copy in large:
+            copy.wait()
     lax.fori_loop(0, used, finish, 0)
 
 
@@ -135,7 +152,7 @@
     core = where_ref[2]
     acc_ref = scratch[0]
     product = functools.partial(jnp.dot, preferred_element_type=jnp.float32)
-    each_used(plan_ref, own_ref, other_ref, a_ref, scratch, product)
+    each_used(plan_ref, own_ref, other_ref, a_ref, scratch, product, True)
 
     def store(q, carry):
         mine_ref[q] = acc_ref[2 * q + core].astype(jnp.bfloat16)
@@ -172,7 +189,7 @@
             block, tile, (((0,), (0,)), ((), ())), preferred_element_type=jnp.float32
         )
 
-    each_used(plan_ref, own_ref, other_ref, a_ref, scratch, product)
+    each_used(plan_ref, own_ref, other_ref, a_ref, scratch, product, False)
 
     def store(q, carry):
         for third, ref in enumerate((own_third_ref, up_third_ref, down_third_ref)):
@@ -320,14 +337,13 @@
     col_id = (y * N_XL + xl) * N_CORE + core
     where = jnp.stack([a_count[0, 0], xh, core, row_id, col_id, z]).astype(jnp.int32)
     tile_vals = a_vals[0, 0]
-    place = a_place[0, 0].reshape(-1)
+    place = a_place[0, 0]
     height, width = res_p.shape[1:]
-    p_flat, r_flat = p_cols.reshape(-1), r_cols.reshape(-1)
     tile = shape((height, width))
     slots = tile_vals.shape[0]
     scratch = (
         pltpu.VMEM(tile_vals.shape, jnp.bfloat16),
-        pltpu.VMEM((slots, height, width), jnp.bfloat16),
+        pltpu.VMEM((max(slots, N_COL, N_ROW), height, width), jnp.bfloat16),
         pltpu.SemaphoreType.DMA((slots,)),
         pltpu.SemaphoreType.DMA((slots,)),
     )
@@ -341,7 +357,7 @@
     p_plan, r_plan = on_device(
         plan_kernel,
         (shape((4 * slots + 8,), jnp.int32),) * 2,
-        (where, place, p_flat, r_flat),
+        (where, place, p_cols.T, r_cols.T),
         scalars_out=2,
     )
 

time: 166 us -> 166 us (level)
  Pallas kernels: 13.3 us -> 19.4 us
  starting transfers between devices: 58.8 us -> 55.8 us
  blocking collectives: 70.2 us -> 67.7 us
    pallas_call x9, Pallas kernels: 13.3 us -> 19.4 us  [on_device(): pl.pallas_call(kernel, out_shape=out_shape, in_specs=[SMEM] * len(scalars...]
    ppermute x10, starting transfers between devices: 41.7 us -> 38.7 us  [turned(): lax.ppermute(array, axis, [((i + by) % size, i) for i in range(size)])]
    all_to_all x2, blocking collectives: 37.2 us -> 34.7 us  [gather(): return lax.all_to_all(copies, axes, 0, 0, tiled=True)]
  transfers between devices with their start and end apart: 12 -> 12, of which waited for: 5 -> 5; matrix products, arithmetic and copies ran while one was open for 1% -> 0% of each run, Pallas kernels for 6% -> 10%
where the time goes in v6:
time: 166 us; the launch traced here: 165 us
  blocking collectives  67.7 us (41%)
  starting transfers between devices  55.8 us (34%)
  Pallas kernels  19.4 us (12%)
  waiting for transfers between devices  18.2 us (11%)
  local copies, waits for them, and re-layouts  2.46 us (1%)
    ppermute x10, starting transfers between devices, turned(): lax.ppermute(array, axis, [((i + by) % size, i) for i in range(size)])  38.7 us
    all_to_all x2, blocking collectives, gather(): return lax.all_to_all(copies, axes, 0, 0, tiled=True)  34.7 us
    all_gather x1, blocking collectives, shards(): p_own = lax.all_gather(res_p, 'z', axis=0, tiled=True)  33 us
    pallas_call x9, Pallas kernels, on_device(): pl.pallas_call(kernel, out_shape=out_shape, in_specs=[SMEM] * len(scalars...  19.4 us
    ppermute x10, waiting for transfers between devices, turned(): lax.ppermute(array, axis, [((i + by) % size, i) for i in range(size)])  18.1 us
    all_to_all x1, starting transfers between devices, gather(): return lax.all_to_all(copies, axes, 0, 0, tiled=True)  8.68 us
    all_to_all x1, starting transfers between devices, shards(): p_parts = [lax.all_to_all(p_sum, ('y', 'xl'), 0, 0, tiled=True)]  8.41 us
  transfers between devices with their start and end apart: 12, of which 5 were waited for; matrix products, arithmetic and copies ran while one was open for 0% of the time, Pallas kernels for 10%

profile of v6, /device:TPU:1, one launch (start us, length us, event | category | flops | bytes accessed | tf_op | source)
XLA Modules:
  0.0 165.3 jit_solution(17633990541172360616)
XLA Ops:
  0.6 0.0 copy-start.6
  0.6 0.0 copy-start.4
  0.7 0.0 copy-start.5
  0.7 2.1 %broadcast_in_dim.36 = bf16[16,256,128]{2,1,0:T(8,128)(2,1)} broadcast(bf16[256,128]{1,0:T(8,128)(2,1)} %bitcast.24), dimensions={1,2} | broadcast | bytes 1114112 | tf_op jit(solution)/shard_map/broadcast_in_dim | solution.py:303
  2.7 8.7 %all-to-all-start = ((bf16[16,256,128]{2,1,0:T(8,128)(2,1)}), bf16[16,256,128]{2,1,0:T(8,128)(2,1)S(1)}, u32[]{:S(2)}, u32[]{:S(2)}) async-start(bf16[16,256,128]{2,1,0:T(8,128)(2,1)} %broadcast_in_dim.36), calls=%async_computation | async-start | bytes 2097152 | tf_op jit(solution)/shard_map/all_to_all | solution.py:304
  11.4 33.0 %all_gather.3.refs_1_.own_ref = bf16[12,256,128]{2,1,0:T(8,128)(2,1)S(1)} all-gather(bf16[1,256,128]{2,1,0:T(8,128)(2,1)} %param.19), channel_id=1, replica_groups=mesh['z'=12,'xh'=2,'y'=8,'xl'=2,'core'=2] {'z'}, dimensions={0}, use_global_device_ids=true | all-gather | bytes 851968 | tf_op jit(solution)/shard_map/all_gather | solution.py:352
  44.4 0.0 all-to-all-done.refs_0_
  44.4 7.4 %collective-permute-start = (bf16[16,256,128]{2,1,0:T(8,128)(2,1)S(1)}, bf16[16,256,128]{2,1,0:T(8,128)(2,1)S(1)}, u32[]{:S(2)}, u32[]{:S(2)}) collective-permute-start(bf16[16,256,128]{2,1,0:T(8,128)(2,1)S(1)} %shard_map.140.own_ref), channel_id=1, source_target_pairs={{1,0},{0,1},{3,2},{2,3},{5,4},{4,5},{7,6},{6,7},{9,8},{8,9},{11,10... | collective-permute-start | bytes 3145736 | tf_op jit(solution)/shard_map/ppermute | solution.py:299
  51.8 4.4 %collective-permute-start.1 = (bf16[12,256,128]{2,1,0:T(8,128)(2,1)S(1)}, bf16[12,256,128]{2,1,0:T(8,128)(2,1)}, u32[]{:S(2)}, u32[]{:S(2)}) collective-permute-start(bf16[12,256,128]{2,1,0:T(8,128)(2,1)S(1)} %all_gather.3.refs_1_.own_ref), channel_id=1, source_target_pairs={{32,0},{0,32},{33,1},{1,33},{34,2},{2,34},{35,3},{3,35},{36,4},{4,... | collective-permute-start | bytes 2359304 | tf_op jit(solution)/shard_map/ppermute | solution.py:299
  56.9 0.1 stack.23.refs_0_
  56.9 0.0 copy-done.6
  56.9 0.0 copy-done.4
  56.9 0.0 copy-done.5
  57.0 2.7 %shard_map.139 = (s32[136]{0:T(256)S(1)}, s32[136]{0:T(256)S(1)}) custom-call(s32[6]{0:T(128)S(1)} %shard_map.138.where_ref, s32[2,32]{1,0:T(2,128)S(1)} %bitcast.33, s32[2,768]{1,0:T(2,128)S(1)} %bitcast.31, s32[2,768]{1,0:T(2,128)S(1)} %bitcast.32), custom_call_target="tpu_custom_call" | custom-call | tf_op jit(solution)/shard_map/pallas_call | solution.py:261
  59.7 0.0 collective-permute-done.other_ref
  59.7 6.5 %shard_map.141 = (bf16[8,256,128]{2,1,0:T(8,128)(2,1)S(1)}, bf16[8,256,128]{2,1,0:T(8,128)(2,1)S(1)}, bf16[8,256,128]{2,1,0:T(8,128)(2,1)S(1)}, s32[6]{0:T(128)S(1)}) custom-call(s32[6]{0:T(128)S(1)} %shard_map.138.where_ref, s32[136]{0:T(256)S(1)} %get-tuple-element.27.plan_ref, bf16[16,256,128]{2,1,0:T(8,128)(2,1)S(1)} %shard_map.140.own_ref, ...), custom_call_target="tpu_custom_call" | custom-call | flops 536870912 | bytes 12582912 | tf_op jit(solution)/shard_map/pallas_call | solution.py:261
  66.2 1.9 %collective-permute-start.2 = (bf16[8,256,128]{2,1,0:T(8,128)(2,1)S(1)}, bf16[8,256,128]{2,1,0:T(8,128)(2,1)S(1)}, u32[]{:S(2)}, u32[]{:S(2)}) collective-permute-start(bf16[8,256,128]{2,1,0:T(8,128)(2,1)S(1)} %get-tuple-element.32), channel_id=1, source_target_pairs={{704,0},{0,64},{64,128},{128,192},{192,256},{256,320},{320,384},{3... | collective-permute-start | bytes 1572872 | tf_op jit(solution)/shard_map/ppermute | solution.py:299
  68.1 4.6 %collective-permute-start.3 = (bf16[8,256,128]{2,1,0:T(8,128)(2,1)S(1)}, bf16[8,256,128]{2,1,0:T(8,128)(2,1)S(1)}, u32[]{:S(2)}, u32[]{:S(2)}) collective-permute-start(bf16[8,256,128]{2,1,0:T(8,128)(2,1)S(1)} %get-tuple-element.33), channel_id=1, source_target_pairs={{64,0},{128,64},{192,128},{256,192},{320,256},{384,320},{448,384},... | collective-permute-start | bytes 1572872 | tf_op jit(solution)/shard_map/ppermute | solution.py:299
  72.7 1.8 %collective-permute-done.1.other_ref = bf16[12,256,128]{2,1,0:T(8,128)(2,1)} collective-permute-done((bf16[12,256,128]{2,1,0:T(8,128)(2,1)S(1)}, bf16[12,256,128]{2,1,0:T(8,128)(2,1)}, u32[]{:S(2)}, u32[]{:S(2)}) %collective-permute-start.1) | collective-permute-done | bytes 786464 | tf_op jit(solution)/shard_map/ppermute | solution.py:299
  74.5 6.1 %shard_map.142 = (bf16[16,256,128]{2,1,0:T(8,128)(2,1)S(1)}, bf16[8,256,128]{2,1,0:T(8,128)(2,1)S(1)}, bf16[8,256,128]{2,1,0:T(8,128)(2,1)S(1)}) custom-call(s32[6]{0:T(128)S(1)} %get-tuple-element.28.where_ref, s32[136]{0:T(256)S(1)} %get-tuple-element.29.plan_ref, bf16[12,256,128]{2,1,0:T(8,128)(2,1)S(1)} %all_gather.3.refs_1_.own_ref, ...), custom_call_target="tpu_custom_call" | custom-call | flops 536870912 | bytes 12582912 | tf_op jit(solution)/shard_map/pallas_call | solution.py:261
  80.6 1.9 %collective-permute-start.4 = (bf16[8,256,128]{2,1,0:T(8,128)(2,1)S(1)}, bf16[8,256,128]{2,1,0:T(8,128)(2,1)S(1)}, u32[]{:S(2)}, u32[]{:S(2)}) collective-permute-start(bf16[8,256,128]{2,1,0:T(8,128)(2,1)S(1)} %get-tuple-element.35), channel_id=1, source_target_pairs={{1,0},{0,1},{3,2},{2,3},{5,4},{4,5},{7,6},{6,7},{9,8},{8,9},{11,10... | collective-permute-start | bytes 1572872 | tf_op jit(solution)/shard_map/ppermute | solution.py:299
  82.5 2.4 %collective-permute-start.5 = (bf16[8,256,128]{2,1,0:T(8,128)(2,1)S(1)}, bf16[8,256,128]{2,1,0:T(8,128)(2,1)S(1)}, u32[]{:S(2)}, u32[]{:S(2)}) collective-permute-start(bf16[8,256,128]{2,1,0:T(8,128)(2,1)S(1)} %get-tuple-element.36), channel_id=1, source_target_pairs={{1,0},{0,1},{3,2},{2,3},{5,4},{4,5},{7,6},{6,7},{9,8},{8,9},{11,10... | collective-permute-start | bytes 1572872 | tf_op jit(solution)/shard_map/ppermute | solution.py:299
  84.9 0.0 collective-permute-done.2.up_ref
  84.9 0.0 collective-permute-done.3.down_ref
  84.9 0.7 shard_map.143
  85.7 0.0 copy-start.8
  85.7 0.0 copy-start.7
  85.7 0.0 copy-start
  85.7 0.0 copy-start.1
  85.8 0.0 copy-start.2
  85.8 0.0 copy-start.3
  85.8 0.0 collective-permute-done.4.near_low_ref
  85.8 0.6 collective-permute-done.5.near_high_ref
  86.4 1.3 shard_map.145
  87.7 8.4 %all-to-all-start.1 = ((bf16[16,256,128]{2,1,0:T(8,128)(2,1)}), bf16[16,256,128]{2,1,0:T(8,128)(2,1)S(1)}, u32[]{:S(2)}, u32[]{:S(2)}) async-start(bf16[16,256,128]{2,1,0:T(8,128)(2,1)} %shard_map.145), calls=%async_computation.1 | async-start | bytes 2097152 | tf_op jit(solution)/shard_map/all_to_all | solution.py:394
  96.1 4.1 %collective-permute-start.6 = (bf16[4,256,128]{2,1,0:T(8,128)(2,1)S(1)}, bf16[4,256,128]{2,1,0:T(8,128)(2,1)S(1)}, u32[]{:S(2)}, u32[]{:S(2)}) collective-permute-start(bf16[4,256,128]{2,1,0:T(8,128)(2,1)S(1)} %get-tuple-element.34.refs_1_), channel_id=1, source_target_pairs={{32,0},{0,32},{33,1},{1,33},{34,2},{2,34},{35,3},{3,35},{36,4},{4,... | collective-permute-start | bytes 786440 | tf_op jit(solution)/shard_map/ppermute | solution.py:299
  100.2 0.0 copy-done.8
  100.2 0.1 eq.17
  100.3 6.9 %collective-permute-done.6.near_ref = bf16[4,256,128]{2,1,0:T(8,128)(2,1)S(1)} collective-permute-done((bf16[4,256,128]{2,1,0:T(8,128)(2,1)S(1)}, bf16[4,256,128]{2,1,0:T(8,128)(2,1)S(1)}, u32[]{:S(2)}, u32[]{:S(2)}) %collective-permute-start.6) | collective-permute-done | bytes 262176 | tf_op jit(solution)/shard_map/ppermute | solution.py:299
  107.2 0.1 shard_map.147
  107.3 1.9 %collective-permute-start.7 = (bf16[256,128]{1,0:T(8,128)(2,1)S(1)}, bf16[256,128]{1,0:T(8,128)(2,1)S(1)}, u32[]{:S(2)}, u32[]{:S(2)}) collective-permute-start(bf16[256,128]{1,0:T(8,128)(2,1)S(1)} %get-tuple-element.40), channel_id=1, source_target_pairs={{576,0},{640,64},{704,128},{0,192},{64,256},{128,320},{192,384},{2... | collective-permute-start | bytes 196616 | tf_op jit(solution)/shard_map/ppermute | solution.py:299
  109.2 7.6 %collective-permute-start.8 = (bf16[256,128]{1,0:T(8,128)(2,1)S(1)}, bf16[256,128]{1,0:T(8,128)(2,1)S(1)}, u32[]{:S(2)}, u32[]{:S(2)}) collective-permute-start(bf16[256,128]{1,0:T(8,128)(2,1)S(1)} %get-tuple-element.41), channel_id=1, source_target_pairs={{384,0},{448,64},{512,128},{576,192},{640,256},{704,320},{0,384},{... | collective-permute-start | bytes 196616 | tf_op jit(solution)/shard_map/ppermute | solution.py:299
  116.9 2.5 %collective-permute-start.9 = (bf16[256,128]{1,0:T(8,128)(2,1)S(1)}, bf16[256,128]{1,0:T(8,128)(2,1)S(1)}, u32[]{:S(2)}, u32[]{:S(2)}) collective-permute-start(bf16[256,128]{1,0:T(8,128)(2,1)S(1)} %get-tuple-element.42), channel_id=1, source_target_pairs={{192,0},{256,64},{320,128},{384,192},{448,256},{512,320},{576,384}... | collective-permute-start | bytes 196616 | tf_op jit(solution)/shard_map/ppermute | solution.py:299
  119.3 0.1 compare_select_fusion.projector_ref
  119.4 0.0 copy-done.7
  119.4 0.1 copy.24.mass_ref
  119.6 0.0 collective-permute-done.7.refs_1_
  119.6 1.3 collective-permute-done.8.refs_2_
  120.9 7.5 %collective-permute-done.9.refs_3_ = bf16[256,128]{1,0:T(8,128)(2,1)S(1)} collective-permute-done((bf16[256,128]{1,0:T(8,128)(2,1)S(1)}, bf16[256,128]{1,0:T(8,128)(2,1)S(1)}, u32[]{:S(2)}, u32[]{:S(2)}) %collective-permute-start.9) | collective-permute-done | bytes 65568 | tf_op jit(solution)/shard_map/ppermute | solution.py:299
  128.4 0.0 copy-done
  128.4 0.3 shard_map.148
  128.7 0.0 all-to-all-done.1.refs_0_
  128.7 0.0 copy-done.1
  128.7 0.7 shard_map.146
  129.5 0.1 maximum_reduce_fusion
  129.6 8.7 %all_to_all.20 = f32[8,1,128]{2,1,0:T(1,128)S(1)} all-to-all(f32[8,1,128]{2,1,0:T(1,128)S(1)} %broadcast_in_dim.39), channel_id=1, replica_groups=mesh['z'=12,'xh'=2,'y'=8,'xl'=2,'core'=2] {'xh','xl','core'}, dimensions={0} | all-to-all | bytes 8192 | tf_op jit(solution)/shard_map/all_to_all | solution.py:304
  138.4 26.0 %all_to_all.21.sums_ref = f32[96,1,128]{2,1,0:T(1,128)S(1)} all-to-all(f32[96,1,128]{2,1,0:T(1,128)S(1)} %broadcast_in_dim.40), channel_id=1, replica_groups=mesh['z'=12,'xh'=2,'y'=8,'xl'=2,'core'=2] {'z','y'}, dimensions={0} | all-to-all | bytes 98304 | tf_op jit(solution)/shard_map/all_to_all | solution.py:304
  164.4 0.0 copy-done.2
  164.4 0.0 copy-done.3
  164.4 1.0 shard_map.149
  (9 shorter events, 0.1 us)
Async XLA Ops:
  0.6 56.3 %copy-start.6 = (s32[1,1,2,32]{3,2,1,0:T(2,128)S(1)}, s32[1,1,2,32]{3,2,1,0:T(2,128)}, u32[]{:S(2)}) copy-start(s32[1,1,2,32]{3,2,1,0:T(2,128)} %param.12) | copy-start | bytes 772
  0.6 56.3 %copy-start.4 = (s32[768,2]{0,1:T(2,128)S(1)}, s32[768,2]{0,1:T(2,128)}, u32[]{:S(2)}) copy-start(s32[768,2]{0,1:T(2,128)} %param.14) | copy-start | bytes 18436
  0.7 56.3 %copy-start.5 = (s32[768,2]{0,1:T(2,128)S(1)}, s32[768,2]{0,1:T(2,128)}, u32[]{:S(2)}) copy-start(s32[768,2]{0,1:T(2,128)} %param.15) | copy-start | bytes 18436
  2.7 41.7 %all-to-all-start = ((bf16[16,256,128]{2,1,0:T(8,128)(2,1)}), bf16[16,256,128]{2,1,0:T(8,128)(2,1)S(1)}, u32[]{:S(2)}, u32[]{:S(2)}) async-start(bf16[16,256,128]{2,1,0:T(8,128)(2,1)} %broadcast_in_dim.36), calls=%async_computation | async-start | bytes 2097152 | tf_op jit(solution)/shard_map/all_to_all | solution.py:304
  44.4 15.3 %collective-permute-start = (bf16[16,256,128]{2,1,0:T(8,128)(2,1)S(1)}, bf16[16,256,128]{2,1,0:T(8,128)(2,1)S(1)}, u32[]{:S(2)}, u32[]{:S(2)}) collective-permute-start(bf16[16,256,128]{2,1,0:T(8,128)(2,1)S(1)} %shard_map.140.own_ref), channel_id=1, source_target_pairs={{1,0},{0,1},{3,2},{2,3},{5,4},{4,5},{7,6},{6,7},{9,8},{8,9},{11,10... | collective-permute-start | bytes 3145736 | tf_op jit(solution)/shard_map/ppermute | solution.py:299
  51.8 22.7 %collective-permute-start.1 = (bf16[12,256,128]{2,1,0:T(8,128)(2,1)S(1)}, bf16[12,256,128]{2,1,0:T(8,128)(2,1)}, u32[]{:S(2)}, u32[]{:S(2)}) collective-permute-start(bf16[12,256,128]{2,1,0:T(8,128)(2,1)S(1)} %all_gather.3.refs_1_.own_ref), channel_id=1, source_target_pairs={{32,0},{0,32},{33,1},{1,33},{34,2},{2,34},{35,3},{3,35},{36,4},{4,... | collective-permute-start | bytes 2359304 | tf_op jit(solution)/shard_map/ppermute | solution.py:299
  66.2 18.7 %collective-permute-start.2 = (bf16[8,256,128]{2,1,0:T(8,128)(2,1)S(1)}, bf16[8,256,128]{2,1,0:T(8,128)(2,1)S(1)}, u32[]{:S(2)}, u32[]{:S(2)}) collective-permute-start(bf16[8,256,128]{2,1,0:T(8,128)(2,1)S(1)} %get-tuple-element.32), channel_id=1, source_target_pairs={{704,0},{0,64},{64,128},{128,192},{192,256},{256,320},{320,384},{3... | collective-permute-start | bytes 1572872 | tf_op jit(solution)/shard_map/ppermute | solution.py:299
  68.1 16.8 %collective-permute-start.3 = (bf16[8,256,128]{2,1,0:T(8,128)(2,1)S(1)}, bf16[8,256,128]{2,1,0:T(8,128)(2,1)S(1)}, u32[]{:S(2)}, u32[]{:S(2)}) collective-permute-start(bf16[8,256,128]{2,1,0:T(8,128)(2,1)S(1)} %get-tuple-element.33), channel_id=1, source_target_pairs={{64,0},{128,64},{192,128},{256,192},{320,256},{384,320},{448,384},... | collective-permute-start | bytes 1572872 | tf_op jit(solution)/shard_map/ppermute | solution.py:299
  80.6 5.2 %collective-permute-start.4 = (bf16[8,256,128]{2,1,0:T(8,128)(2,1)S(1)}, bf16[8,256,128]{2,1,0:T(8,128)(2,1)S(1)}, u32[]{:S(2)}, u32[]{:S(2)}) collective-permute-start(bf16[8,256,128]{2,1,0:T(8,128)(2,1)S(1)} %get-tuple-element.35), channel_id=1, source_target_pairs={{1,0},{0,1},{3,2},{2,3},{5,4},{4,5},{7,6},{6,7},{9,8},{8,9},{11,10... | collective-permute-start | bytes 1572872 | tf_op jit(solution)/shard_map/ppermute | solution.py:299
  82.5 3.9 %collective-permute-start.5 = (bf16[8,256,128]{2,1,0:T(8,128)(2,1)S(1)}, bf16[8,256,128]{2,1,0:T(8,128)(2,1)S(1)}, u32[]{:S(2)}, u32[]{:S(2)}) collective-permute-start(bf16[8,256,128]{2,1,0:T(8,128)(2,1)S(1)} %get-tuple-element.36), channel_id=1, source_target_pairs={{1,0},{0,1},{3,2},{2,3},{5,4},{4,5},{7,6},{6,7},{9,8},{8,9},{11,10... | collective-permute-start | bytes 1572872 | tf_op jit(solution)/shard_map/ppermute | solution.py:299
  85.7 14.5 %copy-start.8 = (s32[64]{0:T(128)S(1)}, s32[64]{0:T(128)}, u32[]{:S(2)}) copy-start(s32[64]{0:T(128)} %param.16) | copy-start | bytes 772
  85.7 33.7 %copy-start.7 = (f32[1,256]{1,0:T(1,128)S(1)}, f32[1,256]{1,0:T(1,128)}, u32[]{:S(2)}) copy-start(f32[1,256]{1,0:T(1,128)} %param.17) | copy-start | bytes 3076
  85.7 42.7 %copy-start = (bf16[1,256,128]{2,1,0:T(8,128)(2,1)S(1)}, bf16[1,256,128]{2,1,0:T(8,128)(2,1)}, u32[]{:S(2)}) copy-start(bf16[1,256,128]{2,1,0:T(8,128)(2,1)} %param.21) | copy-start | bytes 196612
  85.7 43.0 %copy-start.1 = (bf16[1,256,128]{2,1,0:T(8,128)(2,1)S(1)}, bf16[1,256,128]{2,1,0:T(8,128)(2,1)}, u32[]{:S(2)}) copy-start(bf16[1,256,128]{2,1,0:T(8,128)(2,1)} %param.19) | copy-start | bytes 196612
  85.8 78.6 %copy-start.2 = (bf16[1,256,128]{2,1,0:T(8,128)(2,1)S(1)}, bf16[1,256,128]{2,1,0:T(8,128)(2,1)}, u32[]{:S(2)}) copy-start(bf16[1,256,128]{2,1,0:T(8,128)(2,1)} %param.18) | copy-start | bytes 196612
  85.8 78.6 %copy-start.3 = (bf16[1,256,128]{2,1,0:T(8,128)(2,1)S(1)}, bf16[1,256,128]{2,1,0:T(8,128)(2,1)}, u32[]{:S(2)}) copy-start(bf16[1,256,128]{2,1,0:T(8,128)(2,1)} %param.20) | copy-start | bytes 196612
  87.7 41.0 %all-to-all-start.1 = ((bf16[16,256,128]{2,1,0:T(8,128)(2,1)}), bf16[16,256,128]{2,1,0:T(8,128)(2,1)S(1)}, u32[]{:S(2)}, u32[]{:S(2)}) async-start(bf16[16,256,128]{2,1,0:T(8,128)(2,1)} %shard_map.145), calls=%async_computation.1 | async-start | bytes 2097152 | tf_op jit(solution)/shard_map/all_to_all | solution.py:394
  96.1 11.1 %collective-permute-start.6 = (bf16[4,256,128]{2,1,0:T(8,128)(2,1)S(1)}, bf16[4,256,128]{2,1,0:T(8,128)(2,1)S(1)}, u32[]{:S(2)}, u32[]{:S(2)}) collective-permute-start(bf16[4,256,128]{2,1,0:T(8,128)(2,1)S(1)} %get-tuple-element.34.refs_1_), channel_id=1, source_target_pairs={{32,0},{0,32},{33,1},{1,33},{34,2},{2,34},{35,3},{3,35},{36,4},{4,... | collective-permute-start | bytes 786440 | tf_op jit(solution)/shard_map/ppermute | solution.py:299
  107.3 12.3 %collective-permute-start.7 = (bf16[256,128]{1,0:T(8,128)(2,1)S(1)}, bf16[256,128]{1,0:T(8,128)(2,1)S(1)}, u32[]{:S(2)}, u32[]{:S(2)}) collective-permute-start(bf16[256,128]{1,0:T(8,128)(2,1)S(1)} %get-tuple-element.40), channel_id=1, source_target_pairs={{576,0},{640,64},{704,128},{0,192},{64,256},{128,320},{192,384},{2... | collective-permute-start | bytes 196616 | tf_op jit(solution)/shard_map/ppermute | solution.py:299
  109.2 11.7 %collective-permute-start.8 = (bf16[256,128]{1,0:T(8,128)(2,1)S(1)}, bf16[256,128]{1,0:T(8,128)(2,1)S(1)}, u32[]{:S(2)}, u32[]{:S(2)}) collective-permute-start(bf16[256,128]{1,0:T(8,128)(2,1)S(1)} %get-tuple-element.41), channel_id=1, source_target_pairs={{384,0},{448,64},{512,128},{576,192},{640,256},{704,320},{0,384},{... | collective-permute-start | bytes 196616 | tf_op jit(solution)/shard_map/ppermute | solution.py:299
  116.9 11.5 %collective-permute-start.9 = (bf16[256,128]{1,0:T(8,128)(2,1)S(1)}, bf16[256,128]{1,0:T(8,128)(2,1)S(1)}, u32[]{:S(2)}, u32[]{:S(2)}) collective-permute-start(bf16[256,128]{1,0:T(8,128)(2,1)S(1)} %get-tuple-element.42), channel_id=1, source_target_pairs={{192,0},{256,64},{320,128},{384,192},{448,256},{512,320},{576,384}... | collective-permute-start | bytes 196616 | tf_op jit(solution)/shard_map/ppermute | solution.py:299

commit v7 on v5

--- a/solution.py
+++ b/solution.py
@@ -27,8 +27,8 @@
 
 
 def matches(cols_ref, source, target):
-    s0, s1 = cols_ref[2 * source], cols_ref[2 * source + 1]
-    t0, t1 = cols_ref[2 * target], cols_ref[2 * target + 1]
+    s0, s1 = cols_ref[0, source], cols_ref[1, source]
+    t0, t1 = cols_ref[0, target], cols_ref[1, target]
     flag = lambda same, bit: jnp.where(same, bit, 0)
     return flag(s0 == t0, 1) + flag(s1 == t1, 2) + flag(s1 == t0, 4) + flag(s0 == t1, 8)
 
@@ -36,7 +36,7 @@
 def plan_kernel(where_ref, place_ref, p_cols_ref, r_cols_ref, p_plan_ref, r_plan_ref):
     count, xh, core = where_ref[0], where_ref[1], where_ref[2]
     row_id, col_id = where_ref[3], where_ref[4]
-    slots = place_ref.shape[0] // 2
+    slots = place_ref.shape[1]
 
     def note(plan_ref, used, slot, target, index, blocks):
         for field, value in enumerate((slot, target, index, blocks)):
@@ -44,7 +44,7 @@
         return used + jnp.where(blocks != 0, 1, 0)
 
     def body(a, used):
-        local_row, local_col = place_ref[a], place_ref[slots + a]
+        local_row, local_col = place_ref[0, a], place_ref[1, a]
         tile_row = row_id * N_COL + local_row
         tile_col = local_col * N_COL + col_id
         p_index = local_col // N_XH + jnp.where(lax.rem(local_col, N_XH) == xh, 0, N_Z)
@@ -320,9 +320,8 @@
     col_id = (y * N_XL + xl) * N_CORE + core
     where = jnp.stack([a_count[0, 0], xh, core, row_id, col_id, z]).astype(jnp.int32)
     tile_vals = a_vals[0, 0]
-    place = a_place[0, 0].reshape(-1)
+    place = a_place[0, 0]
     height, width = res_p.shape[1:]
-    p_flat, r_flat = p_cols.reshape(-1), r_cols.reshape(-1)
     tile = shape((height, width))
     slots = tile_vals.shape[0]
     scratch = (
@@ -341,7 +340,7 @@
     p_plan, r_plan = on_device(
         plan_kernel,
         (shape((4 * slots + 8,), jnp.int32),) * 2,
-        (where, place, p_flat, r_flat),
+        (where, place, p_cols.T, r_cols.T),
         scalars_out=2,
     )
 
@@ -372,7 +371,7 @@
     )
     r_near = turned(r_theirs, "xh", 1)
     r_quarters = on_device(halves_kernel, (tile,) * 4, (), r_mine, r_near)
-    r_parts = [turned(quarter, "z", -3 * i) for i, quarter in enumerate(r_quarters)]
+    r_parts = [turned(r_quarters[i], "z", -3 * i) for i in (2, 1, 3, 0)]
     p_mine = after(p_mine, r_theirs)
     (p_sum,) = on_device(pair_kernel, (shape((HALF_COL, height, width)),), (), p_mine, *p_near)
     p_parts = [lax.all_to_all(p_sum, ("y", "xl"), 0, 0, tiled=True)]

time: 166 us -> 169 us (1.018); the launches traced: 166 us -> 166 us
  blocking collectives: 70.2 us -> 72.8 us
    all_to_all x1, starting transfers between devices: 8.37 us -> 4.92 us  [shards(): p_parts = [lax.all_to_all(p_sum, ('y', 'xl'), 0, 0, tiled=True)]]
    all_to_all x2, blocking collectives: 37.2 us -> 39.9 us  [gather(): return lax.all_to_all(copies, axes, 0, 0, tiled=True)]
    ppermute x10, starting transfers between devices: 41.7 us -> 43.6 us  [turned(): lax.ppermute(array, axis, [((i + by) % size, i) for i in range(size)])]
  transfers between devices with their start and end apart: 12 -> 12, of which waited for: 5 -> 4; matrix products, arithmetic and copies ran while one was open for 1% -> 0% of each run, Pallas kernels for 6% -> 7%
where the time goes in v7:
time: 169 us; the launch traced here: 166 us
  blocking collectives  72.8 us (43%)
  starting transfers between devices  57.2 us (34%)
  waiting for transfers between devices  17.8 us (11%)
  Pallas kernels  14.1 us (8%)
  local copies, waits for them, and re-layouts  2.46 us (1%)
    ppermute x10, starting transfers between devices, turned(): lax.ppermute(array, axis, [((i + by) % size, i) for i in range(size)])  43.6 us
    all_to_all x2, blocking collectives, gather(): return lax.all_to_all(copies, axes, 0, 0, tiled=True)  39.9 us
    all_gather x1, blocking collectives, shards(): p_own = lax.all_gather(res_p, 'z', axis=0, tiled=True)  33 us
    ppermute x10, waiting for transfers between devices, turned(): lax.ppermute(array, axis, [((i + by) % size, i) for i in range(size)])  17.7 us
    pallas_call x9, Pallas kernels, on_device(): pl.pallas_call(kernel, out_shape=out_shape, in_specs=[SMEM] * len(scalars...  14.1 us
    all_to_all x1, starting transfers between devices, gather(): return lax.all_to_all(copies, axes, 0, 0, tiled=True)  8.68 us
    all_to_all x1, starting transfers between devices, shards(): p_parts = [lax.all_to_all(p_sum, ('y', 'xl'), 0, 0, tiled=True)]  4.92 us
  transfers between devices with their start and end apart: 12, of which 4 were waited for; matrix products, arithmetic and copies ran while one was open for 0% of the time, Pallas kernels for 7%

profile of v7, /device:TPU:1, one launch (start us, length us, event | category | flops | bytes accessed | tf_op | source)
XLA Modules:
  0.0 166.2 jit_solution(12668026885339938517)
XLA Ops:
  0.6 0.0 copy-start.6
  0.6 0.0 copy-start.4
  0.7 0.0 copy-start.5
  0.7 2.1 %broadcast_in_dim.36 = bf16[16,256,128]{2,1,0:T(8,128)(2,1)} broadcast(bf16[256,128]{1,0:T(8,128)(2,1)} %bitcast.24), dimensions={1,2} | broadcast | bytes 1114112 | tf_op jit(solution)/shard_map/broadcast_in_dim | solution.py:286
  2.7 8.7 %all-to-all-start = ((bf16[16,256,128]{2,1,0:T(8,128)(2,1)}), bf16[16,256,128]{2,1,0:T(8,128)(2,1)S(1)}, u32[]{:S(2)}, u32[]{:S(2)}) async-start(bf16[16,256,128]{2,1,0:T(8,128)(2,1)} %broadcast_in_dim.36), calls=%async_computation | async-start | bytes 2097152 | tf_op jit(solution)/shard_map/all_to_all | solution.py:287
  11.4 33.0 %all_gather.3.refs_1_.own_ref = bf16[12,256,128]{2,1,0:T(8,128)(2,1)S(1)} all-gather(bf16[1,256,128]{2,1,0:T(8,128)(2,1)} %param.19), channel_id=1, replica_groups=mesh['z'=12,'xh'=2,'y'=8,'xl'=2,'core'=2] {'z'}, dimensions={0}, use_global_device_ids=true | all-gather | bytes 851968 | tf_op jit(solution)/shard_map/all_gather | solution.py:335
  44.4 0.0 all-to-all-done.refs_0_
  44.4 7.4 %collective-permute-start = (bf16[16,256,128]{2,1,0:T(8,128)(2,1)S(1)}, bf16[16,256,128]{2,1,0:T(8,128)(2,1)S(1)}, u32[]{:S(2)}, u32[]{:S(2)}) collective-permute-start(bf16[16,256,128]{2,1,0:T(8,128)(2,1)S(1)} %shard_map.140.own_ref), channel_id=1, source_target_pairs={{1,0},{0,1},{3,2},{2,3},{5,4},{4,5},{7,6},{6,7},{9,8},{8,9},{11,10... | collective-permute-start | bytes 3145736 | tf_op jit(solution)/shard_map/ppermute | solution.py:282
  51.8 4.4 %collective-permute-start.1 = (bf16[12,256,128]{2,1,0:T(8,128)(2,1)S(1)}, bf16[12,256,128]{2,1,0:T(8,128)(2,1)}, u32[]{:S(2)}, u32[]{:S(2)}) collective-permute-start(bf16[12,256,128]{2,1,0:T(8,128)(2,1)S(1)} %all_gather.3.refs_1_.own_ref), channel_id=1, source_target_pairs={{32,0},{0,32},{33,1},{1,33},{34,2},{2,34},{35,3},{3,35},{36,4},{4,... | collective-permute-start | bytes 2359304 | tf_op jit(solution)/shard_map/ppermute | solution.py:282
  56.9 0.1 stack.23.refs_0_
  56.9 0.0 copy-done.6
  56.9 0.0 copy-done.4
  56.9 0.0 copy-done.5
  57.0 1.9 %shard_map.139 = (s32[136]{0:T(256)S(1)}, s32[136]{0:T(256)S(1)}) custom-call(s32[6]{0:T(128)S(1)} %shard_map.138.where_ref, s32[2,32]{1,0:T(2,128)S(1)} %bitcast.33, s32[2,768]{1,0:T(2,128)S(1)} %bitcast.31, s32[2,768]{1,0:T(2,128)S(1)} %bitcast.32), custom_call_target="tpu_custom_call" | custom-call | tf_op jit(solution)/shard_map/pallas_call | solution.py:244
  58.8 0.0 collective-permute-done.other_ref
  58.8 4.5 %shard_map.141 = (bf16[8,256,128]{2,1,0:T(8,128)(2,1)S(1)}, bf16[8,256,128]{2,1,0:T(8,128)(2,1)S(1)}, bf16[8,256,128]{2,1,0:T(8,128)(2,1)S(1)}, s32[6]{0:T(128)S(1)}) custom-call(s32[6]{0:T(128)S(1)} %shard_map.138.where_ref, s32[136]{0:T(256)S(1)} %get-tuple-element.27.plan_ref, bf16[16,256,128]{2,1,0:T(8,128)(2,1)S(1)} %shard_map.140.own_ref, ...), custom_call_target="tpu_custom_call" | custom-call | flops 536870912 | bytes 12582912 | tf_op jit(solution)/shard_map/pallas_call | solution.py:244
  63.3 1.9 %collective-permute-start.2 = (bf16[8,256,128]{2,1,0:T(8,128)(2,1)S(1)}, bf16[8,256,128]{2,1,0:T(8,128)(2,1)S(1)}, u32[]{:S(2)}, u32[]{:S(2)}) collective-permute-start(bf16[8,256,128]{2,1,0:T(8,128)(2,1)S(1)} %get-tuple-element.32), channel_id=1, source_target_pairs={{704,0},{0,64},{64,128},{128,192},{192,256},{256,320},{320,384},{3... | collective-permute-start | bytes 1572872 | tf_op jit(solution)/shard_map/ppermute | solution.py:282
  65.2 5.7 %collective-permute-start.3 = (bf16[8,256,128]{2,1,0:T(8,128)(2,1)S(1)}, bf16[8,256,128]{2,1,0:T(8,128)(2,1)S(1)}, u32[]{:S(2)}, u32[]{:S(2)}) collective-permute-start(bf16[8,256,128]{2,1,0:T(8,128)(2,1)S(1)} %get-tuple-element.33), channel_id=1, source_target_pairs={{64,0},{128,64},{192,128},{256,192},{320,256},{384,320},{448,384},... | collective-permute-start | bytes 1572872 | tf_op jit(solution)/shard_map/ppermute | solution.py:282
  70.9 3.6 %collective-permute-done.1.other_ref = bf16[12,256,128]{2,1,0:T(8,128)(2,1)} collective-permute-done((bf16[12,256,128]{2,1,0:T(8,128)(2,1)S(1)}, bf16[12,256,128]{2,1,0:T(8,128)(2,1)}, u32[]{:S(2)}, u32[]{:S(2)}) %collective-permute-start.1) | collective-permute-done | bytes 786464 | tf_op jit(solution)/shard_map/ppermute | solution.py:282
  74.5 3.7 %shard_map.142 = (bf16[16,256,128]{2,1,0:T(8,128)(2,1)S(1)}, bf16[8,256,128]{2,1,0:T(8,128)(2,1)S(1)}, bf16[8,256,128]{2,1,0:T(8,128)(2,1)S(1)}) custom-call(s32[6]{0:T(128)S(1)} %get-tuple-element.28.where_ref, s32[136]{0:T(256)S(1)} %get-tuple-element.29.plan_ref, bf16[12,256,128]{2,1,0:T(8,128)(2,1)S(1)} %all_gather.3.refs_1_.own_ref, ...), custom_call_target="tpu_custom_call" | custom-call | flops 536870912 | bytes 12582912 | tf_op jit(solution)/shard_map/pallas_call | solution.py:244
  78.2 6.1 %collective-permute-start.4 = (bf16[8,256,128]{2,1,0:T(8,128)(2,1)S(1)}, bf16[8,256,128]{2,1,0:T(8,128)(2,1)S(1)}, u32[]{:S(2)}, u32[]{:S(2)}) collective-permute-start(bf16[8,256,128]{2,1,0:T(8,128)(2,1)S(1)} %get-tuple-element.35), channel_id=1, source_target_pairs={{1,0},{0,1},{3,2},{2,3},{5,4},{4,5},{7,6},{6,7},{9,8},{8,9},{11,10... | collective-permute-start | bytes 1572872 | tf_op jit(solution)/shard_map/ppermute | solution.py:282
  84.2 1.9 %collective-permute-start.5 = (bf16[8,256,128]{2,1,0:T(8,128)(2,1)S(1)}, bf16[8,256,128]{2,1,0:T(8,128)(2,1)S(1)}, u32[]{:S(2)}, u32[]{:S(2)}) collective-permute-start(bf16[8,256,128]{2,1,0:T(8,128)(2,1)S(1)} %get-tuple-element.36), channel_id=1, source_target_pairs={{1,0},{0,1},{3,2},{2,3},{5,4},{4,5},{7,6},{6,7},{9,8},{8,9},{11,10... | collective-permute-start | bytes 1572872 | tf_op jit(solution)/shard_map/ppermute | solution.py:282
  86.2 0.0 collective-permute-done.2.up_ref
  86.2 0.0 collective-permute-done.3.down_ref
  86.2 0.7 shard_map.143
  87.0 0.0 copy-start.8
  87.0 0.0 copy-start.7
  87.0 0.0 copy-start
  87.0 0.0 copy-start.1
  87.0 0.0 copy-start.2
  87.0 0.0 copy-start.3
  87.0 0.0 collective-permute-done.4.near_low_ref
  87.0 1.0 collective-permute-done.5.near_high_ref
  88.1 1.3 shard_map.145
  89.3 4.9 %all-to-all-start.1 = ((bf16[16,256,128]{2,1,0:T(8,128)(2,1)}), bf16[16,256,128]{2,1,0:T(8,128)(2,1)S(1)}, u32[]{:S(2)}, u32[]{:S(2)}) async-start(bf16[16,256,128]{2,1,0:T(8,128)(2,1)} %shard_map.145), calls=%async_computation.1 | async-start | bytes 2097152 | tf_op jit(solution)/shard_map/all_to_all | solution.py:377
  94.3 4.8 %collective-permute-start.6 = (bf16[4,256,128]{2,1,0:T(8,128)(2,1)S(1)}, bf16[4,256,128]{2,1,0:T(8,128)(2,1)S(1)}, u32[]{:S(2)}, u32[]{:S(2)}) collective-permute-start(bf16[4,256,128]{2,1,0:T(8,128)(2,1)S(1)} %get-tuple-element.34.refs_1_), channel_id=1, source_target_pairs={{32,0},{0,32},{33,1},{1,33},{34,2},{2,34},{35,3},{3,35},{36,4},{4,... | collective-permute-start | bytes 786440 | tf_op jit(solution)/shard_map/ppermute | solution.py:282
  99.0 0.0 copy-done.8
  99.1 0.1 eq.17
  99.1 6.0 %collective-permute-done.6.near_ref = bf16[4,256,128]{2,1,0:T(8,128)(2,1)S(1)} collective-permute-done((bf16[4,256,128]{2,1,0:T(8,128)(2,1)S(1)}, bf16[4,256,128]{2,1,0:T(8,128)(2,1)S(1)}, u32[]{:S(2)}, u32[]{:S(2)}) %collective-permute-start.6) | collective-permute-done | bytes 262176 | tf_op jit(solution)/shard_map/ppermute | solution.py:282
  105.2 0.1 shard_map.147
  105.2 3.2 %collective-permute-start.7 = (bf16[256,128]{1,0:T(8,128)(2,1)S(1)}, bf16[256,128]{1,0:T(8,128)(2,1)S(1)}, u32[]{:S(2)}, u32[]{:S(2)}) collective-permute-start(bf16[256,128]{1,0:T(8,128)(2,1)S(1)} %get-tuple-element.39), channel_id=1, source_target_pairs={{384,0},{448,64},{512,128},{576,192},{640,256},{704,320},{0,384},{... | collective-permute-start | bytes 196616 | tf_op jit(solution)/shard_map/ppermute | solution.py:282
  108.4 4.6 %collective-permute-start.8 = (bf16[256,128]{1,0:T(8,128)(2,1)S(1)}, bf16[256,128]{1,0:T(8,128)(2,1)S(1)}, u32[]{:S(2)}, u32[]{:S(2)}) collective-permute-start(bf16[256,128]{1,0:T(8,128)(2,1)S(1)} %get-tuple-element.40), channel_id=1, source_target_pairs={{576,0},{640,64},{704,128},{0,192},{64,256},{128,320},{192,384},{2... | collective-permute-start | bytes 196616 | tf_op jit(solution)/shard_map/ppermute | solution.py:282
  113.0 3.7 %collective-permute-start.9 = (bf16[256,128]{1,0:T(8,128)(2,1)S(1)}, bf16[256,128]{1,0:T(8,128)(2,1)S(1)}, u32[]{:S(2)}, u32[]{:S(2)}) collective-permute-start(bf16[256,128]{1,0:T(8,128)(2,1)S(1)} %get-tuple-element.41), channel_id=1, source_target_pairs={{192,0},{256,64},{320,128},{384,192},{448,256},{512,320},{576,384}... | collective-permute-start | bytes 196616 | tf_op jit(solution)/shard_map/ppermute | solution.py:282
  116.7 0.1 compare_select_fusion.projector_ref
  116.8 0.0 copy-done.7
  116.8 0.1 copy.24.mass_ref
  117.0 0.0 collective-permute-done.7.refs_0_
  117.0 7.1 %collective-permute-done.8.refs_1_ = bf16[256,128]{1,0:T(8,128)(2,1)S(1)} collective-permute-done((bf16[256,128]{1,0:T(8,128)(2,1)S(1)}, bf16[256,128]{1,0:T(8,128)(2,1)S(1)}, u32[]{:S(2)}, u32[]{:S(2)}) %collective-permute-start.8) | collective-permute-done | bytes 65568 | tf_op jit(solution)/shard_map/ppermute | solution.py:282
  124.1 0.0 collective-permute-done.9.refs_2_
  124.1 0.0 copy-done
  124.1 0.3 shard_map.148
  124.4 0.0 all-to-all-done.1.refs_0_
  124.4 0.0 copy-done.1
  124.5 0.7 shard_map.146
  125.2 0.1 maximum_reduce_fusion
  125.3 9.6 %all_to_all.20 = f32[8,1,128]{2,1,0:T(1,128)S(1)} all-to-all(f32[8,1,128]{2,1,0:T(1,128)S(1)} %broadcast_in_dim.39), channel_id=1, replica_groups=mesh['z'=12,'xh'=2,'y'=8,'xl'=2,'core'=2] {'xh','xl','core'}, dimensions={0} | all-to-all | bytes 8192 | tf_op jit(solution)/shard_map/all_to_all | solution.py:287
  135.0 30.2 %all_to_all.21.sums_ref = f32[96,1,128]{2,1,0:T(1,128)S(1)} all-to-all(f32[96,1,128]{2,1,0:T(1,128)S(1)} %broadcast_in_dim.40), channel_id=1, replica_groups=mesh['z'=12,'xh'=2,'y'=8,'xl'=2,'core'=2] {'z','y'}, dimensions={0} | all-to-all | bytes 98304 | tf_op jit(solution)/shard_map/all_to_all | solution.py:287
  165.3 0.0 copy-done.2
  165.3 0.0 copy-done.3
  165.3 1.0 shard_map.149
  (9 shorter events, 0.1 us)
Async XLA Ops:
  0.6 56.3 %copy-start.6 = (s32[1,1,2,32]{3,2,1,0:T(2,128)S(1)}, s32[1,1,2,32]{3,2,1,0:T(2,128)}, u32[]{:S(2)}) copy-start(s32[1,1,2,32]{3,2,1,0:T(2,128)} %param.12) | copy-start | bytes 772
  0.6 56.3 %copy-start.4 = (s32[768,2]{0,1:T(2,128)S(1)}, s32[768,2]{0,1:T(2,128)}, u32[]{:S(2)}) copy-start(s32[768,2]{0,1:T(2,128)} %param.14) | copy-start | bytes 18436
  0.7 56.3 %copy-start.5 = (s32[768,2]{0,1:T(2,128)S(1)}, s32[768,2]{0,1:T(2,128)}, u32[]{:S(2)}) copy-start(s32[768,2]{0,1:T(2,128)} %param.15) | copy-start | bytes 18436
  2.7 41.7 %all-to-all-start = ((bf16[16,256,128]{2,1,0:T(8,128)(2,1)}), bf16[16,256,128]{2,1,0:T(8,128)(2,1)S(1)}, u32[]{:S(2)}, u32[]{:S(2)}) async-start(bf16[16,256,128]{2,1,0:T(8,128)(2,1)} %broadcast_in_dim.36), calls=%async_computation | async-start | bytes 2097152 | tf_op jit(solution)/shard_map/all_to_all | solution.py:287
  44.4 14.4 %collective-permute-start = (bf16[16,256,128]{2,1,0:T(8,128)(2,1)S(1)}, bf16[16,256,128]{2,1,0:T(8,128)(2,1)S(1)}, u32[]{:S(2)}, u32[]{:S(2)}) collective-permute-start(bf16[16,256,128]{2,1,0:T(8,128)(2,1)S(1)} %shard_map.140.own_ref), channel_id=1, source_target_pairs={{1,0},{0,1},{3,2},{2,3},{5,4},{4,5},{7,6},{6,7},{9,8},{8,9},{11,10... | collective-permute-start | bytes 3145736 | tf_op jit(solution)/shard_map/ppermute | solution.py:282
  51.8 22.7 %collective-permute-start.1 = (bf16[12,256,128]{2,1,0:T(8,128)(2,1)S(1)}, bf16[12,256,128]{2,1,0:T(8,128)(2,1)}, u32[]{:S(2)}, u32[]{:S(2)}) collective-permute-start(bf16[12,256,128]{2,1,0:T(8,128)(2,1)S(1)} %all_gather.3.refs_1_.own_ref), channel_id=1, source_target_pairs={{32,0},{0,32},{33,1},{1,33},{34,2},{2,34},{35,3},{3,35},{36,4},{4,... | collective-permute-start | bytes 2359304 | tf_op jit(solution)/shard_map/ppermute | solution.py:282
  63.3 22.9 %collective-permute-start.2 = (bf16[8,256,128]{2,1,0:T(8,128)(2,1)S(1)}, bf16[8,256,128]{2,1,0:T(8,128)(2,1)S(1)}, u32[]{:S(2)}, u32[]{:S(2)}) collective-permute-start(bf16[8,256,128]{2,1,0:T(8,128)(2,1)S(1)} %get-tuple-element.32), channel_id=1, source_target_pairs={{704,0},{0,64},{64,128},{128,192},{192,256},{256,320},{320,384},{3... | collective-permute-start | bytes 1572872 | tf_op jit(solution)/shard_map/ppermute | solution.py:282
  65.2 21.0 %collective-permute-start.3 = (bf16[8,256,128]{2,1,0:T(8,128)(2,1)S(1)}, bf16[8,256,128]{2,1,0:T(8,128)(2,1)S(1)}, u32[]{:S(2)}, u32[]{:S(2)}) collective-permute-start(bf16[8,256,128]{2,1,0:T(8,128)(2,1)S(1)} %get-tuple-element.33), channel_id=1, source_target_pairs={{64,0},{128,64},{192,128},{256,192},{320,256},{384,320},{448,384},... | collective-permute-start | bytes 1572872 | tf_op jit(solution)/shard_map/ppermute | solution.py:282
  78.2 8.9 %collective-permute-start.4 = (bf16[8,256,128]{2,1,0:T(8,128)(2,1)S(1)}, bf16[8,256,128]{2,1,0:T(8,128)(2,1)S(1)}, u32[]{:S(2)}, u32[]{:S(2)}) collective-permute-start(bf16[8,256,128]{2,1,0:T(8,128)(2,1)S(1)} %get-tuple-element.35), channel_id=1, source_target_pairs={{1,0},{0,1},{3,2},{2,3},{5,4},{4,5},{7,6},{6,7},{9,8},{8,9},{11,10... | collective-permute-start | bytes 1572872 | tf_op jit(solution)/shard_map/ppermute | solution.py:282
  84.2 3.8 %collective-permute-start.5 = (bf16[8,256,128]{2,1,0:T(8,128)(2,1)S(1)}, bf16[8,256,128]{2,1,0:T(8,128)(2,1)S(1)}, u32[]{:S(2)}, u32[]{:S(2)}) collective-permute-start(bf16[8,256,128]{2,1,0:T(8,128)(2,1)S(1)} %get-tuple-element.36), channel_id=1, source_target_pairs={{1,0},{0,1},{3,2},{2,3},{5,4},{4,5},{7,6},{6,7},{9,8},{8,9},{11,10... | collective-permute-start | bytes 1572872 | tf_op jit(solution)/shard_map/ppermute | solution.py:282
  87.0 12.1 %copy-start.8 = (s32[64]{0:T(128)S(1)}, s32[64]{0:T(128)}, u32[]{:S(2)}) copy-start(s32[64]{0:T(128)} %param.16) | copy-start | bytes 772
  87.0 29.9 %copy-start.7 = (f32[1,256]{1,0:T(1,128)S(1)}, f32[1,256]{1,0:T(1,128)}, u32[]{:S(2)}) copy-start(f32[1,256]{1,0:T(1,128)} %param.17) | copy-start | bytes 3076
  87.0 37.1 %copy-start = (bf16[1,256,128]{2,1,0:T(8,128)(2,1)S(1)}, bf16[1,256,128]{2,1,0:T(8,128)(2,1)}, u32[]{:S(2)}) copy-start(bf16[1,256,128]{2,1,0:T(8,128)(2,1)} %param.21) | copy-start | bytes 196612
  87.0 37.5 %copy-start.1 = (bf16[1,256,128]{2,1,0:T(8,128)(2,1)S(1)}, bf16[1,256,128]{2,1,0:T(8,128)(2,1)}, u32[]{:S(2)}) copy-start(bf16[1,256,128]{2,1,0:T(8,128)(2,1)} %param.19) | copy-start | bytes 196612
  87.0 78.2 %copy-start.2 = (bf16[1,256,128]{2,1,0:T(8,128)(2,1)S(1)}, bf16[1,256,128]{2,1,0:T(8,128)(2,1)}, u32[]{:S(2)}) copy-start(bf16[1,256,128]{2,1,0:T(8,128)(2,1)} %param.18) | copy-start | bytes 196612
  87.0 78.2 %copy-start.3 = (bf16[1,256,128]{2,1,0:T(8,128)(2,1)S(1)}, bf16[1,256,128]{2,1,0:T(8,128)(2,1)}, u32[]{:S(2)}) copy-start(bf16[1,256,128]{2,1,0:T(8,128)(2,1)} %param.20) | copy-start | bytes 196612
  89.3 35.1 %all-to-all-start.1 = ((bf16[16,256,128]{2,1,0:T(8,128)(2,1)}), bf16[16,256,128]{2,1,0:T(8,128)(2,1)S(1)}, u32[]{:S(2)}, u32[]{:S(2)}) async-start(bf16[16,256,128]{2,1,0:T(8,128)(2,1)} %shard_map.145), calls=%async_computation.1 | async-start | bytes 2097152 | tf_op jit(solution)/shard_map/all_to_all | solution.py:377
  94.3 10.9 %collective-permute-start.6 = (bf16[4,256,128]{2,1,0:T(8,128)(2,1)S(1)}, bf16[4,256,128]{2,1,0:T(8,128)(2,1)S(1)}, u32[]{:S(2)}, u32[]{:S(2)}) collective-permute-start(bf16[4,256,128]{2,1,0:T(8,128)(2,1)S(1)} %get-tuple-element.34.refs_1_), channel_id=1, source_target_pairs={{32,0},{0,32},{33,1},{1,33},{34,2},{2,34},{35,3},{3,35},{36,4},{4,... | collective-permute-start | bytes 786440 | tf_op jit(solution)/shard_map/ppermute | solution.py:282
  105.2 11.7 %collective-permute-start.7 = (bf16[256,128]{1,0:T(8,128)(2,1)S(1)}, bf16[256,128]{1,0:T(8,128)(2,1)S(1)}, u32[]{:S(2)}, u32[]{:S(2)}) collective-permute-start(bf16[256,128]{1,0:T(8,128)(2,1)S(1)} %get-tuple-element.39), channel_id=1, source_target_pairs={{384,0},{448,64},{512,128},{576,192},{640,256},{704,320},{0,384},{... | collective-permute-start | bytes 196616 | tf_op jit(solution)/shard_map/ppermute | solution.py:282
  108.4 15.7 %collective-permute-start.8 = (bf16[256,128]{1,0:T(8,128)(2,1)S(1)}, bf16[256,128]{1,0:T(8,128)(2,1)S(1)}, u32[]{:S(2)}, u32[]{:S(2)}) collective-permute-start(bf16[256,128]{1,0:T(8,128)(2,1)S(1)} %get-tuple-element.40), channel_id=1, source_target_pairs={{576,0},{640,64},{704,128},{0,192},{64,256},{128,320},{192,384},{2... | collective-permute-start | bytes 196616 | tf_op jit(solution)/shard_map/ppermute | solution.py:282
  113.0 11.1 %collective-permute-start.9 = (bf16[256,128]{1,0:T(8,128)(2,1)S(1)}, bf16[256,128]{1,0:T(8,128)(2,1)S(1)}, u32[]{:S(2)}, u32[]{:S(2)}) collective-permute-start(bf16[256,128]{1,0:T(8,128)(2,1)S(1)} %get-tuple-element.41), channel_id=1, source_target_pairs={{192,0},{256,64},{320,128},{384,192},{448,256},{512,320},{576,384}... | collective-permute-start | bytes 196616 | tf_op jit(solution)/shard_map/ppermute | solution.py:282
